TPU v7x, 32 devices: a whole 2x2x4 slice. The times are simulated.
32 devices in a mesh: dp: 8 (over z, y), tm: 4 (over x, core).
Axes of the slice: x: 2, y: 2, z: 4, core: 2. Of those that a mesh axis runs over, the one named last changes fastest.
Arguments:
- latents: bfloat16 [8, 24, 16, 128, 128], P('dp', 'tm'), may hold values from -6 to 6
- cotangent: bfloat16 [8, 24, 16, 128, 128], P('dp', 'tm'), may hold values from -6 to 6
- first_spatial: bfloat16 [3, 3, 128, 128], replicated, may hold values from -0.1875 to 0.1875
- last_spatial: bfloat16 [3, 3, 128, 128], replicated, may hold values from -0.1875 to 0.1875
- first_temporal: bfloat16 [3, 128, 128], replicated, may hold values from -0.3125 to 0.3125
- second_temporal: bfloat16 [3, 128, 128], replicated, may hold values from -0.3125 to 0.3125
- frame_counts: int32 [8], P('dp'), may hold values from 12 to 24, as said below
- dilations: int32 [2], replicated, may hold values from 1 to 4, as said below
Outputs:
- decoded: bfloat16 [8, 24, 16, 128, 128], P('dp', 'tm')
- latent_grad: bfloat16 [8, 24, 16, 128, 128], P('dp', 'tm')
- first_spatial_grad: float32 [3, 3, 128, 128], replicated
- last_spatial_grad: float32 [3, 3, 128, 128], replicated
- first_temporal_grad: float32 [3, 128, 128], replicated
- second_temporal_grad: float32 [3, 128, 128], replicated
Inputs may be any that keep to these rules, and one draw needn't show every extreme that they name: `frame_counts`: each clip's valid frames stand at the start of its 24 slots; some clip has 24. At least one of the two dilations is 4.
All inputs are finite; a program needn't handle non-finite values.
Results may differ from a plain program's by a relative error of at most 0.0079.
Values may be sent and summed in bfloat16 or wider, within the bound.
No kernel may reach another device: no remote copies, remote signals or barrier semaphores. Data moves between devices by JAX's collectives and lax.ppermute only.
A program may use at most 256 MiB of HBM per device.

v0:
```python
import jax
import jax.numpy as jnp
from jax import lax
from jax.sharding import PartitionSpec as P

TAPS = 3
DILATION_MAX = 4


def silu_slope(values):
    sigma = jax.nn.sigmoid(values)
    return sigma * (1.0 + values * (1.0 - sigma))


def spatial(source, kernel):
    row_count, col_count, channels = source.shape[-3:]
    leading = source.shape[:-3]
    padded = jnp.pad(source, [(0, 0)] * len(leading) + [(1, 1), (1, 1), (0, 0)])
    summed = jnp.zeros(leading + (row_count, col_count, kernel.shape[3]), jnp.float32)
    for row_shift in range(3):
        for col_shift in range(3):
            window = padded[
                ..., row_shift : row_shift + row_count, col_shift : col_shift + col_count, :
            ]
            product = jnp.dot(
                window.reshape(-1, channels),
                kernel[row_shift, col_shift],
                preferred_element_type=jnp.float32,
            )
            summed = summed + product.reshape(summed.shape)
    return summed


def spatial_back(incoming, kernel):
    return spatial(incoming, jnp.transpose(kernel[::-1, ::-1], (0, 1, 3, 2)))


def spatial_kernel(source, incoming):
    row_count, col_count, channels = source.shape[-3:]
    leading = source.shape[:-3]
    padded = jnp.pad(source, [(0, 0)] * len(leading) + [(1, 1), (1, 1), (0, 0)])
    flat_in = incoming.reshape(-1, incoming.shape[-1])
    result_rows = []
    for row_shift in range(3):
        result_cols = []
        for col_shift in range(3):
            window = padded[
                ..., row_shift : row_shift + row_count, col_shift : col_shift + col_count, :
            ]
            result_cols.append(
                lax.dot_general(
                    window.reshape(-1, channels),
                    flat_in,
                    (((0,), (0,)), ((), ())),
                    preferred_element_type=jnp.float32,
                )
            )
        result_rows.append(jnp.stack(result_cols))
    return jnp.stack(result_rows)


def temporal(source, kernel, dilation):
    margin = (TAPS - 1) * DILATION_MAX
    slot_count = source.shape[1]
    padded = jnp.pad(source, ((0, 0), (margin, 0), (0, 0), (0, 0), (0, 0)))
    summed = jnp.zeros(source.shape[:-1] + (kernel.shape[2],), jnp.float32)
    for tap_index in range(kernel.shape[0]):
        begin_at = margin - tap_index * dilation
        window = lax.dynamic_slice_in_dim(padded, begin_at, slot_count, 1)
        product = jnp.dot(
            window.reshape(-1, source.shape[-1]),
            kernel[tap_index],
            preferred_element_type=jnp.float32,
        )
        summed = summed + product.reshape(summed.shape)
    return summed


def temporal_back(incoming, kernel, dilation):
    margin = (TAPS - 1) * DILATION_MAX
    slot_count = incoming.shape[1]
    padded = jnp.pad(incoming, ((0, 0), (0, margin), (0, 0), (0, 0), (0, 0)))
    summed = jnp.zeros(incoming.shape[:-1] + (kernel.shape[1],), jnp.float32)
    for tap_index in range(kernel.shape[0]):
        begin_at = tap_index * dilation
        window = lax.dynamic_slice_in_dim(padded, begin_at, slot_count, 1)
        product = jnp.dot(
            window.reshape(-1, incoming.shape[-1]),
            kernel[tap_index].T,
            preferred_element_type=jnp.float32,
        )
        summed = summed + product.reshape(summed.shape)
    return summed


def temporal_kernel(source, incoming, dilation):
    margin = (TAPS - 1) * DILATION_MAX
    slot_count = source.shape[1]
    padded = jnp.pad(source, ((0, 0), (margin, 0), (0, 0), (0, 0), (0, 0)))
    flat_in = incoming.reshape(-1, incoming.shape[-1])
    result = []
    for tap_index in range(TAPS):
        begin_at = margin - tap_index * dilation
        window = lax.dynamic_slice_in_dim(padded, begin_at, slot_count, 1)
        result.append(
            lax.dot_general(
                window.reshape(-1, source.shape[-1]),
                flat_in,
                (((0,), (0,)), ((), ())),
                preferred_element_type=jnp.float32,
            )
        )
    return jnp.stack(result)


def forward_bands(band_in, first_temporal, second_temporal, dilations):
    pre_mid = temporal(band_in, first_temporal, dilations[0])
    act_mid = jax.nn.silu(pre_mid).astype(jnp.bfloat16)
    act_out = temporal(act_mid, second_temporal, dilations[1]).astype(jnp.bfloat16)
    return (pre_mid, act_mid, act_out)


def on_device(
    latents,
    cotangent,
    first_spatial,
    last_spatial,
    first_temporal,
    second_temporal,
    frame_counts,
    dilations,
):
    local_slots = latents.shape[1]
    first_slot = lax.axis_index("tm") * local_slots
    slot_ids = first_slot + jnp.arange(local_slots, dtype=jnp.int32)
    is_valid = (slot_ids[None, :] < frame_counts[:, None])[:, :, None, None, None]
    total_count = (
        latents.shape[0]
        * lax.axis_size("dp")
        * local_slots
        * lax.axis_size("tm")
        * latents.shape[2]
        * latents.shape[3]
    )
    factor = float(total_count) ** (-0.5)
    pre_in = spatial(latents, first_spatial)
    act_in = jax.nn.silu(pre_in).astype(jnp.bfloat16)
    masked = jnp.where(is_valid, cotangent, jnp.zeros_like(cotangent))
    band_in = lax.all_to_all(act_in, "tm", split_axis=2, concat_axis=1, tiled=True)
    pre_mid, act_mid, act_out = forward_bands(band_in, first_temporal, second_temporal, dilations)
    back_out = spatial_back(masked, last_spatial).astype(jnp.bfloat16)
    band_back = lax.all_to_all(back_out, "tm", split_axis=2, concat_axis=1, tiled=True)
    second_grad = temporal_kernel(act_mid, band_back, dilations[1])
    slope_mid = (
        temporal_back(band_back, second_temporal, dilations[1]) * silu_slope(pre_mid)
    ).astype(jnp.bfloat16)
    first_grad = temporal_kernel(band_in, slope_mid, dilations[0])
    back_in = temporal_back(slope_mid, first_temporal, dilations[0]).astype(jnp.bfloat16)
    frame_out, frame_back = (
        lax.all_to_all(act_out, "tm", split_axis=1, concat_axis=2, tiled=True),
        lax.all_to_all(back_in, "tm", split_axis=1, concat_axis=2, tiled=True),
    )
    decoded = jnp.where(
        is_valid, latents.astype(jnp.float32) + spatial(frame_out, last_spatial), jnp.float32(0.0)
    ).astype(jnp.bfloat16)
    last_grad = spatial_kernel(frame_out, masked)
    slope_in = (frame_back.astype(jnp.float32) * silu_slope(pre_in)).astype(jnp.bfloat16)
    spatial_grad = spatial_kernel(latents, slope_in)
    latent_grad = (masked.astype(jnp.float32) + spatial_back(slope_in, first_spatial)).astype(
        jnp.bfloat16
    )
    partials = (
        factor * spatial_grad,
        factor * last_grad,
        factor * first_grad,
        factor * second_grad,
    )
    reduced = lax.psum((partials[0], partials[1], partials[2], partials[3]), ("dp", "tm"))
    return (decoded, latent_grad, reduced[0], reduced[1], reduced[2], reduced[3])


def solution(mesh):
    in_specs = (
        P("dp", "tm", None, None, None),
        P("dp", "tm", None, None, None),
        P(),
        P(),
        P(),
        P(),
        P("dp"),
        P(),
    )
    out_specs = (
        P("dp", "tm", None, None, None),
        P("dp", "tm", None, None, None),
        P(),
        P(),
        P(),
        P(),
    )
    return jax.shard_map(
        on_device, mesh=mesh, in_specs=in_specs, out_specs=out_specs, check_vma=False
    )
```

profile of v0, /device:TPU:0, one launch (start us, length us, event | category | flops | bytes accessed | tf_op | source)
XLA Modules:
  0.0 526.9 jit_solution(9850024425873125963)
XLA Ops:
  11.2 3.7 fusion.36
  14.9 3.6 fusion.38
  22.1 3.6 fusion.42
  25.8 3.6 fusion.60
  29.4 3.7 fusion.62
  33.1 3.6 fusion.64
  40.3 18.5 %fusion.18 = bf16[1,6,16,128,128]{4,3,2,1,0:T(8,128)(2,1)} fusion(f32[6,16,128,128]{3,2,1,0:T(8,128)} %fusion.36, f32[6,16,128,128]{3,2,1,0:T(8,128)} %fusion.38, f32[6,16,128,128]{3,2,1,0:T(8,128)} %fusion.40, f32[6,16,128,128]{3,2,1,0:T(8,128)} %fusion.42, f32[6,16,128,128]{3,2,1,0:T(8,128)} %fusion.60, f32[6,16,128,128]{3,2,1,0:T(8,128)} %fusion.62, ...), kind=kOutput, calls=%fused_computation.35 | convolution fusion | flops 416808960 | bytes 56655872 | tf_op jit(solution)/shard_map/dot_general | solution.py:25
  58.8 4.0 copy.102
  62.8 5.0 all-to-all-start.2
  67.8 5.6 %fusion.100 = f32[6,16,128,128]{3,2,1,0:T(8,128)} fusion(bf16[1,6,16,128,128]{4,3,2,1,0:T(8,128)(2,1)} %param.8, bf16[3,3,128,128]{3,2,1,0:T(8,128)(2,1)S(1)} %copy-done.11), kind=kOutput, calls=%fused_computation.117 | convolution fusion | flops 402653184 | bytes 9469952 | tf_op jit(solution)/shard_map/dot_general | solution.py:25
  73.4 3.6 fusion.104
  77.1 3.7 fusion.108
  84.3 3.6 fusion.116
  87.9 3.7 fusion.120
  91.6 3.7 fusion.124
  95.3 3.6 fusion.128
  98.9 20.5 %add_add_fusion.1 = f32[6,16,128,128]{3,2,1,0:T(8,128)} fusion(f32[6,16,128,128]{3,2,1,0:T(8,128)} %fusion.100, f32[6,16,128,128]{3,2,1,0:T(8,128)} %fusion.104, f32[6,16,128,128]{3,2,1,0:T(8,128)} %fusion.108, f32[6,16,128,128]{3,2,1,0:T(8,128)} %fusion.112, f32[6,16,128,128]{3,2,1,0:T(8,128)} %fusion.116, f32[6,16,128,128]{3,2,1,0:T(8,128)} %fusion.120, ...), kind=kOutput, calls=%fused_computation.15 | convolution fusion | flops 415236096 | bytes 59801600 | tf_op jit(solution)/shard_map/dot_general | solution.py:25
  119.4 4.4 fusion.150
  125.7 5.2 all-to-all-start
  145.7 22.8 %all-to-all-done = bf16[1,6,16,128,128]{4,3,1,0,2:T(8,128)(2,1)} async-done(((bf16[1,6,16,128,128]{4,3,1,0,2:T(8,128)(2,1)}), bf16[1,6,16,128,128]{4,3,1,0,2:T(8,128)(2,1)}, u32[]{:S(2)}, u32[]{:S(2)}) %all-to-all-start) | async-done | bytes 3145760 | tf_op jit(solution)/shard_map/all_to_all | solution.py:149
  173.6 4.3 multiply_convert_fusion.2
  180.6 3.6 fusion.94
  184.3 3.6 fusion.96
  192.9 3.6 fusion.9
  196.5 3.7 fusion.6
  200.2 8.1 %multiply_convert_fusion.1 = bf16[24,4,128,128]{3,2,1,0:T(8,128)(2,1)S(1)} fusion(f32[24,4,128,128]{3,2,1,0:T(8,128)} %get-tuple-element.15, f32[24,4,128,128]{3,2,1,0:T(8,128)} %fusion.9, f32[24,4,128,128]{3,2,1,0:T(8,128)} %fusion.6, bf16[24,4,128,128]{3,2,1,0:T(8,128)(2,1)S(1)} %bitcast.806, bf16[3,128,128]{2,1,0:T(8,128)(2,1)S(1)} %copy-done.14), kind=kOutput, calls=%fused_computation.7 | convolution fusion | flops 419954688 | bytes 25198592 | tf_op jit(solution)/shard_map/dot_general | solution.py:87
  210.0 5.7 %fusion.17 = bf16[1,24,4,128,128]{4,3,2,0,1:T(8,128)(2,1)} fusion(f32[24,4,128,128]{3,2,1,0:T(8,128)S(1)} %bitcast.821, f32[24,4,128,128]{3,2,1,0:T(8,128)} %fusion.96, bf16[24,4,128,128]{3,2,1,0:T(8,128)(2,1)S(1)} %get-tuple-element.14, bf16[3,128,128]{2,1,0:T(8,128)(2,1)S(1)} %copy-done.14), kind=kOutput, calls=%fused_computation.34 | convolution fusion | flops 407371776 | bytes 18907136 | tf_op jit(solution)/shard_map/dot_general | solution.py:70
  215.7 4.7 all-to-all-start.1
  222.0 3.9 fusion.185
  232.9 24.5 %all-to-all-done.1 = bf16[1,24,4,128,128]{4,3,2,0,1:T(8,128)(2,1)} async-done(((bf16[1,24,4,128,128]{4,3,2,0,1:T(8,128)(2,1)}), bf16[1,24,4,128,128]{4,3,2,0,1:T(8,128)(2,1)}, u32[]{:S(2)}, u32[]{:S(2)}) %all-to-all-start.1) | async-done | bytes 3145760 | tf_op jit(solution)/shard_map/all_to_all | solution.py:160
  257.4 4.7 all-to-all-start.3
  277.4 21.6 %all-to-all-done.3 = bf16[1,24,4,128,128]{4,3,2,0,1:T(8,128)(2,1)} async-done(((bf16[1,24,4,128,128]{4,3,2,0,1:T(8,128)(2,1)}), bf16[1,24,4,128,128]{4,3,2,0,1:T(8,128)(2,1)}, u32[]{:S(2)}, u32[]{:S(2)}) %all-to-all-start.3) | async-done | bytes 3145760 | tf_op jit(solution)/shard_map/all_to_all | solution.py:161
  301.8 4.8 multiply_convert_fusion
  316.1 3.7 fusion.20
  319.8 3.6 fusion.22
  323.4 3.8 fusion.24
  327.2 3.6 fusion.255
  330.9 3.6 fusion.26
  334.5 3.7 fusion.28
  338.2 3.6 fusion.30
  341.8 4.5 fusion.32
  353.5 3.6 fusion.77
  357.1 3.7 fusion.80
  367.9 3.7 fusion.89
  371.6 3.8 fusion.260
  378.6 20.7 %fusion.2 = bf16[1,6,16,128,128]{4,3,2,1,0:T(8,128)(2,1)} fusion(f32[6,16,128,128]{3,2,1,0:T(8,128)} %fusion.71, f32[6,16,128,128]{3,2,1,0:T(8,128)} %fusion.74, f32[6,16,128,128]{3,2,1,0:T(8,128)} %fusion.77, f32[6,16,128,128]{3,2,1,0:T(8,128)} %fusion.80, f32[6,16,128,128]{3,2,1,0:T(8,128)} %fusion.260, f32[6,16,128,128]{3,2,1,0:T(8,128)} %fusion.83, ...), kind=kOutput, calls=%fused_computation.4 | convolution fusion | flops 421527552 | bytes 59802112 | tf_op jit(solution)/shard_map/dot_general | solution.py:25
  399.3 18.8 %fusion = bf16[1,6,16,128,128]{4,3,2,1,0:T(8,128)(2,1)} fusion(f32[6,16,128,128]{3,2,1,0:T(8,128)} %fusion.20, f32[6,16,128,128]{3,2,1,0:T(8,128)} %fusion.22, f32[6,16,128,128]{3,2,1,0:T(8,128)} %fusion.24, f32[6,16,128,128]{3,2,1,0:T(8,128)} %fusion.26, f32[6,16,128,128]{3,2,1,0:T(8,128)} %fusion.255, f32[6,16,128,128]{3,2,1,0:T(8,128)} %fusion.28, ...), kind=kOutput, calls=%fused_computation.1 | convolution fusion | flops 419954688 | bytes 59801600 | tf_op jit(solution)/shard_map/dot_general | solution.py:25
  418.1 94.7 %all-reduce.11.cloned.1.call-done = (f32[3,3,128,128]{3,2,1,0:T(8,128)}, f32[3,3,128,128]{3,2,1,0:T(8,128)}, f32[3,128,128]{2,1,0:T(8,128)}, f32[3,128,128]{2,1,0:T(8,128)}) async-done(((f32[3,3,128,128]{3,2,1,0:T(8,128)}, f32[3,3,128,128]{3,2,1,0:T(8,128)}, f32[3,128,128]{2,1,0:T(8,128)}, f32[3,128,128]{2,1,0:T(8,128)}), (f32[3,3,128,128]{3,2,1,0:T(8,128)}, f32[3,3,128,128]{3,2,1,0:T(8,128)}, ...) | async-done | bytes 1572880 | tf_op jit(solution)/shard_map/psum | solution.py:178
  (124 shorter events, 98.1 us)
Async XLA Ops:
  9.0 2.2 copy-start.25
  62.8 5.0 copy-start.11
  62.8 62.9 %all-to-all-start.2 = ((bf16[1,6,16,128,128]{4,3,1,0,2:T(8,128)(2,1)}), bf16[1,6,16,128,128]{4,3,1,0,2:T(8,128)(2,1)}, u32[]{:S(2)}, u32[]{:S(2)}) async-start(bf16[1,6,16,128,128]{4,3,1,0,2:T(8,128)(2,1)} %copy.102), calls=%async_computation.2 | async-start | bytes 6291456 | tf_op jit(solution)/shard_map/all_to_all | solution.py:152
  67.8 5.6 %copy-start = (bf16[1,6,16,128,128]{4,3,2,1,0:T(8,128)(2,1)S(1)}, bf16[1,6,16,128,128]{4,3,2,1,0:T(8,128)(2,1)}, u32[]{:S(2)}) copy-start(bf16[1,6,16,128,128]{4,3,2,1,0:T(8,128)(2,1)} %param.8) | copy-start | bytes 9437188
  125.7 5.2 copy-start.24
  125.7 42.8 %all-to-all-start = ((bf16[1,6,16,128,128]{4,3,1,0,2:T(8,128)(2,1)}), bf16[1,6,16,128,128]{4,3,1,0,2:T(8,128)(2,1)}, u32[]{:S(2)}, u32[]{:S(2)}) async-start(bf16[1,6,16,128,128]{4,3,1,0,2:T(8,128)(2,1)} %copy.94), calls=%async_computation | async-start | bytes 6291456 | tf_op jit(solution)/shard_map/all_to_all | solution.py:149
  141.2 197.0 %copy-start.13 = (bf16[3,3,128,128]{3,2,1,0:T(8,128)(2,1)}, bf16[3,3,128,128]{3,2,1,0:T(8,128)(2,1)S(1)}, u32[]{:S(2)}) copy-start(bf16[3,3,128,128]{3,2,1,0:T(8,128)(2,1)S(1)} %reverse_bitcast_fusion) | copy-start | bytes 884740
  170.8 0.9 copy-start.15
  171.2 37.1 %copy-start.9 = (bf16[1,4,6,4,128,128]{5,4,3,2,1,0:T(8,128)(2,1)}, bf16[1,4,6,4,128,128]{5,4,3,2,1,0:T(8,128)(2,1)S(1)}, u32[]{:S(2)}) copy-start(bf16[1,4,6,4,128,128]{5,4,3,2,1,0:T(8,128)(2,1)S(1)} %copy.96) | copy-start | bytes 9437188
  178.0 2.6 copy-start.14
  184.3 3.6 copy-start.6
  196.5 13.5 %slice-start = ((s8[6291456]{0:T(1024)(128)(4,1)}), s8[4194304]{0:T(1024)(128)(4,1)S(1)}, s32[]{:S(2)}) async-start(s8[6291456]{0:T(1024)(128)(4,1)} %bitcast.820), calls=%async_computation.5 | async-start | bytes 8388608
  200.2 9.9 %slice-start.1 = ((s8[6291456]{0:T(1024)(128)(4,1)}), s8[2097152]{0:T(1024)(128)(4,1)S(1)}, s32[]{:S(2)}) async-start(s8[6291456]{0:T(1024)(128)(4,1)} %bitcast.820), calls=%async_computation.6 | async-start | bytes 4194304
  208.3 1.7 copy-start.7
  215.7 41.7 %all-to-all-start.1 = ((bf16[1,24,4,128,128]{4,3,2,0,1:T(8,128)(2,1)}), bf16[1,24,4,128,128]{4,3,2,0,1:T(8,128)(2,1)}, u32[]{:S(2)}, u32[]{:S(2)}) async-start(bf16[1,24,4,128,128]{4,3,2,0,1:T(8,128)(2,1)} %fusion.17), calls=%async_computation.1 | async-start | bytes 6291456 | tf_op jit(solution)/shard_map/all_to_all | solution.py:160
  222.0 3.9 copy-start.8
  222.0 4.6 copy-start.10
  226.6 1.1 copy-start.23
  257.4 41.7 %all-to-all-start.3 = ((bf16[1,24,4,128,128]{4,3,2,0,1:T(8,128)(2,1)}), bf16[1,24,4,128,128]{4,3,2,0,1:T(8,128)(2,1)}, u32[]{:S(2)}, u32[]{:S(2)}) async-start(bf16[1,24,4,128,128]{4,3,2,0,1:T(8,128)(2,1)} %fusion.19), calls=%async_computation.3 | async-start | bytes 6291456 | tf_op jit(solution)/shard_map/all_to_all | solution.py:161
  262.1 250.7 %all-reduce.11.cloned.1.call-start = ((), (), s32[]{:S(2)}) async-start(), calls=%async_computation.4 | async-start | bytes 3145728 | tf_op jit(solution)/shard_map/psum | solution.py:178
  264.6 11.1 %copy-start.2 = (bf16[1,6,4,4,128,128]{5,4,3,2,1,0:T(8,128)(2,1)}, bf16[1,6,4,4,128,128]{5,4,3,2,1,0:T(8,128)(2,1)S(1)}, u32[]{:S(2)}) copy-start(bf16[1,6,4,4,128,128]{5,4,3,2,1,0:T(8,128)(2,1)S(1)} %copy.99) | copy-start | bytes 9437188
  301.8 4.8 copy-start.1
  306.6 35.2 %copy-start.4 = (bf16[6,16,128,128]{3,2,1,0:T(8,128)(2,1)}, bf16[6,16,128,128]{3,2,1,0:T(8,128)(2,1)S(1)}, u32[]{:S(2)}) copy-start(bf16[6,16,128,128]{3,2,1,0:T(8,128)(2,1)S(1)} %multiply_convert_fusion) | copy-start | bytes 9437188
  341.8 4.5 copy-start.3
  341.8 4.5 copy-start.12
  375.3 1.3 copy-start.20
  375.3 1.4 copy-start.21
  375.3 1.4 copy-start.22
  375.3 1.4 copy-start.16
  375.3 1.4 copy-start.17
  375.3 1.4 copy-start.18
  375.3 1.4 copy-start.19
  376.7 1.9 copy-start.26
  378.6 20.7 %copy-start.5 = (bf16[6,16,128,128]{3,2,1,0:T(8,128)(2,1)S(1)}, bf16[6,16,128,128]{3,2,1,0:T(8,128)(2,1)}, u32[]{:S(2)}) copy-start(bf16[6,16,128,128]{3,2,1,0:T(8,128)(2,1)} %copy-done.4) | copy-start | bytes 9437188
Sparse Core Ops, SparseCore 0:
  378.7 133.9 all-reduce.10
where the time goes:
time: 535 us; the launch traced here: 527 us
  matrix products  272 us (51%)
  waiting for transfers between devices  164 us (31%)
  local copies, waits for them, and re-layouts  32.7 us (6%)
  between operations  23.2 us (4%)
  starting transfers between devices  19.8 us (4%)
  other arithmetic  15.6 us (3%)
    dot_general x36, matrix products, spatial(): jnp.dot(window.reshape(-1, channels), kernel[row_shift, col_shift], prefe...  198 us
    psum x1, waiting for transfers between devices, on_device(): lax.psum((partials[0], partials[1], partials[2], partials[3]), ('dp', 'tm'))  94.7 us
    all_to_all x1, waiting for transfers between devices, on_device(): lax.all_to_all(act_out, 'tm', split_axis=1, concat_axis=2, tiled=True)  24.5 us
    dot_general x18, matrix products, spatial_kernel(): lax.dot_general(window.reshape(-1, channels), flat_in, (((0,), (0,)), (()...  23.5 us
    all_to_all x1, waiting for transfers between devices, on_device(): lax.all_to_all(act_in, 'tm', split_axis=2, concat_axis=1, tiled=True)  22.8 us
    all_to_all x1, waiting for transfers between devices, on_device(): lax.all_to_all(back_in, 'tm', split_axis=1, concat_axis=2, tiled=True)  21.6 us
    dot_general x6, matrix products, temporal_back(): jnp.dot(window.reshape(-1, incoming.shape[-1]), kernel[tap_index].T, pref...  20.1 us
    dot_general x6, matrix products, temporal(): jnp.dot(window.reshape(-1, source.shape[-1]), kernel[tap_index], preferre...  19.2 us
  transfers between devices with their start and end apart: 5, of which 4 were waited for; matrix products, arithmetic and copies ran while one was open for 25% of the time, Pallas kernels for 0%

commit v1 on v0

--- a/solution.py
+++ b/solution.py
@@ -1,6 +1,10 @@
+import functools
+
 import jax
 import jax.numpy as jnp
 from jax import lax
+from jax.experimental import pallas as pl
+from jax.experimental.pallas import tpu as pltpu
 from jax.sharding import PartitionSpec as P
 
 TAPS = 3
@@ -179,6 +183,577 @@
     return (decoded, latent_grad, reduced[0], reduced[1], reduced[2], reduced[3])
 
 
+REACH = (TAPS - 1) * DILATION_MAX
+CHUNKS = 2
+VMEM_LIMIT = 56 * 1024 * 1024
+BF = jnp.bfloat16
+F32 = jnp.float32
+
+
+def params():
+    return pltpu.CompilerParams(
+        dimension_semantics=("arbitrary",), vmem_limit_bytes=VMEM_LIMIT
+    )
+
+
+def cost(flops, nbytes):
+    return pl.CostEstimate(flops=int(flops), bytes_accessed=int(nbytes), transcendentals=0)
+
+
+def zero_borders(pad, pairs):
+    pad[...] = jnp.zeros(pad.shape, F32)
+    lanes = pairs.shape[2]
+    width = pairs.shape[1]
+    pairs[0, :, 0 : lanes // 2] = jnp.zeros((width, lanes // 2), BF)
+    pairs[pairs.shape[0] - 1, :, lanes // 2 : lanes] = jnp.zeros((width, lanes // 2), BF)
+
+
+def fill_pairs(frame, pad, pairs):
+    rows, width, chans = frame.shape
+    pad[:, 8 : 8 + width, :] = frame[...].astype(F32)
+    for shift in range(3):
+        if shift == 1:
+            seen = frame[...]
+        else:
+            seen = pad[:, 7 + shift : 7 + shift + width, :].astype(BF)
+        seen = seen.reshape(rows // 2, 2, width, chans)
+        low = shift * chans
+        pairs[0 : rows // 2, :, (3 * chans + low) : (3 * chans + low + chans)] = seen[:, 0]
+        pairs[1 : rows // 2 + 1, :, low : low + chans] = seen[:, 1]
+
+
+def two_row_conv(pairs, weights, first, count):
+    width = pairs.shape[1]
+    lanes = pairs.shape[2]
+    upper = pairs[first : first + count].reshape(count * width, lanes)
+    lower = pairs[first + 1 : first + 1 + count].reshape(count * width, lanes)
+    return jnp.dot(
+        jnp.concatenate([upper, lower], axis=1), weights[...], preferred_element_type=F32
+    )
+
+
+def front_kernel(
+    ids, latents, cotangent, w_in, w_back,
+    act_keep, act_send, back_keep, back_send, slope,
+    pad, pairs, frame, result,
+):
+    at = pl.program_id(0)
+    core = ids[1]
+    rows, width, chans = frame.shape
+    half = rows // 2
+    step = half // 2
+
+    @pl.when(at == 0)
+    def _():
+        zero_borders(pad, pairs)
+
+    frame[...] = latents[0]
+    fill_pairs(frame, pad, pairs)
+    for part in range(2):
+        pre = two_row_conv(pairs, w_in, part * step, step)
+        sigma = jax.nn.sigmoid(pre)
+        act = (pre * sigma).astype(BF).reshape(step, width, 2 * chans)
+        grad = (sigma * (1.0 + pre * (1.0 - sigma))).astype(BF).reshape(step, width, 2 * chans)
+        for pair in range(step):
+            for odd in range(2):
+                row = part * half + 2 * pair + odd
+                lanes = slice(odd * chans, odd * chans + chans)
+                result[row] = act[pair, :, lanes]
+                slope[0, row] = grad[pair, :, lanes]
+    act_keep[0] = result[pl.ds(core * half, half)]
+    act_send[0] = result[pl.ds(half - core * half, half)]
+
+    keep = jnp.where(at < ids[2], 1.0, 0.0).astype(F32)
+    frame[...] = (cotangent[0].astype(F32) * keep).astype(BF)
+    fill_pairs(frame, pad, pairs)
+    for part in range(2):
+        back = two_row_conv(pairs, w_back, part * step, step)
+        back = back.astype(BF).reshape(step, width, 2 * chans)
+        for pair in range(step):
+            for odd in range(2):
+                row = part * half + 2 * pair + odd
+                result[row] = back[pair, :, odd * chans : odd * chans + chans]
+    back_keep[0] = result[pl.ds(core * half, half)]
+    back_send[0] = result[pl.ds(half - core * half, half)]
+
+
+def front(ids, latents, cotangent, w_in, w_back):
+    slots, rows, width, chans = latents.shape
+    half = rows // 2
+    whole = pl.BlockSpec((1, rows, width, chans), lambda i, ids: (i, 0, 0, 0))
+    part = pl.BlockSpec((1, half, width, chans), lambda i, ids: (i, 0, 0, 0))
+    fixed = pl.BlockSpec(w_in.shape, lambda i, ids: (0, 0))
+    halves = jax.ShapeDtypeStruct((slots, half, width, chans), BF)
+    return pl.pallas_call(
+        front_kernel,
+        grid_spec=pltpu.PrefetchScalarGridSpec(
+            num_scalar_prefetch=1,
+            grid=(slots,),
+            in_specs=[whole, whole, fixed, fixed],
+            out_specs=[part, part, part, part, whole],
+            scratch_shapes=[
+                pltpu.VMEM((rows, width + 16, chans), F32),
+                pltpu.VMEM((half + 1, width, 6 * chans), BF),
+                pltpu.VMEM((rows, width, chans), BF),
+                pltpu.VMEM((rows, width, chans), BF),
+            ],
+        ),
+        out_shape=[halves, halves, halves, halves, jax.ShapeDtypeStruct(latents.shape, BF)],
+        compiler_params=params(),
+        cost_estimate=cost(4 * latents.size * chans * 12, 10 * latents.size),
+        name="front",
+    )(ids, latents, cotangent, w_in, w_back)
+
+
+def taps_of(held, start, step, count):
+    size = held.shape[1]
+    chans = held.shape[2]
+    seen = []
+    for tap in range(TAPS):
+        seen.append(held[pl.ds(start + tap * step, count)].reshape(count * size, chans))
+    return jnp.concatenate(seen, axis=1)
+
+
+def outer(left, right):
+    return lax.dot_general(left, right, (((0,), (0,)), ((), ())), preferred_element_type=F32)
+
+
+def middle_kernel(
+    ids, own_in, got_in, own_back, got_back, halo, w_mid, w_mid_back, w_first,
+    mid_send, mid_keep, first_keep, first_send, grad_first, grad_second,
+    held_in, held_back, held_mid, result,
+):
+    at = pl.program_id(0)
+    side, core, near, far = ids[0], ids[1], ids[3], ids[4]
+    slots = own_in.shape[0]
+    frames = 2 * slots
+    mine = core * slots
+    other = slots - mine
+
+    @pl.when(at == 0)
+    def _():
+        blank = jnp.zeros((REACH,) + held_in.shape[1:], BF)
+        held_in[0:REACH] = blank
+        held_back[frames : frames + REACH] = blank
+        held_mid[0:REACH] = blank
+        held_mid[REACH + frames : 2 * REACH + frames] = blank
+        grad_first[...] = jnp.zeros_like(grad_first)
+        grad_second[...] = jnp.zeros_like(grad_second)
+
+    held_in[pl.ds(REACH + mine, slots)] = own_in[:, 0]
+    held_in[pl.ds(REACH + other, slots)] = got_in[:, 0]
+    held_back[pl.ds(mine, slots)] = own_back[:, 0]
+    held_back[pl.ds(other, slots)] = got_back[:, 0]
+
+    @pl.when(side == 0)
+    def _():
+        held_back[frames : frames + REACH] = halo[:, 0]
+
+    @pl.when(side == 1)
+    def _():
+        held_in[0:REACH] = halo[:, 0]
+
+    size, chans = held_in.shape[1:]
+    taps_in = taps_of(held_in, REACH, -near, frames)
+    taps_back = taps_of(held_back, 0, far, frames)
+    pre = jnp.dot(taps_in, w_mid[...], preferred_element_type=F32)
+    sigma = jax.nn.sigmoid(pre)
+    act = (pre * sigma).astype(BF)
+    back = jnp.dot(taps_back, w_mid_back[...], preferred_element_type=F32)
+    grad = (back * (sigma * (1.0 + pre * (1.0 - sigma)))).astype(BF)
+    grad_second[...] += outer(act, taps_back)
+    grad_first[...] += outer(grad, taps_in)
+    act = act.reshape(frames, size, chans)
+    grad = grad.reshape(frames, size, chans)
+
+    @pl.when(side == 0)
+    def _():
+        held_mid[REACH : REACH + frames] = act
+        mid_keep[:, 0] = grad
+        mid_send[:, 0] = act[frames - REACH :]
+
+    @pl.when(side == 1)
+    def _():
+        held_mid[REACH : REACH + frames] = grad
+        mid_keep[:, 0] = act
+        mid_send[:, 0] = grad[:REACH]
+
+    step = jnp.where(side == 0, -far, near)
+    first = jnp.dot(
+        taps_of(held_mid, REACH, step, frames), w_first[...], preferred_element_type=F32
+    )
+    result[...] = first.astype(BF).reshape(frames, size, chans)
+    first_keep[:, 0] = result[pl.ds(mine, slots)]
+    first_send[:, 0] = result[pl.ds(other, slots)]
+
+
+def middle(chunk, ids, own_in, got_in, own_back, got_back, halo, w_mid, w_mid_back, w_first):
+    slots, half, width, chans = own_in.shape
+    frames = 2 * slots
+    rows = halo.shape[1]
+    source = pl.BlockSpec((slots, 1, width, chans), lambda i, ids: (0, chunk * rows + i, 0, 0))
+    fixed = pl.BlockSpec(w_mid.shape, lambda i, ids: (0, 0))
+    sums = pl.BlockSpec((chans, TAPS * chans), lambda i, ids: (0, 0))
+
+    def rowwise(count):
+        return pl.BlockSpec((count, 1, width, chans), lambda i, ids: (0, i, 0, 0))
+
+    def shaped(count):
+        return jax.ShapeDtypeStruct((count, rows, width, chans), BF)
+
+    summed = jax.ShapeDtypeStruct((chans, TAPS * chans), F32)
+    return pl.pallas_call(
+        middle_kernel,
+        grid_spec=pltpu.PrefetchScalarGridSpec(
+            num_scalar_prefetch=1,
+            grid=(rows,),
+            in_specs=[source, source, source, source, rowwise(REACH), fixed, fixed, fixed],
+            out_specs=[
+                rowwise(REACH), rowwise(frames), rowwise(slots), rowwise(slots), sums, sums,
+            ],
+            scratch_shapes=[
+                pltpu.VMEM((REACH + frames, width, chans), BF),
+                pltpu.VMEM((REACH + frames, width, chans), BF),
+                pltpu.VMEM((2 * REACH + frames, width, chans), BF),
+                pltpu.VMEM((frames, width, chans), BF),
+            ],
+        ),
+        out_shape=[
+            shaped(REACH), shaped(frames), shaped(slots), shaped(slots), summed, summed,
+        ],
+        compiler_params=params(),
+        cost_estimate=cost(
+            2 * frames * rows * width * chans * chans * 30, 14 * frames * rows * width * chans
+        ),
+        name="middle",
+    )(ids, own_in, got_in, own_back, got_back, halo, w_mid, w_mid_back, w_first)
+
+
+def second_kernel(ids, mid, halo, w_second, keep, send, held, result):
+    at = pl.program_id(0)
+    side, core, near, far = ids[0], ids[1], ids[3], ids[4]
+    frames = mid.shape[0]
+    slots = frames // 2
+    mine = core * slots
+
+    @pl.when(at == 0)
+    def _():
+        blank = jnp.zeros((REACH,) + held.shape[1:], BF)
+        held[0:REACH] = blank
+        held[REACH + frames : 2 * REACH + frames] = blank
+
+    held[REACH : REACH + frames] = mid[:, 0]
+
+    @pl.when(side == 0)
+    def _():
+        held[REACH + frames : 2 * REACH + frames] = halo[:, 0]
+
+    @pl.when(side == 1)
+    def _():
+        held[0:REACH] = halo[:, 0]
+
+    step = jnp.where(side == 0, near, -far)
+    made = jnp.dot(
+        taps_of(held, REACH, step, frames), w_second[...], preferred_element_type=F32
+    )
+    result[...] = made.astype(BF).reshape(result.shape)
+    keep[:, 0] = result[pl.ds(mine, slots)]
+    send[:, 0] = result[pl.ds(slots - mine, slots)]
+
+
+def second(ids, mid, halo, w_second):
+    frames, rows, width, chans = mid.shape
+    slots = frames // 2
+
+    def rowwise(count):
+        return pl.BlockSpec((count, 1, width, chans), lambda i, ids: (0, i, 0, 0))
+
+    shape = jax.ShapeDtypeStruct((slots, rows, width, chans), BF)
+    return pl.pallas_call(
+        second_kernel,
+        grid_spec=pltpu.PrefetchScalarGridSpec(
+            num_scalar_prefetch=1,
+            grid=(rows,),
+            in_specs=[
+                rowwise(frames), rowwise(REACH),
+                pl.BlockSpec(w_second.shape, lambda i, ids: (0, 0)),
+            ],
+            out_specs=[rowwise(slots), rowwise(slots)],
+            scratch_shapes=[
+                pltpu.VMEM((2 * REACH + frames, width, chans), BF),
+                pltpu.VMEM((frames, width, chans), BF),
+            ],
+        ),
+        out_shape=[shape, shape],
+        compiler_params=params(),
+        cost_estimate=cost(2 * mid.size * chans * 6, 6 * mid.size),
+        name="second",
+    )(ids, mid, halo, w_second)
+
+
+def ending_kernel(factor, ids, *refs):
+    own, got = refs[0:CHUNKS], refs[CHUNKS : 2 * CHUNKS]
+    latents, cotangent, slope, weights, out, sums, pad, pairs, frame, beside, total = refs[
+        2 * CHUNKS :
+    ]
+    at = pl.program_id(0)
+    core, role = ids[1], ids[5]
+    rows, width, chans = frame.shape
+    half = rows // 2
+    step = half // 2
+    piece = half // CHUNKS
+
+    @pl.when(at == 0)
+    def _():
+        zero_borders(pad, pairs)
+        total[...] = jnp.zeros_like(total)
+
+    for chunk in range(CHUNKS):
+        frame[pl.ds(core * half + chunk * piece, piece)] = own[chunk][0]
+        frame[pl.ds(half - core * half + chunk * piece, piece)] = got[chunk][0]
+
+    @pl.when(role == 1)
+    def _():
+        frame[...] = (frame[...].astype(F32) * slope[0].astype(F32)).astype(BF)
+
+    fill_pairs(frame, pad, pairs)
+    valid = jnp.where(at < ids[2], 1.0, 0.0).astype(F32)
+
+    @pl.when(role == 0)
+    def _():
+        masked = (cotangent[0].astype(F32) * valid).astype(BF)
+        masked = masked.reshape(half, 2, width, chans)
+        beside[:, :, 0:chans] = masked[:, 0]
+        beside[:, :, chans : 2 * chans] = masked[:, 1]
+        frame[...] = latents[0]
+
+    @pl.when(role == 1)
+    def _():
+        plain = latents[0].reshape(half, 2, width, chans)
+        beside[:, :, 0:chans] = plain[:, 0]
+        beside[:, :, chans : 2 * chans] = plain[:, 1]
+        frame[...] = cotangent[0]
+
+    scale = jnp.where(role == 0, valid, 1.0).astype(F32)
+    for part in range(2):
+        made = two_row_conv(pairs, weights, part * step, step) * scale
+        made = made.reshape(step, width, 2 * chans)
+        for pair in range(step):
+            for odd in range(2):
+                row = part * half + 2 * pair + odd
+                plus = frame[row].astype(F32) * valid
+                out[0, row] = (plus + made[pair, :, odd * chans : odd * chans + chans]).astype(BF)
+
+    lanes = pairs.shape[2]
+    flat = beside[...].reshape(half * width, 2 * chans)
+    for part in range(2):
+        seen = pairs[part : part + half].reshape(half * width, lanes)
+        total[:, part * lanes : (part + 1) * lanes] += outer(flat, seen)
+
+    @pl.when(at == pl.num_programs(0) - 1)
+    def _():
+        span = 9 * chans
+        sums[...] = factor * (
+            total[0:chans, 0:span] + total[chans : 2 * chans, 3 * chans : 3 * chans + span]
+        )
+
+
+def ending(factor, ids, own, got, latents, cotangent, slope, weights):
+    slots, rows, width, chans = latents.shape
+    half = rows // 2
+    whole = pl.BlockSpec((1, rows, width, chans), lambda i, ids: (i, 0, 0, 0))
+    part = pl.BlockSpec((1, half // CHUNKS, width, chans), lambda i, ids: (i, 0, 0, 0))
+    gated = pl.BlockSpec((1, rows, width, chans), lambda i, ids: (i * ids[5], 0, 0, 0))
+    return pl.pallas_call(
+        functools.partial(ending_kernel, factor),
+        grid_spec=pltpu.PrefetchScalarGridSpec(
+            num_scalar_prefetch=1,
+            grid=(slots,),
+            in_specs=[part] * (2 * CHUNKS)
+            + [whole, whole, gated, pl.BlockSpec(weights.shape, lambda i, ids: (0, 0))],
+            out_specs=[whole, pl.BlockSpec((chans, 9 * chans), lambda i, ids: (0, 0))],
+            scratch_shapes=[
+                pltpu.VMEM((rows, width + 16, chans), F32),
+                pltpu.VMEM((half + 1, width, 6 * chans), BF),
+                pltpu.VMEM((rows, width, chans), BF),
+                pltpu.VMEM((half, width, 2 * chans), BF),
+                pltpu.VMEM((2 * chans, 12 * chans), F32),
+            ],
+        ),
+        out_shape=[
+            jax.ShapeDtypeStruct(latents.shape, BF),
+            jax.ShapeDtypeStruct((chans, 9 * chans), F32),
+        ],
+        compiler_params=params(),
+        cost_estimate=cost(4 * latents.size * chans * 12, 10 * latents.size),
+        name="ending",
+    )(ids, *own, *got, latents, cotangent, slope, weights)
+
+
+def two_row_weights(kernel):
+    flat = kernel.reshape(-1, kernel.shape[3])
+    shift = 3 * kernel.shape[2]
+    return jnp.concatenate(
+        [jnp.pad(flat, ((0, shift), (0, 0))), jnp.pad(flat, ((shift, 0), (0, 0)))], axis=1
+    )
+
+
+def turned(kernel):
+    return jnp.transpose(kernel[::-1, ::-1], (0, 1, 3, 2))
+
+
+def flips(dp_size, tm_size):
+    count = dp_size * tm_size
+    digit = 1
+    result = []
+    while digit < count:
+        result.append([(place, place ^ digit) for place in range(count)])
+        digit *= 2
+    return result
+
+
+def halve(values, digits, pairs, place):
+    for digit in digits:
+        size = values.shape[0] // 2
+        upper = (place >> digit) & 1
+        keep = lax.dynamic_slice_in_dim(values, upper * size, size, 0)
+        send = lax.dynamic_slice_in_dim(values, (1 - upper) * size, size, 0)
+        values = keep + lax.ppermute(send, ("dp", "tm"), pairs[digit])
+    return values
+
+
+def double(values, digits, pairs, place, axis=0):
+    for digit in digits:
+        upper = (place >> digit) & 1
+        other = lax.ppermute(values, ("dp", "tm"), pairs[digit])
+        values = jnp.where(
+            upper == 0,
+            jnp.concatenate([values, other], axis),
+            jnp.concatenate([other, values], axis),
+        )
+    return values
+
+
+def on_chip_pair(
+    dp_size,
+    latents,
+    cotangent,
+    first_spatial,
+    last_spatial,
+    first_temporal,
+    second_temporal,
+    frame_counts,
+    dilations,
+):
+    latents, cotangent = latents[0], cotangent[0]
+    slots, rows, width, chans = latents.shape
+    half = rows // 2
+    tm_index = lax.axis_index("tm")
+    side, core = tm_index // 2, tm_index % 2
+    factor = float(dp_size * 4 * slots * rows * width) ** (-0.5)
+
+    def ids_for(role):
+        return jnp.stack(
+            [side, core, frame_counts[0] - tm_index * slots, dilations[0], dilations[1], role]
+        ).astype(jnp.int32)
+
+    ids = ids_for(side)
+    swap_cores = [(0, 1), (1, 0), (2, 3), (3, 2)]
+    swap_sides = [(0, 2), (2, 0), (1, 3), (3, 1)]
+
+    w_in = two_row_weights(first_spatial)
+    w_out = two_row_weights(last_spatial)
+    w_in_back = two_row_weights(turned(first_spatial))
+    w_out_back = two_row_weights(turned(last_spatial))
+    w_one = first_temporal.reshape(-1, chans)
+    w_two = second_temporal.reshape(-1, chans)
+    w_one_back = jnp.transpose(first_temporal, (0, 2, 1)).reshape(-1, chans)
+    w_two_back = jnp.transpose(second_temporal, (0, 2, 1)).reshape(-1, chans)
+    at_zero = side == 0
+
+    act_own, act_send, back_own, back_send, slope = front(
+        ids, latents, cotangent, w_in, w_out_back
+    )
+    act_got = lax.ppermute(act_send, "tm", swap_cores)
+    back_got = lax.ppermute(back_send, "tm", swap_cores)
+
+    size = half // CHUNKS
+    tail = REACH - slots
+    middles = []
+    for chunk in range(CHUNKS):
+        low = chunk * size
+        pieces = [value[:, low : low + size] for value in (act_own, act_got, back_own, back_got)]
+        act_low = jnp.where(core == 0, pieces[0][slots - tail :], pieces[1][slots - tail :])
+        act_high = jnp.where(core == 0, pieces[1], pieces[0])
+        back_low = jnp.where(core == 0, pieces[2], pieces[3])
+        back_high = jnp.where(core == 0, pieces[3][:tail], pieces[2][:tail])
+        leaving = jnp.where(
+            at_zero,
+            jnp.concatenate([act_low, act_high], 0),
+            jnp.concatenate([back_low, back_high], 0),
+        )
+        halo = lax.ppermute(leaving, "tm", swap_sides)
+        middles.append(
+            middle(
+                chunk, ids, act_own, act_got, back_own, back_got, halo,
+                w_one, w_two_back, jnp.where(at_zero, w_two, w_one_back),
+            )
+        )
+    halos = [lax.ppermute(made[0], "tm", swap_sides) for made in middles]
+
+    first_own = [made[2] for made in middles]
+    first_got = [lax.ppermute(made[3], "tm", swap_cores) for made in middles]
+    out_first, sums_first = ending(
+        factor, ids, first_own, first_got, latents, cotangent, slope,
+        jnp.where(at_zero, w_out, w_in_back),
+    )
+
+    w_second = jnp.where(at_zero, w_one_back, w_two)
+    seconds = [second(ids, made[1], halo, w_second) for made, halo in zip(middles, halos)]
+    second_own = [made[0] for made in seconds]
+    second_got = [lax.ppermute(made[1], "tm", swap_cores) for made in seconds]
+    out_second, sums_second = ending(
+        factor, ids_for(1 - side), second_own, second_got, latents, cotangent, slope,
+        jnp.where(at_zero, w_in_back, w_out),
+    )
+
+    pairs = flips(dp_size, 4)
+    place = lax.axis_index("dp") * 4 + tm_index
+    digits = [0] + list(range(2, len(pairs)))
+    temporal_sums = factor * jnp.concatenate(
+        [sum(made[4] for made in middles), sum(made[5] for made in middles)], 0
+    )
+    temporal_sums = halve(temporal_sums, digits + [1], pairs, place)
+    temporal_sums = double(temporal_sums, [1] + digits[::-1], pairs, place)
+    early = halve(sums_first, digits, pairs, place)
+    late = halve(sums_second, digits, pairs, place)
+    both = jnp.stack([early, late])
+    other = lax.ppermute(both, ("dp", "tm"), pairs[1])
+    spatial_sums = jnp.where(
+        at_zero,
+        jnp.stack([early + other[1], late + other[0]]),
+        jnp.stack([late + other[0], early + other[1]]),
+    )
+    spatial_sums = double(spatial_sums, digits[::-1], pairs, place, 1)
+
+    decoded = jnp.where(at_zero, out_first, out_second)
+    latent_grad = jnp.where(at_zero, out_second, out_first)
+    last_grad = jnp.transpose(spatial_sums[0].reshape(chans, 3, 3, chans), (1, 2, 3, 0))
+    first_grad = jnp.transpose(spatial_sums[1].reshape(chans, 3, 3, chans), (1, 2, 0, 3))
+    first_grad = first_grad[::-1, ::-1]
+    near_grad = jnp.transpose(temporal_sums[:chans].reshape(chans, TAPS, chans), (1, 2, 0))
+    far_grad = jnp.transpose(temporal_sums[chans:].reshape(chans, TAPS, chans), (1, 0, 2))
+    return (decoded[None], latent_grad[None], first_grad, last_grad, near_grad, far_grad)
+
+
+def on_any_device(dp_size, tm_size, latents, cotangent, *rest):
+    clips, slots, rows = latents.shape[:3]
+    fits = clips == 1 and tm_size == 4 and slots <= REACH <= 2 * slots and rows % 8 == 0
+    if fits and dp_size & (dp_size - 1) == 0:
+        return on_chip_pair(dp_size, latents, cotangent, *rest)
+    return on_device(latents, cotangent, *rest)
+
+
 def solution(mesh):
     in_specs = (
         P("dp", "tm", None, None, None),
@@ -199,5 +774,5 @@
         P(),
     )
     return jax.shard_map(
-        on_device, mesh=mesh, in_specs=in_specs, out_specs=out_specs, check_vma=False
-    )
+        functools.partial(on_any_device, mesh.shape["dp"], mesh.shape["tm"]), mesh=mesh, in_specs=in_specs, out_specs=out_specs, check_vma=False
+    )

time: 535 us -> 247 us (0.46); the launches traced: 527 us -> 246 us
  matrix products: 272 us -> 0 us
  Pallas kernels: 0 us -> 88.7 us
  waiting for transfers between devices: 164 us -> 87.1 us
  between operations: 23.2 us -> 1.83 us
  local copies, waits for them, and re-layouts: 32.7 us -> 14.9 us
  starting transfers between devices: 19.8 us -> 32.3 us
  other arithmetic: 15.6 us -> 21.2 us
    dot_general x72 -> x0, matrix products: 272 us -> none  [the longest x36 198 us: spatial(): jnp.dot(window.reshape(-1, channels), kernel[row_shift, col_shift], prefe...]
    psum x1 -> x0, waiting for transfers between devices: 94.7 us -> none  [on_device(): lax.psum((partials[0], partials[1], partials[2], partials[3]), ('dp', 'tm'))]
    pallas_call x0 -> x7, Pallas kernels: none -> 88.7 us  [the longest x2 36.4 us: ending(): pl.pallas_call(functools.partial(ending_kernel, factor), grid_spec=pltpu....]
    ppermute x0 -> x33, waiting for transfers between devices: none -> 87.1 us  [the longest x2 31.6 us: on_chip_pair(): halo = lax.ppermute(leaving, 'tm', swap_sides)]
    all_to_all x4 -> x0, waiting for transfers between devices: 68.9 us -> none  [the longest x1 24.5 us: on_device(): lax.all_to_all(act_out, 'tm', split_axis=1, concat_axis=2, tiled=True)]
    ppermute x0 -> x33, starting transfers between devices: none -> 32.3 us  [the longest x13 17.9 us: halve(): values = keep + lax.ppermute(send, ('dp', 'tm'), pairs[digit])]
    all_to_all x4 -> x0, starting transfers between devices: 19.5 us -> none  [the longest x1 5.19 us: on_device(): lax.all_to_all(act_in, 'tm', split_axis=2, concat_axis=1, tiled=True)]
    all_to_all x5 -> x0, local copies, waits for them, and re-layouts: 9.44 us -> none  [the longest x2 4.49 us: on_device(): lax.all_to_all(back_out, 'tm', split_axis=2, concat_axis=1, tiled=True)]
  transfers between devices with their start and end apart: 5 -> 33, of which waited for: 4 -> 18; matrix products, arithmetic and copies ran while one was open for 25% -> 6% of each run, Pallas kernels for 0% -> 24%
where the time goes in v1:
time: 247 us; the launch traced here: 246 us
  Pallas kernels  88.7 us (36%)
  waiting for transfers between devices  87.1 us (35%)
  starting transfers between devices  32.3 us (13%)
  other arithmetic  21.2 us (9%)
  local copies, waits for them, and re-layouts  14.9 us (6%)
    pallas_call x2, Pallas kernels, ending(): pl.pallas_call(functools.partial(ending_kernel, factor), grid_spec=pltpu....  36.4 us
    ppermute x2, waiting for transfers between devices, on_chip_pair(): halo = lax.ppermute(leaving, 'tm', swap_sides)  31.6 us
    pallas_call x2, Pallas kernels, middle(): pl.pallas_call(middle_kernel, grid_spec=pltpu.PrefetchScalarGridSpec(num_...  23.8 us
    ppermute x2, waiting for transfers between devices, on_chip_pair(): halos = [lax.ppermute(made[0], 'tm', swap_sides) for made in middles]  18.2 us
    ppermute x13, starting transfers between devices, halve(): values = keep + lax.ppermute(send, ('dp', 'tm'), pairs[digit])  17.9 us
    ppermute x13, waiting for transfers between devices, halve(): values = keep + lax.ppermute(send, ('dp', 'tm'), pairs[digit])  17.7 us
    pallas_call x1, Pallas kernels, front(): pl.pallas_call(front_kernel, grid_spec=pltpu.PrefetchScalarGridSpec(num_s...  16.9 us
    ppermute x9, waiting for transfers between devices, double(): other = lax.ppermute(values, ('dp', 'tm'), pairs[digit])  12 us
  transfers between devices with their start and end apart: 33, of which 18 were waited for; matrix products, arithmetic and copies ran while one was open for 6% of the time, Pallas kernels for 24%

profile of v1, /device:TPU:0, one launch (start us, length us, event | category | flops | bytes accessed | tf_op | source)
XLA Modules:
  0.0 246.0 jit_solution(15849153995478704727)
XLA Ops:
  2.5 2.5 %fusion.8 = (bf16[1536,256]{1,0:T(8,128)(2,1)}, bf16[1536,256]{1,0:T(8,128)(2,1)}) fusion(bf16[1152,128]{1,0:T(8,128)(2,1)} %bitcast.63, bf16[1152,128]{1,0:T(8,128)(2,1)S(1)} %bitcast.64), kind=kLoop, calls=%fused_computation.15 | loop fusion | flops 5505024 | bytes 2162688 | tf_op jit(solution)/shard_map/concatenate | solution.py:596
  5.6 16.9 %front.1 = (bf16[6,8,128,128]{3,2,1,0:T(8,128)(2,1)}, bf16[6,8,128,128]{3,2,1,0:T(8,128)(2,1)}, bf16[6,8,128,128]{3,2,1,0:T(8,128)(2,1)}, bf16[6,8,128,128]{3,2,1,0:T(8,128)(2,1)}, bf16[6,16,128,128]{3,2,1,0:T(8,128)(2,1)}) custom-call(s32[6]{0:T(128)} %stack.48.ids, bf16[6,16,128,128]{3,2,1,0:T(8,128)(2,1)} %bitcast.77, bf16[6,16,128,128]{3,2,1,0:T(8,128)(2,1)} %bitcast.80, ...), custom_call_target="tpu_custom_call" | custom-call | flops 9663676416 | bytes 15728640 | tf_op jit(solution)/shard_map/front/pallas_call | solution.py:287
  23.2 4.6 %collective-permute-done.got_in = bf16[6,8,128,128]{3,2,1,0:T(8,128)(2,1)S(1)} collective-permute-done((bf16[6,8,128,128]{3,2,1,0:T(8,128)(2,1)}, bf16[6,8,128,128]{3,2,1,0:T(8,128)(2,1)S(1)}, u32[]{:S(2)}, u32[]{:S(2)}) %collective-permute-start) | collective-permute-done | bytes 1572896 | tf_op jit(solution)/shard_map/ppermute | solution.py:677
  27.8 1.5 slice_select_fusion.5
  29.5 1.2 copy-done.2
  30.7 1.1 slice_select_fusion.4
  31.8 1.5 slice_select_fusion
  33.5 2.9 %collective-permute-start.2 = (bf16[8,4,128,128]{3,2,1,0:T(8,128)(2,1)S(1)}, bf16[8,4,128,128]{3,2,1,0:T(8,128)(2,1)}, u32[]{:S(2)}, u32[]{:S(2)}) collective-permute-start(bf16[8,4,128,128]{3,2,1,0:T(8,128)(2,1)S(1)} %maximum_select_fusion.1), channel_id=1, source_target_pairs={{0,2},{2,0},{1,3},{3,1},{4,6},{6,4},{5,7},{7,5},{8,10},{10,8},{9,1... | collective-permute-start | bytes 3145736 | tf_op jit(solution)/shard_map/ppermute | solution.py:695
  38.9 21.6 %collective-permute-done.2.halo = bf16[8,4,128,128]{3,2,1,0:T(8,128)(2,1)} collective-permute-done((bf16[8,4,128,128]{3,2,1,0:T(8,128)(2,1)S(1)}, bf16[8,4,128,128]{3,2,1,0:T(8,128)(2,1)}, u32[]{:S(2)}, u32[]{:S(2)}) %collective-permute-start.2) | collective-permute-done | bytes 1048608 | tf_op jit(solution)/shard_map/ppermute | solution.py:695
  60.5 11.9 %middle.2 = (bf16[8,4,128,128]{3,2,1,0:T(8,128)(2,1)}, bf16[12,4,128,128]{3,2,1,0:T(8,128)(2,1)}, bf16[6,4,128,128]{3,2,1,0:T(8,128)(2,1)}, bf16[6,4,128,128]{3,...) custom-call(s32[6]{0:T(128)} %stack.48.ids, bf16[6,8,128,128]{3,2,1,0:T(8,128)(2,1)} %get-tuple-element.31.own_in, ...), custom_call_target="tpu_custom_call" | custom-call | flops 6039797760 | bytes 11010048 | tf_op jit(solution)/shard_map/middle/pallas_call | solution.py:405
  72.4 10.1 %collective-permute-done.3.halo = bf16[8,4,128,128]{3,2,1,0:T(8,128)(2,1)} collective-permute-done((bf16[8,4,128,128]{3,2,1,0:T(8,128)(2,1)S(1)}, bf16[8,4,128,128]{3,2,1,0:T(8,128)(2,1)}, u32[]{:S(2)}, u32[]{:S(2)}) %collective-permute-start.3) | collective-permute-done | bytes 1048608 | tf_op jit(solution)/shard_map/ppermute | solution.py:695
  82.5 11.9 %middle.3 = (bf16[8,4,128,128]{3,2,1,0:T(8,128)(2,1)}, bf16[12,4,128,128]{3,2,1,0:T(8,128)(2,1)}, bf16[6,4,128,128]{3,2,1,0:T(8,128)(2,1)}, bf16[6,4,128,128]{3,...) custom-call(s32[6]{0:T(128)} %stack.48.ids, bf16[6,8,128,128]{3,2,1,0:T(8,128)(2,1)} %get-tuple-element.31.own_in, ...), custom_call_target="tpu_custom_call" | custom-call | flops 6039797760 | bytes 11010048 | tf_op jit(solution)/shard_map/middle/pallas_call | solution.py:405
  96.6 1.4 collective-permute-done.23
  98.1 1.8 collective-permute-start.24
  99.9 3.1 %collective-permute-done.24 = f32[64,384]{1,0:T(8,128)S(1)} collective-permute-done((f32[64,384]{1,0:T(8,128)S(1)}, f32[64,384]{1,0:T(8,128)S(1)}, u32[]{:S(2)}, u32[]{:S(2)}) %collective-permute-start.24) | collective-permute-done | bytes 98336 | tf_op jit(solution)/shard_map/ppermute | solution.py:621
  103.0 1.9 collective-permute-start.25
  104.9 2.3 collective-permute-done.25
  107.2 2.9 %collective-permute-start.26 = (f32[16,384]{1,0:T(8,128)S(1)}, f32[16,384]{1,0:T(8,128)S(1)}, u32[]{:S(2)}, u32[]{:S(2)}) collective-permute-start(f32[16,384]{1,0:T(8,128)S(1)} %constant_dynamic-slice_fusion.1), channel_id=1, source_target_pairs={{0,16},{1,17},{2,18},{3,19},{4,20},{5,21},{6,22},{7,23},{8,24},{9,... | collective-permute-start | bytes 73736 | tf_op jit(solution)/shard_map/ppermute | solution.py:621
  110.9 1.1 collective-permute-done.26
  112.0 1.8 collective-permute-start.27
  113.9 1.4 broadcast_select_fusion
  116.1 1.8 collective-permute-start.7
  118.2 17.8 %ending.2 = (bf16[6,16,128,128]{3,2,1,0:T(8,128)(2,1)}, f32[128,1152]{1,0:T(8,128)}) custom-call(s32[6]{0:T(128)} %stack.48.ids, bf16[6,4,128,128]{3,2,1,0:T(8,128)(2,1)} %get-tuple-element.35.refs_0_, bf16[6,4,128,128]{3,2,1,0:T(8,128)(2,1)} %get-tuple-element.36.refs_1_, bf16[6,4,128,128]{3,2,1,0:T(8,128)(2,1)} %collective-permute-done.4.refs_2_, ...), custom_call_target="tpu_custom_call" | custom-call | flops 9663676416 | bytes 15728640 | tf_op jit(solution)/shard_map/ending/pallas_call | solution.py:567
  137.1 4.9 %collective-permute-done.6.halo = bf16[8,4,128,128]{3,2,1,0:T(8,128)(2,1)S(1)} collective-permute-done((bf16[8,4,128,128]{3,2,1,0:T(8,128)(2,1)S(1)}, bf16[8,4,128,128]{3,2,1,0:T(8,128)(2,1)S(1)}, u32[]{:S(2)}, u32[]{:S(2)}) %collective-permute-start.6) | collective-permute-done | bytes 1048608 | tf_op jit(solution)/shard_map/ppermute | solution.py:702
  142.9 5.8 %second.2 = (bf16[6,4,128,128]{3,2,1,0:T(8,128)(2,1)}, bf16[6,4,128,128]{3,2,1,0:T(8,128)(2,1)}) custom-call(s32[6]{0:T(128)} %stack.48.ids, bf16[12,4,128,128]{3,2,1,0:T(8,128)(2,1)} %get-tuple-element.41.mid, bf16[8,4,128,128]{3,2,1,0:T(8,128)(2,1)} %copy-done.15, bf16[384,128]{1,0:T(8,128)(2,1)} %bitcast.73), custom_call_target="tpu_custom_call" | custom-call | flops 1207959552 | bytes 4718592 | tf_op jit(solution)/shard_map/second/pallas_call | solution.py:472
  148.8 13.3 %collective-permute-done.7.halo = bf16[8,4,128,128]{3,2,1,0:T(8,128)(2,1)S(1)} collective-permute-done((bf16[8,4,128,128]{3,2,1,0:T(8,128)(2,1)S(1)}, bf16[8,4,128,128]{3,2,1,0:T(8,128)(2,1)S(1)}, u32[]{:S(2)}, u32[]{:S(2)}) %collective-permute-start.7) | collective-permute-done | bytes 1048608 | tf_op jit(solution)/shard_map/ppermute | solution.py:702
  163.0 5.8 %second.3 = (bf16[6,4,128,128]{3,2,1,0:T(8,128)(2,1)}, bf16[6,4,128,128]{3,2,1,0:T(8,128)(2,1)}) custom-call(s32[6]{0:T(128)} %stack.48.ids, bf16[12,4,128,128]{3,2,1,0:T(8,128)(2,1)} %get-tuple-element.44.mid, bf16[8,4,128,128]{3,2,1,0:T(8,128)(2,1)} %copy-done.14, bf16[384,128]{1,0:T(8,128)(2,1)} %bitcast.74), custom_call_target="tpu_custom_call" | custom-call | flops 1207959552 | bytes 4718592 | tf_op jit(solution)/shard_map/second/pallas_call | solution.py:472
  169.9 1.6 collective-permute-start.11
  172.7 18.5 %ending.3 = (bf16[6,16,128,128]{3,2,1,0:T(8,128)(2,1)}, f32[128,1152]{1,0:T(8,128)}) custom-call(s32[6]{0:T(128)} %stack.50.ids, bf16[6,4,128,128]{3,2,1,0:T(8,128)(2,1)} %get-tuple-element.43.refs_0_, bf16[6,4,128,128]{3,2,1,0:T(8,128)(2,1)} %get-tuple-element.46.refs_1_, bf16[6,4,128,128]{3,2,1,0:T(8,128)(2,1)} %copy-done.16, ...), custom_call_target="tpu_custom_call" | custom-call | flops 9663676416 | bytes 15728640 | tf_op jit(solution)/shard_map/ending/pallas_call | solution.py:567
  192.3 1.8 collective-permute-start.12
  195.2 1.1 collective-permute-start.15
  197.1 4.1 %collective-permute-done.15 = f32[32,1152]{1,0:T(8,128)S(1)} collective-permute-done((f32[32,1152]{1,0:T(8,128)S(1)}, f32[32,1152]{1,0:T(8,128)S(1)}, u32[]{:S(2)}, u32[]{:S(2)}) %collective-permute-start.15) | collective-permute-done | bytes 147488 | tf_op jit(solution)/shard_map/ppermute | solution.py:621
  201.2 1.4 collective-permute-start.16
  202.7 1.9 collective-permute-start.13
  204.5 1.5 collective-permute-done.16
  206.1 1.5 collective-permute-start.17
  208.1 2.9 %collective-permute-done.17 = f32[8,1152]{1,0:T(8,128)S(1)} collective-permute-done((f32[8,1152]{1,0:T(8,128)S(1)}, f32[8,1152]{1,0:T(8,128)S(1)}, u32[]{:S(2)}, u32[]{:S(2)}) %collective-permute-start.17) | collective-permute-done | bytes 36896 | tf_op jit(solution)/shard_map/ppermute | solution.py:621
  211.1 1.4 collective-permute-start.30
  212.5 3.0 %collective-permute-done.18 = f32[2,8,1152]{2,1,0:T(8,128)S(1)} collective-permute-done((f32[2,8,1152]{2,1,0:T(8,128)S(1)}, f32[2,8,1152]{2,1,0:T(8,128)S(1)}, u32[]{:S(2)}, u32[]{:S(2)}) %collective-permute-start.18) | collective-permute-done | bytes 73760 | tf_op jit(solution)/shard_map/ppermute | solution.py:731
  215.5 1.6 collective-permute-start.19
  217.7 3.2 %collective-permute-done.19 = f32[2,8,1152]{2,1,0:T(8,128)S(1)} collective-permute-done((f32[2,8,1152]{2,1,0:T(8,128)S(1)}, f32[2,8,1152]{2,1,0:T(8,128)S(1)}, u32[]{:S(2)}, u32[]{:S(2)}) %collective-permute-start.19) | collective-permute-done | bytes 73760 | tf_op jit(solution)/shard_map/ppermute | solution.py:628
  220.9 1.9 collective-permute-start.20
  222.9 3.2 %collective-permute-done.20 = f32[2,16,1152]{2,1,0:T(8,128)S(1)} collective-permute-done((f32[2,16,1152]{2,1,0:T(8,128)S(1)}, f32[2,16,1152]{2,1,0:T(8,128)S(1)}, u32[]{:S(2)}, u32[]{:S(2)}) %collective-permute-start.20) | collective-permute-done | bytes 147488 | tf_op jit(solution)/shard_map/ppermute | solution.py:628
  226.2 1.3 collective-permute-start.21
  227.5 5.6 %collective-permute-done.21 = f32[2,32,1152]{2,1,0:T(8,128)} collective-permute-done((f32[2,32,1152]{2,1,0:T(8,128)S(1)}, f32[2,32,1152]{2,1,0:T(8,128)}, u32[]{:S(2)}, u32[]{:S(2)}) %collective-permute-start.21) | collective-permute-done | bytes 294944 | tf_op jit(solution)/shard_map/ppermute | solution.py:628
  233.0 1.9 maximum_select_fusion.3
  236.8 5.0 %select_bitcast_fusion = (bf16[1,6,16,128,128]{4,3,2,1,0:T(8,128)(2,1)}, bf16[1,6,16,128,128]{4,3,2,1,0:T(8,128)(2,1)}) fusion(bf16[6,16,128,128]{3,2,1,0:T(8,128)(2,1)} %get-tuple-element.49, bf16[6,16,128,128]{3,2,1,0:T(8,128)(2,1)S(1)} %copy-done, pred[]{:T(512)S(6)} %eq.16), kind=kLoop, calls=%fused_computation | loop fusion | flops 3145728 | bytes 12582913 | tf_op jit(solution)/shard_map/broadcast_in_dim | solution.py:746
  241.8 1.7 maximum_select_fusion
  (129 shorter events, 23.2 us)
Async XLA Ops:
  1.3 3.7 %copy-start.11 = (s32[2]{0:T(128)S(1)}, s32[2]{0:T(128)}, u32[]{:S(2)}) copy-start(s32[2]{0:T(128)} %param.15) | copy-start | bytes 28
  22.6 6.7 %copy-start.1 = (bf16[6,8,128,128]{3,2,1,0:T(8,128)(2,1)S(1)}, bf16[6,8,128,128]{3,2,1,0:T(8,128)(2,1)}, u32[]{:S(2)}) copy-start(bf16[6,8,128,128]{3,2,1,0:T(8,128)(2,1)} %get-tuple-element.31.own_in) | copy-start | bytes 4718596
  22.6 5.2 %collective-permute-start = (bf16[6,8,128,128]{3,2,1,0:T(8,128)(2,1)}, bf16[6,8,128,128]{3,2,1,0:T(8,128)(2,1)S(1)}, u32[]{:S(2)}, u32[]{:S(2)}) collective-permute-start(bf16[6,8,128,128]{3,2,1,0:T(8,128)(2,1)} %get-tuple-element.32), channel_id=1, source_target_pairs={{0,1},{1,0},{2,3},{3,2},{4,5},{5,4},{6,7},{7,6},{8,9},{9,8},{10,11... | collective-permute-start | bytes 4718600 | tf_op jit(solution)/shard_map/ppermute | solution.py:677
  23.1 6.4 %collective-permute-start.1 = (bf16[6,8,128,128]{3,2,1,0:T(8,128)(2,1)}, bf16[6,8,128,128]{3,2,1,0:T(8,128)(2,1)}, u32[]{:S(2)}, u32[]{:S(2)}) collective-permute-start(bf16[6,8,128,128]{3,2,1,0:T(8,128)(2,1)} %get-tuple-element.34), channel_id=1, source_target_pairs={{0,1},{1,0},{2,3},{3,2},{4,5},{5,4},{6,7},{7,6},{8,9},{9,8},{10,11... | collective-permute-start | bytes 4718600 | tf_op jit(solution)/shard_map/ppermute | solution.py:678
  27.8 5.5 %copy-start.3 = (bf16[6,8,128,128]{3,2,1,0:T(8,128)(2,1)}, bf16[6,8,128,128]{3,2,1,0:T(8,128)(2,1)S(1)}, u32[]{:S(2)}) copy-start(bf16[6,8,128,128]{3,2,1,0:T(8,128)(2,1)S(1)} %collective-permute-done.got_in) | copy-start | bytes 4718596
  29.3 1.4 copy-start.2
  33.5 27.0 %collective-permute-start.2 = (bf16[8,4,128,128]{3,2,1,0:T(8,128)(2,1)S(1)}, bf16[8,4,128,128]{3,2,1,0:T(8,128)(2,1)}, u32[]{:S(2)}, u32[]{:S(2)}) collective-permute-start(bf16[8,4,128,128]{3,2,1,0:T(8,128)(2,1)S(1)} %maximum_select_fusion.1), channel_id=1, source_target_pairs={{0,2},{2,0},{1,3},{3,1},{4,6},{6,4},{5,7},{7,5},{8,10},{10,8},{9,1... | collective-permute-start | bytes 3145736 | tf_op jit(solution)/shard_map/ppermute | solution.py:695
  36.4 1.6 copy-start.10
  36.6 45.9 %collective-permute-start.3 = (bf16[8,4,128,128]{3,2,1,0:T(8,128)(2,1)S(1)}, bf16[8,4,128,128]{3,2,1,0:T(8,128)(2,1)}, u32[]{:S(2)}, u32[]{:S(2)}) collective-permute-start(bf16[8,4,128,128]{3,2,1,0:T(8,128)(2,1)S(1)} %maximum_select_fusion.2), channel_id=1, source_target_pairs={{0,2},{2,0},{1,3},{3,1},{4,6},{6,4},{5,7},{7,5},{8,10},{10,8},{9,1... | collective-permute-start | bytes 3145736 | tf_op jit(solution)/shard_map/ppermute | solution.py:695
  72.4 22.0 %copy-start.9 = (f32[128,384]{1,0:T(8,128)S(1)}, f32[128,384]{1,0:T(8,128)}, u32[]{:S(2)}) copy-start(f32[128,384]{1,0:T(8,128)} %get-tuple-element.54) | copy-start | bytes 589828
  72.4 23.0 %copy-start.8 = (f32[128,384]{1,0:T(8,128)S(1)}, f32[128,384]{1,0:T(8,128)}, u32[]{:S(2)}) copy-start(f32[128,384]{1,0:T(8,128)} %get-tuple-element.52) | copy-start | bytes 589828
  95.4 14.7 %copy-start.5 = (bf16[3,3,128,128]{3,2,1,0:T(8,128)(2,1)S(1)}, bf16[3,3,128,128]{3,2,1,0:T(8,128)(2,1)}, u32[]{:S(2)}) copy-start(bf16[3,3,128,128]{3,2,1,0:T(8,128)(2,1)} %param.10) | copy-start | bytes 884740
  96.5 17.4 %copy-start.4 = (bf16[3,3,128,128]{3,2,1,0:T(8,128)(2,1)S(1)}, bf16[3,3,128,128]{3,2,1,0:T(8,128)(2,1)}, u32[]{:S(2)}) copy-start(bf16[3,3,128,128]{3,2,1,0:T(8,128)(2,1)} %param.11) | copy-start | bytes 884740
  96.5 1.5 collective-permute-start.23
  98.1 4.9 %collective-permute-start.24 = (f32[64,384]{1,0:T(8,128)S(1)}, f32[64,384]{1,0:T(8,128)S(1)}, u32[]{:S(2)}, u32[]{:S(2)}) collective-permute-start(f32[64,384]{1,0:T(8,128)S(1)} %constant_dynamic-slice_fusion.3), channel_id=1, source_target_pairs={{0,4},{1,5},{2,6},{3,7},{4,0},{5,1},{6,2},{7,3},{8,12},{9,13},{10,... | collective-permute-start | bytes 294920 | tf_op jit(solution)/shard_map/ppermute | solution.py:621
  103.0 4.2 %collective-permute-start.25 = (f32[32,384]{1,0:T(8,128)S(1)}, f32[32,384]{1,0:T(8,128)S(1)}, u32[]{:S(2)}, u32[]{:S(2)}) collective-permute-start(f32[32,384]{1,0:T(8,128)S(1)} %constant_dynamic-slice_fusion.2), channel_id=1, source_target_pairs={{0,8},{1,9},{2,10},{3,11},{4,12},{5,13},{6,14},{7,15},{8,0},{9,1},... | collective-permute-start | bytes 147464 | tf_op jit(solution)/shard_map/ppermute | solution.py:621
  107.2 4.8 %collective-permute-start.26 = (f32[16,384]{1,0:T(8,128)S(1)}, f32[16,384]{1,0:T(8,128)S(1)}, u32[]{:S(2)}, u32[]{:S(2)}) collective-permute-start(f32[16,384]{1,0:T(8,128)S(1)} %constant_dynamic-slice_fusion.1), channel_id=1, source_target_pairs={{0,16},{1,17},{2,18},{3,19},{4,20},{5,21},{6,22},{7,23},{8,24},{9,... | collective-permute-start | bytes 73736 | tf_op jit(solution)/shard_map/ppermute | solution.py:621
  110.1 5.8 %copy-start.13 = (bf16[8,4,128,128]{3,2,1,0:T(8,128)(2,1)S(1)}, bf16[8,4,128,128]{3,2,1,0:T(8,128)(2,1)}, u32[]{:S(2)}) copy-start(bf16[8,4,128,128]{3,2,1,0:T(8,128)(2,1)} %get-tuple-element.42) | copy-start | bytes 3145732
  110.1 6.0 %copy-start.12 = (bf16[8,4,128,128]{3,2,1,0:T(8,128)(2,1)S(1)}, bf16[8,4,128,128]{3,2,1,0:T(8,128)(2,1)}, u32[]{:S(2)}) copy-start(bf16[8,4,128,128]{3,2,1,0:T(8,128)(2,1)} %get-tuple-element.45) | copy-start | bytes 3145732
  110.4 7.8 %collective-permute-start.4 = (bf16[6,4,128,128]{3,2,1,0:T(8,128)(2,1)}, bf16[6,4,128,128]{3,2,1,0:T(8,128)(2,1)}, u32[]{:S(2)}, u32[]{:S(2)}) collective-permute-start(bf16[6,4,128,128]{3,2,1,0:T(8,128)(2,1)} %get-tuple-element.37), channel_id=1, source_target_pairs={{0,1},{1,0},{2,3},{3,2},{4,5},{5,4},{6,7},{7,6},{8,9},{9,8},{10,11... | collective-permute-start | bytes 2359304 | tf_op jit(solution)/shard_map/ppermute | solution.py:705
  110.4 7.7 %collective-permute-start.5 = (bf16[6,4,128,128]{3,2,1,0:T(8,128)(2,1)}, bf16[6,4,128,128]{3,2,1,0:T(8,128)(2,1)}, u32[]{:S(2)}, u32[]{:S(2)}) collective-permute-start(bf16[6,4,128,128]{3,2,1,0:T(8,128)(2,1)} %get-tuple-element.38), channel_id=1, source_target_pairs={{0,1},{1,0},{2,3},{3,2},{4,5},{5,4},{6,7},{7,6},{8,9},{9,8},{10,11... | collective-permute-start | bytes 2359304 | tf_op jit(solution)/shard_map/ppermute | solution.py:705
  112.0 5.9 %collective-permute-start.27 = (f32[8,384]{1,0:T(8,128)S(1)}, f32[8,384]{1,0:T(8,128)S(1)}, u32[]{:S(2)}, u32[]{:S(2)}) collective-permute-start(f32[8,384]{1,0:T(8,128)S(1)} %constant_dynamic-slice_fusion), channel_id=1, source_target_pairs={{0,2},{1,3},{2,0},{3,1},{4,6},{5,7},{6,4},{7,5},{8,10},{9,11},{10,... | collective-permute-start | bytes 36872 | tf_op jit(solution)/shard_map/ppermute | solution.py:621
  115.9 26.1 %collective-permute-start.6 = (bf16[8,4,128,128]{3,2,1,0:T(8,128)(2,1)S(1)}, bf16[8,4,128,128]{3,2,1,0:T(8,128)(2,1)S(1)}, u32[]{:S(2)}, u32[]{:S(2)}) collective-permute-start(bf16[8,4,128,128]{3,2,1,0:T(8,128)(2,1)S(1)} %copy-done.13), channel_id=1, source_target_pairs={{0,2},{2,0},{1,3},{3,1},{4,6},{6,4},{5,7},{7,5},{8,10},{10,8},{9,1... | collective-permute-start | bytes 3145736 | tf_op jit(solution)/shard_map/ppermute | solution.py:702
  116.1 45.9 %collective-permute-start.7 = (bf16[8,4,128,128]{3,2,1,0:T(8,128)(2,1)S(1)}, bf16[8,4,128,128]{3,2,1,0:T(8,128)(2,1)S(1)}, u32[]{:S(2)}, u32[]{:S(2)}) collective-permute-start(bf16[8,4,128,128]{3,2,1,0:T(8,128)(2,1)S(1)} %copy-done.12), channel_id=1, source_target_pairs={{0,2},{2,0},{1,3},{3,1},{4,6},{6,4},{5,7},{7,5},{8,10},{10,8},{9,1... | collective-permute-start | bytes 3145736 | tf_op jit(solution)/shard_map/ppermute | solution.py:702
  117.9 50.9 %collective-permute-start.28 = (f32[8,384]{1,0:T(8,128)S(1)}, f32[8,384]{1,0:T(8,128)S(1)}, u32[]{:S(2)}, u32[]{:S(2)}) collective-permute-start(f32[8,384]{1,0:T(8,128)S(1)} %dynamic-slice_add_fusion.12), channel_id=1, source_target_pairs={{0,2},{1,3},{2,0},{3,1},{4,6},{5,7},{6,4},{7,5},{8,10},{9,11},{10,... | collective-permute-start | bytes 36872 | tf_op jit(solution)/shard_map/ppermute | solution.py:628
  137.0 32.9 %collective-permute-start.10 = (f32[64,1152]{1,0:T(8,128)S(1)}, f32[64,1152]{1,0:T(8,128)S(1)}, u32[]{:S(2)}, u32[]{:S(2)}) collective-permute-start(f32[64,1152]{1,0:T(8,128)S(1)} %constant_dynamic-slice_fusion.12), channel_id=1, source_target_pairs={{0,1},{1,0},{2,3},{3,2},{4,5},{5,4},{6,7},{7,6},{8,9},{9,8},{10,11... | collective-permute-start | bytes 884744 | tf_op jit(solution)/shard_map/ppermute | solution.py:621
  142.0 1.0 copy-start.15
  148.8 22.7 %collective-permute-start.8 = (bf16[6,4,128,128]{3,2,1,0:T(8,128)(2,1)}, bf16[6,4,128,128]{3,2,1,0:T(8,128)(2,1)S(1)}, u32[]{:S(2)}, u32[]{:S(2)}) collective-permute-start(bf16[6,4,128,128]{3,2,1,0:T(8,128)(2,1)} %get-tuple-element.47), channel_id=1, source_target_pairs={{0,1},{1,0},{2,3},{3,2},{4,5},{5,4},{6,7},{7,6},{8,9},{9,8},{10,11... | collective-permute-start | bytes 2359304 | tf_op jit(solution)/shard_map/ppermute | solution.py:714
  163.0 6.8 %copy-start.6 = (f32[128,1152]{1,0:T(8,128)S(1)}, f32[128,1152]{1,0:T(8,128)}, u32[]{:S(2)}) copy-start(f32[128,1152]{1,0:T(8,128)} %get-tuple-element.50) | copy-start | bytes 1769476
  168.8 2.7 %collective-permute-start.9 = (bf16[6,4,128,128]{3,2,1,0:T(8,128)(2,1)}, bf16[6,4,128,128]{3,2,1,0:T(8,128)(2,1)S(1)}, u32[]{:S(2)}, u32[]{:S(2)}) collective-permute-start(bf16[6,4,128,128]{3,2,1,0:T(8,128)(2,1)} %get-tuple-element.48), channel_id=1, source_target_pairs={{0,1},{1,0},{2,3},{3,2},{4,5},{5,4},{6,7},{7,6},{8,9},{9,8},{10,11... | collective-permute-start | bytes 2359304 | tf_op jit(solution)/shard_map/ppermute | solution.py:714
  168.9 42.2 %collective-permute-start.29 = (f32[16,384]{1,0:T(8,128)S(1)}, f32[16,384]{1,0:T(8,128)S(1)}, u32[]{:S(2)}, u32[]{:S(2)}) collective-permute-start(f32[16,384]{1,0:T(8,128)S(1)} %maximum_select_fusion.11), channel_id=1, source_target_pairs={{0,16},{1,17},{2,18},{3,19},{4,20},{5,21},{6,22},{7,23},{8,24},{9,... | collective-permute-start | bytes 73736 | tf_op jit(solution)/shard_map/ppermute | solution.py:628
  169.9 22.4 %collective-permute-start.11 = (f32[32,1152]{1,0:T(8,128)S(1)}, f32[32,1152]{1,0:T(8,128)S(1)}, u32[]{:S(2)}, u32[]{:S(2)}) collective-permute-start(f32[32,1152]{1,0:T(8,128)S(1)} %constant_dynamic-slice_fusion.11), channel_id=1, source_target_pairs={{0,4},{1,5},{2,6},{3,7},{4,0},{5,1},{6,2},{7,3},{8,12},{9,13},{10,... | collective-permute-start | bytes 442376 | tf_op jit(solution)/shard_map/ppermute | solution.py:621
  171.5 1.2 copy-start.17
  192.2 1.9 collective-permute-start.14
  192.3 4.7 %collective-permute-start.12 = (f32[16,1152]{1,0:T(8,128)S(1)}, f32[16,1152]{1,0:T(8,128)S(1)}, u32[]{:S(2)}, u32[]{:S(2)}) collective-permute-start(f32[16,1152]{1,0:T(8,128)S(1)} %constant_dynamic-slice_fusion.10), channel_id=1, source_target_pairs={{0,8},{1,9},{2,10},{3,11},{4,12},{5,13},{6,14},{7,15},{8,0},{9,1},... | collective-permute-start | bytes 221192 | tf_op jit(solution)/shard_map/ppermute | solution.py:621
  195.2 6.0 %collective-permute-start.15 = (f32[32,1152]{1,0:T(8,128)S(1)}, f32[32,1152]{1,0:T(8,128)S(1)}, u32[]{:S(2)}, u32[]{:S(2)}) collective-permute-start(f32[32,1152]{1,0:T(8,128)S(1)} %constant_dynamic-slice_fusion.7), channel_id=1, source_target_pairs={{0,4},{1,5},{2,6},{3,7},{4,0},{5,1},{6,2},{7,3},{8,12},{9,13},{10,... | collective-permute-start | bytes 442376 | tf_op jit(solution)/shard_map/ppermute | solution.py:621
  201.2 4.8 %collective-permute-start.16 = (f32[16,1152]{1,0:T(8,128)S(1)}, f32[16,1152]{1,0:T(8,128)S(1)}, u32[]{:S(2)}, u32[]{:S(2)}) collective-permute-start(f32[16,1152]{1,0:T(8,128)S(1)} %constant_dynamic-slice_fusion.6), channel_id=1, source_target_pairs={{0,8},{1,9},{2,10},{3,11},{4,12},{5,13},{6,14},{7,15},{8,0},{9,1},... | collective-permute-start | bytes 221192 | tf_op jit(solution)/shard_map/ppermute | solution.py:621
  202.7 5.5 %collective-permute-start.13 = (f32[8,1152]{1,0:T(8,128)S(1)}, f32[8,1152]{1,0:T(8,128)S(1)}, u32[]{:S(2)}, u32[]{:S(2)}) collective-permute-start(f32[8,1152]{1,0:T(8,128)S(1)} %constant_dynamic-slice_fusion.9), channel_id=1, source_target_pairs={{0,16},{1,17},{2,18},{3,19},{4,20},{5,21},{6,22},{7,23},{8,24},{9,... | collective-permute-start | bytes 110600 | tf_op jit(solution)/shard_map/ppermute | solution.py:621
  206.1 4.9 %collective-permute-start.17 = (f32[8,1152]{1,0:T(8,128)S(1)}, f32[8,1152]{1,0:T(8,128)S(1)}, u32[]{:S(2)}, u32[]{:S(2)}) collective-permute-start(f32[8,1152]{1,0:T(8,128)S(1)} %constant_dynamic-slice_fusion.5), channel_id=1, source_target_pairs={{0,16},{1,17},{2,18},{3,19},{4,20},{5,21},{6,22},{7,23},{8,24},{9,... | collective-permute-start | bytes 110600 | tf_op jit(solution)/shard_map/ppermute | solution.py:621
  211.0 4.4 %collective-permute-start.18 = (f32[2,8,1152]{2,1,0:T(8,128)S(1)}, f32[2,8,1152]{2,1,0:T(8,128)S(1)}, u32[]{:S(2)}, u32[]{:S(2)}) collective-permute-start(f32[2,8,1152]{2,1,0:T(8,128)S(1)} %pad_maximum_fusion), channel_id=1, source_target_pairs={{0,2},{1,3},{2,0},{3,1},{4,6},{5,7},{6,4},{7,5},{8,10},{9,11},{10,... | collective-permute-start | bytes 221192 | tf_op jit(solution)/shard_map/ppermute | solution.py:731
  211.1 6.0 %collective-permute-start.30 = (f32[32,384]{1,0:T(8,128)S(1)}, f32[32,384]{1,0:T(8,128)S(1)}, u32[]{:S(2)}, u32[]{:S(2)}) collective-permute-start(f32[32,384]{1,0:T(8,128)S(1)} %maximum_select_fusion.10), channel_id=1, source_target_pairs={{0,8},{1,9},{2,10},{3,11},{4,12},{5,13},{6,14},{7,15},{8,0},{9,1},... | collective-permute-start | bytes 147464 | tf_op jit(solution)/shard_map/ppermute | solution.py:628
  215.5 5.4 %collective-permute-start.19 = (f32[2,8,1152]{2,1,0:T(8,128)S(1)}, f32[2,8,1152]{2,1,0:T(8,128)S(1)}, u32[]{:S(2)}, u32[]{:S(2)}) collective-permute-start(f32[2,8,1152]{2,1,0:T(8,128)S(1)} %maximum_select_fusion.9), channel_id=1, source_target_pairs={{0,16},{1,17},{2,18},{3,19},{4,20},{5,21},{6,22},{7,23},{8,24},{9,... | collective-permute-start | bytes 221192 | tf_op jit(solution)/shard_map/ppermute | solution.py:628
  217.1 5.7 %collective-permute-start.31 = (f32[64,384]{1,0:T(8,128)S(1)}, f32[64,384]{1,0:T(8,128)S(1)}, u32[]{:S(2)}, u32[]{:S(2)}) collective-permute-start(f32[64,384]{1,0:T(8,128)S(1)} %maximum_select_fusion.8), channel_id=1, source_target_pairs={{0,4},{1,5},{2,6},{3,7},{4,0},{5,1},{6,2},{7,3},{8,12},{9,13},{10,... | collective-permute-start | bytes 294920 | tf_op jit(solution)/shard_map/ppermute | solution.py:628
  220.9 5.2 %collective-permute-start.20 = (f32[2,16,1152]{2,1,0:T(8,128)S(1)}, f32[2,16,1152]{2,1,0:T(8,128)S(1)}, u32[]{:S(2)}, u32[]{:S(2)}) collective-permute-start(f32[2,16,1152]{2,1,0:T(8,128)S(1)} %maximum_select_fusion.7), channel_id=1, source_target_pairs={{0,8},{1,9},{2,10},{3,11},{4,12},{5,13},{6,14},{7,15},{8,0},{9,1},... | collective-permute-start | bytes 442376 | tf_op jit(solution)/shard_map/ppermute | solution.py:628
  222.8 4.6 %collective-permute-start.32 = (f32[128,384]{1,0:T(8,128)S(1)}, f32[128,384]{1,0:T(8,128)S(1)}, u32[]{:S(2)}, u32[]{:S(2)}) collective-permute-start(f32[128,384]{1,0:T(8,128)S(1)} %maximum_select_fusion.6), channel_id=1, source_target_pairs={{0,1},{1,0},{2,3},{3,2},{4,5},{5,4},{6,7},{7,6},{8,9},{9,8},{10,11... | collective-permute-start | bytes 589832 | tf_op jit(solution)/shard_map/ppermute | solution.py:628
  226.2 6.9 %collective-permute-start.21 = (f32[2,32,1152]{2,1,0:T(8,128)S(1)}, f32[2,32,1152]{2,1,0:T(8,128)}, u32[]{:S(2)}, u32[]{:S(2)}) collective-permute-start(f32[2,32,1152]{2,1,0:T(8,128)S(1)} %maximum_select_fusion.5), channel_id=1, source_target_pairs={{0,4},{1,5},{2,6},{3,7},{4,0},{5,1},{6,2},{7,3},{8,12},{9,13},{10,... | collective-permute-start | bytes 884744 | tf_op jit(solution)/shard_map/ppermute | solution.py:628
  227.5 9.3 %copy-start = (bf16[6,16,128,128]{3,2,1,0:T(8,128)(2,1)S(1)}, bf16[6,16,128,128]{3,2,1,0:T(8,128)(2,1)}, u32[]{:S(2)}) copy-start(bf16[6,16,128,128]{3,2,1,0:T(8,128)(2,1)} %get-tuple-element.40) | copy-start | bytes 9437188
  235.0 6.8 %collective-permute-start.22 = (f32[2,64,1152]{2,1,0:T(8,128)}, f32[2,64,1152]{2,1,0:T(8,128)}, u32[]{:S(2)}, u32[]{:S(2)}) collective-permute-start(f32[2,64,1152]{2,1,0:T(8,128)} %maximum_select_fusion.3), channel_id=1, source_target_pairs={{0,1},{1,0},{2,3},{3,2},{4,5},{5,4},{6,7},{7,6},{8,9},{9,8},{10,11... | collective-permute-start | bytes 1769480 | tf_op jit(solution)/shard_map/ppermute | solution.py:628
  (3 other events, 2.8 us)

commit v2 on v1

--- a/solution.py
+++ b/solution.py
@@ -196,113 +196,137 @@
     )
 
 
-def cost(flops, nbytes):
-    return pl.CostEstimate(flops=int(flops), bytes_accessed=int(nbytes), transcendentals=0)
-
-
-def zero_borders(pad, pairs):
+COST = 0.1
+
+
+def cost(micros):
+    return pl.CostEstimate(flops=int(micros * COST * 1e9), bytes_accessed=1000, transcendentals=0)
+
+
+def pair_range(chunk, rows):
+    size = rows // CHUNKS
+    low = 0 if chunk == 0 else chunk * size // 2 - 1
+    high = rows // 2 if chunk == CHUNKS - 1 else (chunk + 1) * size // 2 - 1
+    return low, high
+
+
+def seen_rows(low, high, rows):
+    return max(0, 2 * low - 1), min(rows, 2 * high + 1)
+
+
+def zero_borders(pad, pairs, low, high, rows):
     pad[...] = jnp.zeros(pad.shape, F32)
-    lanes = pairs.shape[2]
-    width = pairs.shape[1]
-    pairs[0, :, 0 : lanes // 2] = jnp.zeros((width, lanes // 2), BF)
-    pairs[pairs.shape[0] - 1, :, lanes // 2 : lanes] = jnp.zeros((width, lanes // 2), BF)
-
-
-def fill_pairs(frame, pad, pairs):
-    rows, width, chans = frame.shape
-    pad[:, 8 : 8 + width, :] = frame[...].astype(F32)
-    for shift in range(3):
-        if shift == 1:
-            seen = frame[...]
-        else:
-            seen = pad[:, 7 + shift : 7 + shift + width, :].astype(BF)
-        seen = seen.reshape(rows // 2, 2, width, chans)
-        low = shift * chans
-        pairs[0 : rows // 2, :, (3 * chans + low) : (3 * chans + low + chans)] = seen[:, 0]
-        pairs[1 : rows // 2 + 1, :, low : low + chans] = seen[:, 1]
-
-
-def two_row_conv(pairs, weights, first, count):
-    width = pairs.shape[1]
-    lanes = pairs.shape[2]
-    upper = pairs[first : first + count].reshape(count * width, lanes)
-    lower = pairs[first + 1 : first + 1 + count].reshape(count * width, lanes)
-    return jnp.dot(
-        jnp.concatenate([upper, lower], axis=1), weights[...], preferred_element_type=F32
-    )
-
-
-def front_kernel(
-    ids, latents, cotangent, w_in, w_back,
-    act_keep, act_send, back_keep, back_send, slope,
-    pad, pairs, frame, result,
-):
+    frames, _, width, lanes = pairs.shape
+    for frame in range(frames):
+        if low == 0:
+            pairs[frame, 0, :, 0 : lanes // 2] = jnp.zeros((width, lanes // 2), BF)
+        if 2 * high == rows:
+            pairs[frame, high - low, :, lanes // 2 : lanes] = jnp.zeros((width, lanes // 2), BF)
+
+
+def fill_pairs(read_row, pad, pairs, low, high, rows):
+    frames, _, width, lanes = pairs.shape
+    chans = lanes // 6
+    begin, end = seen_rows(low, high, rows)
+    for frame in range(frames):
+        for row in range(begin, end):
+            pad[frame, row - begin, 8 : 8 + width, :] = read_row(frame, row).astype(F32)
+    for frame in range(frames):
+        for row in range(begin, end):
+            at = (row + 1) // 2 - low
+            side = 3 * chans * (1 - row % 2)
+            pairs[frame, at, :, side + chans : side + 2 * chans] = read_row(frame, row)
+            for shift in (0, 2):
+                seen = pad[frame, row - begin, 7 + shift : 7 + shift + width, :].astype(BF)
+                lane = side + shift * chans
+                pairs[frame, at, :, lane : lane + chans] = seen
+
+
+def front_kernel(ids, *refs):
+    latents, cotangent = refs[0:2], refs[2:4]
+    w_in, w_back, act, back, slope, pad, pairs = refs[4:]
     at = pl.program_id(0)
-    core = ids[1]
-    rows, width, chans = frame.shape
-    half = rows // 2
-    step = half // 2
+    core, shift_rows = ids[1], ids[7]
+    spread, width, chans = latents[0].shape[1:]
+    count = spread // 2 - 1
+    lanes = 6 * chans
+    slots = pl.num_programs(0)
 
     @pl.when(at == 0)
     def _():
-        zero_borders(pad, pairs)
-
-    frame[...] = latents[0]
-    fill_pairs(frame, pad, pairs)
-    for part in range(2):
-        pre = two_row_conv(pairs, w_in, part * step, step)
-        sigma = jax.nn.sigmoid(pre)
-        act = (pre * sigma).astype(BF).reshape(step, width, 2 * chans)
-        grad = (sigma * (1.0 + pre * (1.0 - sigma))).astype(BF).reshape(step, width, 2 * chans)
-        for pair in range(step):
-            for odd in range(2):
-                row = part * half + 2 * pair + odd
-                lanes = slice(odd * chans, odd * chans + chans)
-                result[row] = act[pair, :, lanes]
-                slope[0, row] = grad[pair, :, lanes]
-    act_keep[0] = result[pl.ds(core * half, half)]
-    act_send[0] = result[pl.ds(half - core * half, half)]
-
-    keep = jnp.where(at < ids[2], 1.0, 0.0).astype(F32)
-    frame[...] = (cotangent[0].astype(F32) * keep).astype(BF)
-    fill_pairs(frame, pad, pairs)
-    for part in range(2):
-        back = two_row_conv(pairs, w_back, part * step, step)
-        back = back.astype(BF).reshape(step, width, 2 * chans)
-        for pair in range(step):
-            for odd in range(2):
-                row = part * half + 2 * pair + odd
-                result[row] = back[pair, :, odd * chans : odd * chans + chans]
-    back_keep[0] = result[pl.ds(core * half, half)]
-    back_send[0] = result[pl.ds(half - core * half, half)]
+        pad[...] = jnp.zeros(pad.shape, F32)
+
+    def conv(blocks, weights):
+        for index in range(2):
+            for row in range(spread):
+                place = index * (spread + 2) + 1 + row
+                pad[place, 8 : 8 + width, :] = blocks[index][0, row].astype(F32)
+        for index in range(2):
+            for row in range(spread):
+                place = index * (spread + 2) + 1 + row + shift_rows
+                side = 3 * chans * (row % 2)
+                to = index * (count + 1) + row // 2
+                for shift in range(3):
+                    seen = pad[place, 7 + shift : 7 + shift + width, :].astype(BF)
+                    pairs[to, :, side + shift * chans : side + (shift + 1) * chans] = seen
+        stacked = []
+        for lower in range(2):
+            both = [
+                pairs[index * (count + 1) + lower : index * (count + 1) + lower + count]
+                for index in range(2)
+            ]
+            stacked.append(jnp.concatenate(both, axis=0).reshape(2 * count * width, lanes))
+        return jnp.dot(
+            jnp.concatenate(stacked, axis=1), weights[...], preferred_element_type=F32
+        )
+
+    def store(target, values):
+        values = values.reshape(2 * count, width, 2 * chans)
+        for index in range(2):
+            owner = core if index == 0 else 1 - core
+            for row in range(2 * count):
+                lane = row % 2 * chans
+                target[owner, 0, row] = values[index * count + row // 2, :, lane : lane + chans]
+
+    pre = conv(latents, w_in)
+    sigma = jax.nn.sigmoid(pre)
+    store(act, (pre * sigma).astype(BF))
+    store(slope, (sigma * (1.0 + pre * (1.0 - sigma))).astype(BF))
+    summed = conv(cotangent, w_back)
+    half = count * width
+    mine = jnp.where(core * slots + at < ids[2], 1.0, 0.0).astype(F32)
+    other = jnp.where((1 - core) * slots + at < ids[2], 1.0, 0.0).astype(F32)
+    store(back, jnp.concatenate([summed[:half] * mine, summed[half:] * other], 0).astype(BF))
 
 
 def front(ids, latents, cotangent, w_in, w_back):
-    slots, rows, width, chans = latents.shape
-    half = rows // 2
-    whole = pl.BlockSpec((1, rows, width, chans), lambda i, ids: (i, 0, 0, 0))
-    part = pl.BlockSpec((1, half, width, chans), lambda i, ids: (i, 0, 0, 0))
+    slots, spread, width, chans = latents[1].shape
+    rows = spread - 2
+    own = pl.BlockSpec(
+        (pl.Element(1), pl.Element(spread), pl.Element(width), pl.Element(chans)),
+        lambda i, ids: (i, ids[6], 0, 0),
+    )
+    got = pl.BlockSpec((1, spread, width, chans), lambda i, ids: (i, 0, 0, 0))
+    target = pl.BlockSpec((2, 1, rows, width, chans), lambda i, ids: (0, i, 0, 0, 0))
     fixed = pl.BlockSpec(w_in.shape, lambda i, ids: (0, 0))
-    halves = jax.ShapeDtypeStruct((slots, half, width, chans), BF)
-    return pl.pallas_call(
+    made = pl.pallas_call(
         front_kernel,
         grid_spec=pltpu.PrefetchScalarGridSpec(
             num_scalar_prefetch=1,
             grid=(slots,),
-            in_specs=[whole, whole, fixed, fixed],
-            out_specs=[part, part, part, part, whole],
+            in_specs=[own, got, own, got, fixed, fixed],
+            out_specs=[target] * 3,
             scratch_shapes=[
-                pltpu.VMEM((rows, width + 16, chans), F32),
-                pltpu.VMEM((half + 1, width, 6 * chans), BF),
-                pltpu.VMEM((rows, width, chans), BF),
-                pltpu.VMEM((rows, width, chans), BF),
+                pltpu.VMEM((2 * (spread + 2), width + 16, chans), F32),
+                pltpu.VMEM((spread, width, 6 * chans), BF),
             ],
         ),
-        out_shape=[halves, halves, halves, halves, jax.ShapeDtypeStruct(latents.shape, BF)],
+        out_shape=[jax.ShapeDtypeStruct((2, slots, rows, width, chans), BF)] * 3,
         compiler_params=params(),
-        cost_estimate=cost(4 * latents.size * chans * 12, 10 * latents.size),
+        cost_estimate=cost(22.0 / CHUNKS),
         name="front",
-    )(ids, latents, cotangent, w_in, w_back)
+    )(ids, *latents, *cotangent, w_in, w_back)
+    return [value.reshape(2 * slots, rows, width, chans) for value in made]
 
 
 def taps_of(held, start, step, count):
@@ -319,14 +343,14 @@
 
 
 def middle_kernel(
-    ids, own_in, got_in, own_back, got_back, halo, w_mid, w_mid_back, w_first,
+    ids, act_in, act_back, slope, halo, w_mid, w_mid_back, w_first,
     mid_send, mid_keep, first_keep, first_send, grad_first, grad_second,
     held_in, held_back, held_mid, result,
 ):
     at = pl.program_id(0)
     side, core, near, far = ids[0], ids[1], ids[3], ids[4]
-    slots = own_in.shape[0]
-    frames = 2 * slots
+    frames = act_in.shape[0]
+    slots = frames // 2
     mine = core * slots
     other = slots - mine
 
@@ -340,10 +364,8 @@
         grad_first[...] = jnp.zeros_like(grad_first)
         grad_second[...] = jnp.zeros_like(grad_second)
 
-    held_in[pl.ds(REACH + mine, slots)] = own_in[:, 0]
-    held_in[pl.ds(REACH + other, slots)] = got_in[:, 0]
-    held_back[pl.ds(mine, slots)] = own_back[:, 0]
-    held_back[pl.ds(other, slots)] = got_back[:, 0]
+    held_in[REACH : REACH + frames] = act_in[:, 0]
+    held_back[0:frames] = act_back[:, 0]
 
     @pl.when(side == 0)
     def _():
@@ -383,15 +405,18 @@
         taps_of(held_mid, REACH, step, frames), w_first[...], preferred_element_type=F32
     )
     result[...] = first.astype(BF).reshape(frames, size, chans)
+
+    @pl.when(side == 1)
+    def _():
+        result[...] = (result[...].astype(F32) * slope[:, 0].astype(F32)).astype(BF)
+
     first_keep[:, 0] = result[pl.ds(mine, slots)]
     first_send[:, 0] = result[pl.ds(other, slots)]
 
 
-def middle(chunk, ids, own_in, got_in, own_back, got_back, halo, w_mid, w_mid_back, w_first):
-    slots, half, width, chans = own_in.shape
-    frames = 2 * slots
-    rows = halo.shape[1]
-    source = pl.BlockSpec((slots, 1, width, chans), lambda i, ids: (0, chunk * rows + i, 0, 0))
+def middle(ids, act_in, act_back, slope, halo, w_mid, w_mid_back, w_first):
+    frames, rows, width, chans = act_in.shape
+    slots = frames // 2
     fixed = pl.BlockSpec(w_mid.shape, lambda i, ids: (0, 0))
     sums = pl.BlockSpec((chans, TAPS * chans), lambda i, ids: (0, 0))
 
@@ -407,7 +432,7 @@
         grid_spec=pltpu.PrefetchScalarGridSpec(
             num_scalar_prefetch=1,
             grid=(rows,),
-            in_specs=[source, source, source, source, rowwise(REACH), fixed, fixed, fixed],
+            in_specs=[rowwise(frames)] * 3 + [rowwise(REACH), fixed, fixed, fixed],
             out_specs=[
                 rowwise(REACH), rowwise(frames), rowwise(slots), rowwise(slots), sums, sums,
             ],
@@ -422,14 +447,12 @@
             shaped(REACH), shaped(frames), shaped(slots), shaped(slots), summed, summed,
         ],
         compiler_params=params(),
-        cost_estimate=cost(
-            2 * frames * rows * width * chans * chans * 30, 14 * frames * rows * width * chans
-        ),
+        cost_estimate=cost(24.0 / CHUNKS),
         name="middle",
-    )(ids, own_in, got_in, own_back, got_back, halo, w_mid, w_mid_back, w_first)
-
-
-def second_kernel(ids, mid, halo, w_second, keep, send, held, result):
+    )(ids, act_in, act_back, slope, halo, w_mid, w_mid_back, w_first)
+
+
+def second_kernel(ids, mid, slope, halo, w_second, keep, send, held, result):
     at = pl.program_id(0)
     side, core, near, far = ids[0], ids[1], ids[3], ids[4]
     frames = mid.shape[0]
@@ -457,11 +480,16 @@
         taps_of(held, REACH, step, frames), w_second[...], preferred_element_type=F32
     )
     result[...] = made.astype(BF).reshape(result.shape)
+
+    @pl.when(side == 0)
+    def _():
+        result[...] = (result[...].astype(F32) * slope[:, 0].astype(F32)).astype(BF)
+
     keep[:, 0] = result[pl.ds(mine, slots)]
     send[:, 0] = result[pl.ds(slots - mine, slots)]
 
 
-def second(ids, mid, halo, w_second):
+def second(ids, mid, slope, halo, w_second):
     frames, rows, width, chans = mid.shape
     slots = frames // 2
 
@@ -475,7 +503,7 @@
             num_scalar_prefetch=1,
             grid=(rows,),
             in_specs=[
-                rowwise(frames), rowwise(REACH),
+                rowwise(frames), rowwise(frames), rowwise(REACH),
                 pl.BlockSpec(w_second.shape, lambda i, ids: (0, 0)),
             ],
             out_specs=[rowwise(slots), rowwise(slots)],
@@ -486,108 +514,143 @@
         ),
         out_shape=[shape, shape],
         compiler_params=params(),
-        cost_estimate=cost(2 * mid.size * chans * 6, 6 * mid.size),
+        cost_estimate=cost(10.0 / CHUNKS),
         name="second",
-    )(ids, mid, halo, w_second)
-
-
-def ending_kernel(factor, ids, *refs):
-    own, got = refs[0:CHUNKS], refs[CHUNKS : 2 * CHUNKS]
-    latents, cotangent, slope, weights, out, sums, pad, pairs, frame, beside, total = refs[
-        2 * CHUNKS :
-    ]
+    )(ids, mid, slope, halo, w_second)
+
+
+def ending_kernel(chunk, rows, factor, with_outs, ids, *refs):
+    refs = list(refs)
+    used = 1 if chunk == 0 else 2
+    own = [refs.pop(0) for _ in range(used)]
+    got = [refs.pop(0) for _ in range(used)]
+    latents, cotangent, weights, before = [refs.pop(0) for _ in range(4)]
+    if with_outs:
+        refs.pop(0), refs.pop(0)
+    outs = (refs.pop(0), refs.pop(0))
+    sums, pad, pairs, frame, buffer, sems, beside, total = refs
     at = pl.program_id(0)
+    last = pl.num_programs(0) - 1
     core, role = ids[1], ids[5]
-    rows, width, chans = frame.shape
-    half = rows // 2
-    step = half // 2
-    piece = half // CHUNKS
+    frames, _, width, lanes = pairs.shape
+    chans = lanes // 6
+    low, high = pair_range(chunk, rows)
+    size = rows // CHUNKS
+    half = size // 2
+    base = (chunk + 1 - used) * size
+    count = high - low
+
+    def each_copy(step, act):
+        for way in range(2):
+            @pl.when(role == way)
+            def _():
+                target = outs[way].at[pl.ds(step * frames, frames), pl.ds(2 * low, 2 * count)]
+                act(pltpu.make_async_copy(buffer.at[step % 2], target, sems.at[step % 2]))
 
     @pl.when(at == 0)
     def _():
-        zero_borders(pad, pairs)
+        zero_borders(pad, pairs, low, high, rows)
         total[...] = jnp.zeros_like(total)
 
-    for chunk in range(CHUNKS):
-        frame[pl.ds(core * half + chunk * piece, piece)] = own[chunk][0]
-        frame[pl.ds(half - core * half + chunk * piece, piece)] = got[chunk][0]
-
-    @pl.when(role == 1)
-    def _():
-        frame[...] = (frame[...].astype(F32) * slope[0].astype(F32)).astype(BF)
-
-    fill_pairs(frame, pad, pairs)
-    valid = jnp.where(at < ids[2], 1.0, 0.0).astype(F32)
-
-    @pl.when(role == 0)
-    def _():
-        masked = (cotangent[0].astype(F32) * valid).astype(BF)
-        masked = masked.reshape(half, 2, width, chans)
-        beside[:, :, 0:chans] = masked[:, 0]
-        beside[:, :, chans : 2 * chans] = masked[:, 1]
-        frame[...] = latents[0]
-
-    @pl.when(role == 1)
-    def _():
-        plain = latents[0].reshape(half, 2, width, chans)
-        beside[:, :, 0:chans] = plain[:, 0]
-        beside[:, :, chans : 2 * chans] = plain[:, 1]
-        frame[...] = cotangent[0]
-
-    scale = jnp.where(role == 0, valid, 1.0).astype(F32)
+    @pl.when(at >= 2)
+    def _():
+        each_copy(at - 2, lambda copy: copy.wait())
+
+    for index in range(used):
+        frame[:, pl.ds(index * size + core * half, half)] = own[index][...]
+        frame[:, pl.ds(index * size + half - core * half, half)] = got[index][...]
+    fill_pairs(lambda which, row: frame[which, row - base], pad, pairs, low, high, rows)
+    slot = at % 2
+    one = jnp.where(role == 1, 1.0, 0.0).astype(F32)
+    for which in range(frames):
+        place = (core * (last + 1) + at) * frames + which
+        valid = jnp.where(place < ids[2], 1.0, 0.0).astype(F32)
+        zero = (1.0 - one) * valid
+        upper = pairs[which, 0:count].reshape(count * width, lanes)
+        lower = pairs[which, 1 : 1 + count].reshape(count * width, lanes)
+        made = jnp.dot(
+            jnp.concatenate([upper, lower], axis=1), weights[...], preferred_element_type=F32
+        )
+        made = made.reshape(count, width, 2 * chans)
+        for row in range(2 * count):
+            lane = row % 2 * chans
+            latent = latents[which, row].astype(F32)
+            arriving = cotangent[which, row].astype(F32)
+            beside[which, row // 2, :, lane : lane + chans] = (
+                latent * one + arriving * zero
+            ).astype(BF)
+            buffer[slot, which, row] = (
+                latent * zero
+                + arriving * (one * valid)
+                + made[row // 2, :, lane : lane + chans] * (one + zero)
+            ).astype(BF)
+    flat = beside[...].reshape(frames * count * width, 2 * chans)
     for part in range(2):
-        made = two_row_conv(pairs, weights, part * step, step) * scale
-        made = made.reshape(step, width, 2 * chans)
-        for pair in range(step):
-            for odd in range(2):
-                row = part * half + 2 * pair + odd
-                plus = frame[row].astype(F32) * valid
-                out[0, row] = (plus + made[pair, :, odd * chans : odd * chans + chans]).astype(BF)
-
-    lanes = pairs.shape[2]
-    flat = beside[...].reshape(half * width, 2 * chans)
-    for part in range(2):
-        seen = pairs[part : part + half].reshape(half * width, lanes)
+        seen = pairs[:, part : part + count].reshape(frames * count * width, lanes)
         total[:, part * lanes : (part + 1) * lanes] += outer(flat, seen)
-
-    @pl.when(at == pl.num_programs(0) - 1)
+    each_copy(at, lambda copy: copy.start())
+
+    @pl.when(at == last)
     def _():
         span = 9 * chans
-        sums[...] = factor * (
+        sums[...] = before[...] + factor * (
             total[0:chans, 0:span] + total[chans : 2 * chans, 3 * chans : 3 * chans + span]
         )
-
-
-def ending(factor, ids, own, got, latents, cotangent, slope, weights):
+        each_copy(at - 1, lambda copy: copy.wait())
+        each_copy(at, lambda copy: copy.wait())
+
+
+def ending(chunk, factor, ids, own, got, latents, cotangent, weights, before, outs=None):
     slots, rows, width, chans = latents.shape
-    half = rows // 2
-    whole = pl.BlockSpec((1, rows, width, chans), lambda i, ids: (i, 0, 0, 0))
-    part = pl.BlockSpec((1, half // CHUNKS, width, chans), lambda i, ids: (i, 0, 0, 0))
-    gated = pl.BlockSpec((1, rows, width, chans), lambda i, ids: (i * ids[5], 0, 0, 0))
+    size = rows // CHUNKS
+    low, high = pair_range(chunk, rows)
+    count = high - low
+    begin, end = seen_rows(low, high, rows)
+    used = 1 if chunk == 0 else 2
+    each = 2
+    area = pl.BlockSpec(
+        (pl.Element(each), pl.Element(2 * count), pl.Element(width), pl.Element(chans)),
+        lambda i, ids: (i * each, 2 * low, 0, 0),
+    )
+    part = pl.BlockSpec((each, size // 2, width, chans), lambda i, ids: (i, 0, 0, 0))
+    summed = pl.BlockSpec((chans, 9 * chans), lambda i, ids: (0, 0))
+    anywhere = pl.BlockSpec(memory_space=pl.ANY)
+    pick = slice(chunk + 1 - used, chunk + 1)
+    args = [*own[pick], *got[pick], latents, cotangent, weights, before]
+    in_specs = [part] * (2 * used) + [area, area]
+    in_specs += [pl.BlockSpec(weights.shape, lambda i, ids: (0, 0)), summed]
+    aliases = {}
+    if outs is not None:
+        aliases = {1 + len(args): 0, 2 + len(args): 1}
+        args += list(outs)
+        in_specs += [anywhere, anywhere]
     return pl.pallas_call(
-        functools.partial(ending_kernel, factor),
+        functools.partial(ending_kernel, chunk, rows, factor, outs is not None),
         grid_spec=pltpu.PrefetchScalarGridSpec(
             num_scalar_prefetch=1,
-            grid=(slots,),
-            in_specs=[part] * (2 * CHUNKS)
-            + [whole, whole, gated, pl.BlockSpec(weights.shape, lambda i, ids: (0, 0))],
-            out_specs=[whole, pl.BlockSpec((chans, 9 * chans), lambda i, ids: (0, 0))],
+            grid=(slots // each,),
+            in_specs=in_specs,
+            out_specs=[anywhere, anywhere, summed],
             scratch_shapes=[
-                pltpu.VMEM((rows, width + 16, chans), F32),
-                pltpu.VMEM((half + 1, width, 6 * chans), BF),
-                pltpu.VMEM((rows, width, chans), BF),
-                pltpu.VMEM((half, width, 2 * chans), BF),
+                pltpu.VMEM((each, end - begin, width + 16, chans), F32),
+                pltpu.VMEM((each, count + 1, width, 6 * chans), BF),
+                pltpu.VMEM((each, used * size, width, chans), BF),
+                pltpu.VMEM((2, each, 2 * count, width, chans), BF),
+                pltpu.SemaphoreType.DMA((2,)),
+                pltpu.VMEM((each, count, width, 2 * chans), BF),
                 pltpu.VMEM((2 * chans, 12 * chans), F32),
             ],
         ),
         out_shape=[
             jax.ShapeDtypeStruct(latents.shape, BF),
+            jax.ShapeDtypeStruct(latents.shape, BF),
             jax.ShapeDtypeStruct((chans, 9 * chans), F32),
         ],
+        input_output_aliases=aliases,
         compiler_params=params(),
-        cost_estimate=cost(4 * latents.size * chans * 12, 10 * latents.size),
+        cost_estimate=cost(26.0 / CHUNKS),
         name="ending",
-    )(ids, *own, *got, latents, cotangent, slope, weights)
+    )(ids, *args)
 
 
 def two_row_weights(kernel):
@@ -596,6 +659,10 @@
     return jnp.concatenate(
         [jnp.pad(flat, ((0, shift), (0, 0))), jnp.pad(flat, ((shift, 0), (0, 0)))], axis=1
     )
+
+
+def after(value, *earlier):
+    return lax.optimization_barrier((value,) + earlier)[0]
 
 
 def turned(kernel):
@@ -654,7 +721,7 @@
 
     def ids_for(role):
         return jnp.stack(
-            [side, core, frame_counts[0] - tm_index * slots, dilations[0], dilations[1], role]
+            [side, core, frame_counts[0] - side * 2 * slots, dilations[0], dilations[1], role]
         ).astype(jnp.int32)
 
     ids = ids_for(side)
@@ -670,85 +737,101 @@
     w_one_back = jnp.transpose(first_temporal, (0, 2, 1)).reshape(-1, chans)
     w_two_back = jnp.transpose(second_temporal, (0, 2, 1)).reshape(-1, chans)
     at_zero = side == 0
-
-    act_own, act_send, back_own, back_send, slope = front(
-        ids, latents, cotangent, w_in, w_out_back
-    )
-    act_got = lax.ppermute(act_send, "tm", swap_cores)
-    back_got = lax.ppermute(back_send, "tm", swap_cores)
-
-    size = half // CHUNKS
-    tail = REACH - slots
-    middles = []
+    w_first = jnp.where(at_zero, w_two, w_one_back)
+    w_second = jnp.where(at_zero, w_one_back, w_two)
+    w_ending = jnp.where(at_zero, w_out, w_in_back)
+    w_other = jnp.where(at_zero, w_in_back, w_out)
+
+    band = rows // CHUNKS // 2
+    got = []
     for chunk in range(CHUNKS):
-        low = chunk * size
-        pieces = [value[:, low : low + size] for value in (act_own, act_got, back_own, back_got)]
-        act_low = jnp.where(core == 0, pieces[0][slots - tail :], pieces[1][slots - tail :])
-        act_high = jnp.where(core == 0, pieces[1], pieces[0])
-        back_low = jnp.where(core == 0, pieces[2], pieces[3])
-        back_high = jnp.where(core == 0, pieces[3][:tail], pieces[2][:tail])
-        leaving = jnp.where(
-            at_zero,
-            jnp.concatenate([act_low, act_high], 0),
-            jnp.concatenate([back_low, back_high], 0),
-        )
+        start = chunk * 2 * band + (1 - core) * band - 1
+        sent = [
+            lax.dynamic_slice_in_dim(value, jnp.clip(start, 0, rows - band - 2), band + 2, 1)
+            for value in (latents, cotangent)
+        ]
+        if chunk > 0:
+            sent = [after(value, *got[0]) for value in sent]
+        got.append([lax.ppermute(value, "tm", swap_cores) for value in sent])
+    middles, slopes = [], []
+    for chunk in range(CHUNKS):
+        start = chunk * 2 * band + core * band - 1
+        kept = jnp.clip(start, 0, rows - band - 2)
+        front_ids = jnp.concatenate([ids, jnp.stack([kept, start - kept]).astype(jnp.int32)])
+        act, back, slope = front(
+            front_ids, [latents, got[chunk][0]], [cotangent, got[chunk][1]], w_in, w_out_back
+        )
+        slopes.append(slope)
+        leaving = jnp.where(at_zero, act[2 * slots - REACH :], back[:REACH])
+        if chunk > 0:
+            leaving = after(leaving, halo)
         halo = lax.ppermute(leaving, "tm", swap_sides)
-        middles.append(
-            middle(
-                chunk, ids, act_own, act_got, back_own, back_got, halo,
-                w_one, w_two_back, jnp.where(at_zero, w_two, w_one_back),
-            )
-        )
-    halos = [lax.ppermute(made[0], "tm", swap_sides) for made in middles]
-
-    first_own = [made[2] for made in middles]
-    first_got = [lax.ppermute(made[3], "tm", swap_cores) for made in middles]
-    out_first, sums_first = ending(
-        factor, ids, first_own, first_got, latents, cotangent, slope,
-        jnp.where(at_zero, w_out, w_in_back),
-    )
-
-    w_second = jnp.where(at_zero, w_one_back, w_two)
-    seconds = [second(ids, made[1], halo, w_second) for made, halo in zip(middles, halos)]
-    second_own = [made[0] for made in seconds]
-    second_got = [lax.ppermute(made[1], "tm", swap_cores) for made in seconds]
-    out_second, sums_second = ending(
-        factor, ids_for(1 - side), second_own, second_got, latents, cotangent, slope,
-        jnp.where(at_zero, w_in_back, w_out),
-    )
+        middles.append(middle(ids, act, back, slope, halo, w_one, w_two_back, w_first))
+    halos, own, got = [], [], []
+    outs = None
+    sums_first = jnp.zeros((chans, 9 * chans), F32)
+    for chunk, made in enumerate(middles):
+        halo = lax.ppermute(after(made[0], halo, sums_first), "tm", swap_sides)
+        halos.append(halo)
+        own.append(made[2])
+        leaving = made[3] if chunk == 0 else after(made[3], sums_first)
+        got.append(lax.ppermute(leaving, "tm", swap_cores))
+        *outs, sums_first = ending(
+            chunk, factor, ids, own, got, latents, cotangent, w_ending, sums_first, outs
+        )
+
+    halos[-1] = after(halos[-1], sums_first)
+    seconds = [
+        second(ids, made[1], slope, halo, w_second)
+        for made, slope, halo in zip(middles, slopes, halos)
+    ]
+    own = [made[0] for made in seconds]
+    got = [lax.ppermute(made[1], "tm", swap_cores) for made in seconds]
+    ids = ids_for(1 - side)
+    sums_second = jnp.zeros((chans, 9 * chans), F32)
+    for chunk in range(CHUNKS):
+        *outs, sums_second = ending(
+            chunk, factor, ids, own, got, latents, cotangent, w_other, sums_second, outs
+        )
+    decoded, latent_grad = outs
 
     pairs = flips(dp_size, 4)
     place = lax.axis_index("dp") * 4 + tm_index
     digits = [0] + list(range(2, len(pairs)))
-    temporal_sums = factor * jnp.concatenate(
-        [sum(made[4] for made in middles), sum(made[5] for made in middles)], 0
-    )
-    temporal_sums = halve(temporal_sums, digits + [1], pairs, place)
-    temporal_sums = double(temporal_sums, [1] + digits[::-1], pairs, place)
-    early = halve(sums_first, digits, pairs, place)
+    span = 9 * chans
+    early = jnp.concatenate(
+        [
+            sums_first,
+            factor * sum(made[4] for made in middles),
+            factor * sum(made[5] for made in middles),
+        ],
+        1,
+    )
+    early = after(early, halos[-2])
+    early = halve(early, digits, pairs, place)
     late = halve(sums_second, digits, pairs, place)
-    both = jnp.stack([early, late])
+    both = jnp.concatenate([early, late], 1)
     other = lax.ppermute(both, ("dp", "tm"), pairs[1])
-    spatial_sums = jnp.where(
-        at_zero,
-        jnp.stack([early + other[1], late + other[0]]),
-        jnp.stack([late + other[0], early + other[1]]),
-    )
-    spatial_sums = double(spatial_sums, digits[::-1], pairs, place, 1)
-
-    decoded = jnp.where(at_zero, out_first, out_second)
-    latent_grad = jnp.where(at_zero, out_second, out_first)
+    swapped = jnp.concatenate([other[:, -span:], other[:, span:-span], other[:, :span]], 1)
+    both = both + swapped
+    both = jnp.where(
+        at_zero, both, jnp.concatenate([both[:, -span:], both[:, span:-span], both[:, :span]], 1)
+    )
+    both = double(both, digits[::-1], pairs, place)
+    spatial_sums = (both[:, :span], both[:, -span:])
+    temporal_sums = both[:, span:-span]
+
     last_grad = jnp.transpose(spatial_sums[0].reshape(chans, 3, 3, chans), (1, 2, 3, 0))
     first_grad = jnp.transpose(spatial_sums[1].reshape(chans, 3, 3, chans), (1, 2, 0, 3))
     first_grad = first_grad[::-1, ::-1]
-    near_grad = jnp.transpose(temporal_sums[:chans].reshape(chans, TAPS, chans), (1, 2, 0))
-    far_grad = jnp.transpose(temporal_sums[chans:].reshape(chans, TAPS, chans), (1, 0, 2))
+    near_grad = jnp.transpose(temporal_sums[:, : TAPS * chans].reshape(chans, TAPS, chans), (1, 2, 0))
+    far_grad = jnp.transpose(temporal_sums[:, TAPS * chans :].reshape(chans, TAPS, chans), (1, 0, 2))
     return (decoded[None], latent_grad[None], first_grad, last_grad, near_grad, far_grad)
 
 
 def on_any_device(dp_size, tm_size, latents, cotangent, *rest):
     clips, slots, rows = latents.shape[:3]
-    fits = clips == 1 and tm_size == 4 and slots <= REACH <= 2 * slots and rows % 8 == 0
+    fits = clips == 1 and tm_size == 4 and slots <= REACH <= 2 * slots and rows % 8 == 0 and slots % 2 == 0
     if fits and dp_size & (dp_size - 1) == 0:
         return on_chip_pair(dp_size, latents, cotangent, *rest)
     return on_device(latents, cotangent, *rest)

time: 247 us -> 215 us (0.87)
  waiting for transfers between devices: 87.1 us -> 50.1 us
  Pallas kernels: 88.7 us -> 102 us
  starting transfers between devices: 32.3 us -> 22.6 us
  local copies, waits for them, and re-layouts: 14.9 us -> 23.8 us
  other arithmetic: 21.2 us -> 13.5 us
    ppermute x8 -> x10, waiting for transfers between devices: 22.8 us -> 3.32 us  [the longest x2 2.97 us: on_chip_pair(): halo = lax.ppermute(after(made[0], halo, sums_first), 'tm', swap_sides)]
    ppermute x2, waiting for transfers between devices: 31.6 us -> 13.9 us  [on_chip_pair(): halo = lax.ppermute(leaving, 'tm', swap_sides)]
    ppermute x13 -> x8, waiting for transfers between devices: 17.7 us -> 9.08 us  [halve(): values = keep + lax.ppermute(send, ('dp', 'tm'), pairs[digit])]
    pallas_call x1 -> x2, Pallas kernels: 16.9 us -> 24.9 us  [front(): pl.pallas_call(front_kernel, grid_spec=pltpu.PrefetchScalarGridSpec(num_s...]
    ppermute x9 -> x4, waiting for transfers between devices: 12 us -> 19.8 us  [double(): other = lax.ppermute(values, ('dp', 'tm'), pairs[digit])]
    ppermute x13 -> x8, starting transfers between devices: 17.9 us -> 10.5 us  [halve(): values = keep + lax.ppermute(send, ('dp', 'tm'), pairs[digit])]
    pallas_call x2 -> x4, Pallas kernels: 36.4 us -> 41.6 us  [ending(): pl.pallas_call(functools.partial(ending_kernel, chunk, rows, factor, outs...]
    ppermute x9 -> x4, starting transfers between devices: 8.04 us -> 2.87 us  [double(): other = lax.ppermute(values, ('dp', 'tm'), pairs[digit])]
  transfers between devices with their start and end apart: 33 -> 25, of which waited for: 18 -> 14; matrix products, arithmetic and copies ran while one was open for 6% -> 11% of each run, Pallas kernels for 24% -> 48%
where the time goes in v2:
time: 215 us; the launch traced here: 214 us
  Pallas kernels  102 us (47%)
  waiting for transfers between devices  50.1 us (23%)
  local copies, waits for them, and re-layouts  23.8 us (11%)
  starting transfers between devices  22.6 us (11%)
  other arithmetic  13.5 us (6%)
    pallas_call x4, Pallas kernels, ending(): pl.pallas_call(functools.partial(ending_kernel, chunk, rows, factor, outs...  41.6 us
    pallas_call x2, Pallas kernels, front(): pl.pallas_call(front_kernel, grid_spec=pltpu.PrefetchScalarGridSpec(num_s...  24.9 us
    pallas_call x2, Pallas kernels, middle(): pl.pallas_call(middle_kernel, grid_spec=pltpu.PrefetchScalarGridSpec(num_...  23.6 us
    ppermute x4, waiting for transfers between devices, double(): other = lax.ppermute(values, ('dp', 'tm'), pairs[digit])  19.8 us
    ppermute x2, waiting for transfers between devices, on_chip_pair(): halo = lax.ppermute(leaving, 'tm', swap_sides)  13.9 us
    pallas_call x2, Pallas kernels, second(): pl.pallas_call(second_kernel, grid_spec=pltpu.PrefetchScalarGridSpec(num_...  12.2 us
    ppermute x8, starting transfers between devices, halve(): values = keep + lax.ppermute(send, ('dp', 'tm'), pairs[digit])  10.5 us
    ppermute x8, waiting for transfers between devices, halve(): values = keep + lax.ppermute(send, ('dp', 'tm'), pairs[digit])  9.08 us
  transfers between devices with their start and end apart: 25, of which 14 were waited for; matrix products, arithmetic and copies ran while one was open for 11% of the time, Pallas kernels for 48%

profile of v2, /device:TPU:0, one launch (start us, length us, event | category | flops | bytes accessed | tf_op | source)
XLA Modules:
  0.0 214.0 jit_solution(1713560925274256273)
XLA Ops:
  0.7 3.0 %dynamic-slice_bitcast_fusion.1 = (bf16[6,6,128,128]{3,2,1,0:T(8,128)(2,1)}, bf16[6,6,128,128]{3,2,1,0:T(8,128)(2,1)S(1)}) fusion(bf16[1,6,16,128,128]{4,3,2,1,0:T(8,128)(2,1)} %param.8, s32[]{:T(128)S(6)} %min.18, s32[]{:T(128)S(6)} %min.16), kind=kLoop, calls=%fused_computation.12 | loop fusion | bytes 4718600 | tf_op jit(solution)/shard_map/dynamic_slice | solution.py:750
  4.2 1.2 dynamic-slice_bitcast_fusion
  6.2 1.8 copy.28
  8.8 2.6 %fusion.8 = (bf16[1536,256]{1,0:T(8,128)(2,1)}, bf16[1536,256]{1,0:T(8,128)(2,1)}) fusion(bf16[1152,128]{1,0:T(8,128)(2,1)} %bitcast.85, bf16[1152,128]{1,0:T(8,128)(2,1)} %bitcast.86), kind=kLoop, calls=%fused_computation.18 | loop fusion | flops 5505024 | bytes 2162688 | tf_op jit(solution)/shard_map/concatenate | solution.py:659
  12.7 12.6 %front.2 = (bf16[2,6,4,128,128]{4,3,2,1,0:T(8,128)(2,1)}, bf16[2,6,4,128,128]{4,3,2,1,0:T(8,128)(2,1)}, bf16[2,6,4,128,128]{4,3,2,1,0:T(8,128)(2,1)}) custom-call(s32[8]{0:T(128)} %concatenate.56.ids, bf16[6,16,128,128]{3,2,1,0:T(8,128)(2,1)} %bitcast.56, bf16[6,6,128,128]{3,2,1,0:T(8,128)(2,1)} %collective-permute-done.refs_1_, ...), custom_call_target="tpu_custom_call" | custom-call | flops 1100000000 | bytes 1000 | tf_op jit(solution)/shard_map/front/pallas_call | solution.py:312
  25.3 1.7 slice_select_fusion.1
  26.9 2.9 %collective-permute-start.2 = (bf16[8,4,128,128]{3,2,1,0:T(8,128)(2,1)S(1)}, bf16[8,4,128,128]{3,2,1,0:T(8,128)(2,1)}, u32[]{:S(2)}, u32[]{:S(2)}) collective-permute-start(bf16[8,4,128,128]{3,2,1,0:T(8,128)(2,1)S(1)} %slice_select_fusion.1), channel_id=1, source_target_pairs={{0,2},{2,0},{1,3},{3,1},{4,6},{6,4},{5,7},{7,5},{8,10},{10,8},{9,1... | collective-permute-start | bytes 3145736 | tf_op jit(solution)/shard_map/ppermute | solution.py:768
  30.5 1.0 copy-done.3
  31.5 1.1 copy-done.4
  32.6 12.3 %front.3 = (bf16[2,6,4,128,128]{4,3,2,1,0:T(8,128)(2,1)}, bf16[2,6,4,128,128]{4,3,2,1,0:T(8,128)(2,1)}, bf16[2,6,4,128,128]{4,3,2,1,0:T(8,128)(2,1)}) custom-call(s32[8]{0:T(128)} %concatenate.59.ids, bf16[6,16,128,128]{3,2,1,0:T(8,128)(2,1)} %bitcast.57, bf16[6,6,128,128]{3,2,1,0:T(8,128)(2,1)} %copy-done.3, bf16[6,16,128,128]{3,2,1,0:T(8,128)(2,1)} %bitcast.63, ...), custom_call_target="tpu_custom_call" | custom-call | flops 1100000000 | bytes 1000 | tf_op jit(solution)/shard_map/front/pallas_call | solution.py:312
  44.8 2.7 %slice_select_fusion = bf16[8,4,128,128]{3,2,1,0:T(8,128)(2,1)} fusion(bf16[12,4,128,128]{3,2,1,0:T(8,128)(2,1)} %bitcast.76, bf16[12,4,128,128]{3,2,1,0:T(8,128)(2,1)} %bitcast.74, pred[]{:T(512)S(6)} %eq.17), kind=kLoop, calls=%fused_computation.15 | loop fusion | flops 524288 | bytes 3145729 | tf_op jit(solution)/shard_map/jit(_where)/select_n | solution.py:765
  47.5 5.5 %collective-permute-done.2.halo = bf16[8,4,128,128]{3,2,1,0:T(8,128)(2,1)} collective-permute-done((bf16[8,4,128,128]{3,2,1,0:T(8,128)(2,1)S(1)}, bf16[8,4,128,128]{3,2,1,0:T(8,128)(2,1)}, u32[]{:S(2)}, u32[]{:S(2)}) %collective-permute-start.2) | collective-permute-done | bytes 1048608 | tf_op jit(solution)/shard_map/ppermute | solution.py:768
  53.1 1.7 collective-permute-start.5
  57.0 11.8 %middle.2 = (bf16[8,4,128,128]{3,2,1,0:T(8,128)(2,1)}, bf16[12,4,128,128]{3,2,1,0:T(8,128)(2,1)}, bf16[6,4,128,128]{3,2,1,0:T(8,128)(2,1)}, bf16[6,4,128,128]{3,...) custom-call(s32[6]{0:T(128)} %stack.39.ids, bf16[12,4,128,128]{3,2,1,0:T(8,128)(2,1)} %bitcast.79, ...), custom_call_target="tpu_custom_call" | custom-call | flops 1200000000 | bytes 1000 | tf_op jit(solution)/shard_map/middle/pallas_call | solution.py:430
  69.2 8.4 %collective-permute-done.5.halo = bf16[8,4,128,128]{3,2,1,0:T(8,128)(2,1)S(1)} collective-permute-done((bf16[8,4,128,128]{3,2,1,0:T(8,128)(2,1)}, bf16[8,4,128,128]{3,2,1,0:T(8,128)(2,1)S(1)}, u32[]{:S(2)}, u32[]{:S(2)}) %collective-permute-start.5) | collective-permute-done | bytes 1048608 | tf_op jit(solution)/shard_map/ppermute | solution.py:768
  77.5 1.4 collective-permute-start.6
  79.0 1.4 broadcast_select_fusion
  81.5 8.5 %ending.4 = (bf16[6,16,128,128]{3,2,1,0:T(8,128)(2,1)}, bf16[6,16,128,128]{3,2,1,0:T(8,128)(2,1)}, f32[128,1152]{1,0:T(8,128)}) custom-call(s32[6]{0:T(128)} %stack.39.ids, bf16[6,4,128,128]{3,2,1,0:T(8,128)(2,1)} %get-tuple-element.63.refs_0_, bf16[6,4,128,128]{3,2,1,0:T(8,128)(2,1)} %copy-done.2, bf16[6,16,128,128]{3,2,1,0:T(8,128)(2,1)} %bitcast.58, ...), custom_call_target="tpu_custom_call" | custom-call | flops 1300000000 | bytes 1000 | tf_op jit(solution)/shard_map/ending/pallas_call | solution.py:627
  90.0 11.8 %middle.3 = (bf16[8,4,128,128]{3,2,1,0:T(8,128)(2,1)}, bf16[12,4,128,128]{3,2,1,0:T(8,128)(2,1)}, bf16[6,4,128,128]{3,2,1,0:T(8,128)(2,1)}, bf16[6,4,128,128]{3,...) custom-call(s32[6]{0:T(128)} %stack.39.ids, bf16[12,4,128,128]{3,2,1,0:T(8,128)(2,1)} %bitcast.75, ...), custom_call_target="tpu_custom_call" | custom-call | flops 1200000000 | bytes 1000 | tf_op jit(solution)/shard_map/middle/pallas_call | solution.py:430
  102.0 1.0 add_multiply_fusion
  103.9 1.0 copy-done.10
  104.9 1.0 collective-permute-start.8
  106.8 12.4 %ending.5 = (bf16[6,16,128,128]{3,2,1,0:T(8,128)(2,1)}, bf16[6,16,128,128]{3,2,1,0:T(8,128)(2,1)}, f32[128,1152]{1,0:T(8,128)}) custom-call(s32[6]{0:T(128)} %stack.39.ids, bf16[6,4,128,128]{3,2,1,0:T(8,128)(2,1)} %get-tuple-element.63.refs_0_, bf16[6,4,128,128]{3,2,1,0:T(8,128)(2,1)} %get-tuple-element.67.refs_1_, ...), custom_call_target="tpu_custom_call", output_to_operand_aliasing={{0}: (9, {}), {1}: (10, {})} | custom-call | flops 1300000000 | bytes 1000 | tf_op jit(solution)/shard_map/ending/pallas_call | solution.py:627
  119.2 1.1 pad_maximum_fusion
  120.7 6.1 %second.2 = (bf16[6,4,128,128]{3,2,1,0:T(8,128)(2,1)}, bf16[6,4,128,128]{3,2,1,0:T(8,128)(2,1)}) custom-call(s32[6]{0:T(128)} %stack.39.ids, bf16[12,4,128,128]{3,2,1,0:T(8,128)(2,1)} %get-tuple-element.51.mid, bf16[12,4,128,128]{3,2,1,0:T(8,128)(2,1)} %bitcast.73, bf16[8,4,128,128]{3,2,1,0:T(8,128)(2,1)} %copy-done.10, bf16[384,128]{1,0:T(8,128)(2,1)} %bitcast.91), custom_call_target="tpu_custom_call" | custom-call | flops 500000000 | bytes 1000 | tf_op jit(solution)/shard_map/second/pallas_call | solution.py:500
  127.7 3.0 %collective-permute-done.8.halo = bf16[8,4,128,128]{3,2,1,0:T(8,128)(2,1)S(1)} collective-permute-done((bf16[8,4,128,128]{3,2,1,0:T(8,128)(2,1)}, bf16[8,4,128,128]{3,2,1,0:T(8,128)(2,1)S(1)}, u32[]{:S(2)}, u32[]{:S(2)}) %collective-permute-start.8) | collective-permute-done | bytes 1048608 | tf_op jit(solution)/shard_map/ppermute | solution.py:774
  130.6 1.0 copy-done.9
  131.7 6.1 %second.3 = (bf16[6,4,128,128]{3,2,1,0:T(8,128)(2,1)}, bf16[6,4,128,128]{3,2,1,0:T(8,128)(2,1)}) custom-call(s32[6]{0:T(128)} %stack.39.ids, bf16[12,4,128,128]{3,2,1,0:T(8,128)(2,1)} %get-tuple-element.61.mid, bf16[12,4,128,128]{3,2,1,0:T(8,128)(2,1)} %bitcast.71, bf16[8,4,128,128]{3,2,1,0:T(8,128)(2,1)} %copy-done.9, bf16[384,128]{1,0:T(8,128)(2,1)} %bitcast.92), custom_call_target="tpu_custom_call" | custom-call | flops 500000000 | bytes 1000 | tf_op jit(solution)/shard_map/second/pallas_call | solution.py:500
  137.8 1.1 dynamic-slice_add_fusion
  138.9 1.6 collective-permute-start.13
  141.4 8.5 %ending.6 = (bf16[6,16,128,128]{3,2,1,0:T(8,128)(2,1)}, bf16[6,16,128,128]{3,2,1,0:T(8,128)(2,1)}, f32[128,1152]{1,0:T(8,128)}) custom-call(s32[6]{0:T(128)} %stack.38.ids, bf16[6,4,128,128]{3,2,1,0:T(8,128)(2,1)} %get-tuple-element.59.refs_0_, bf16[6,4,128,128]{3,2,1,0:T(8,128)(2,1)} %copy-done.1, ...), custom_call_target="tpu_custom_call", output_to_operand_aliasing={{0}: (7, {}), {1}: (8, {})} | custom-call | flops 1300000000 | bytes 1000 | tf_op jit(solution)/shard_map/ending/pallas_call | solution.py:627
  150.8 12.2 %ending.7 = (bf16[6,16,128,128]{3,2,1,0:T(8,128)(2,1)}, bf16[6,16,128,128]{3,2,1,0:T(8,128)(2,1)}, f32[128,1152]{1,0:T(8,128)}) custom-call(s32[6]{0:T(128)} %stack.38.ids, bf16[6,4,128,128]{3,2,1,0:T(8,128)(2,1)} %get-tuple-element.59.refs_0_, bf16[6,4,128,128]{3,2,1,0:T(8,128)(2,1)} %get-tuple-element.74.refs_1_, ...), custom_call_target="tpu_custom_call", output_to_operand_aliasing={{0}: (9, {}), {1}: (10, {})} | custom-call | flops 1300000000 | bytes 1000 | tf_op jit(solution)/shard_map/ending/pallas_call | solution.py:627
  163.0 1.0 constant_dynamic-slice_fusion.3
  164.4 1.7 collective-permute-start.14
  166.7 3.3 %collective-permute-done.14 = f32[16,1920]{1,0:T(8,128)S(1)} collective-permute-done((f32[16,1920]{1,0:T(8,128)S(1)}, f32[16,1920]{1,0:T(8,128)S(1)}, u32[]{:S(2)}, u32[]{:S(2)}) %collective-permute-start.14) | collective-permute-done | bytes 122912 | tf_op jit(solution)/shard_map/ppermute | solution.py:688
  170.0 1.9 collective-permute-done.17
  172.0 1.5 collective-permute-start.18
  173.5 2.6 %collective-permute-start.15 = (f32[8,1920]{1,0:T(8,128)S(1)}, f32[8,1920]{1,0:T(8,128)S(1)}, u32[]{:S(2)}, u32[]{:S(2)}) collective-permute-start(f32[8,1920]{1,0:T(8,128)S(1)} %constant_dynamic-slice_fusion.4), channel_id=1, source_target_pairs={{0,16},{1,17},{2,18},{3,19},{4,20},{5,21},{6,22},{7,23},{8,24},{9,... | collective-permute-start | bytes 184328 | tf_op jit(solution)/shard_map/ppermute | solution.py:688
  177.1 2.0 collective-permute-start.19
  179.9 2.1 %collective-permute-done.19 = f32[8,1152]{1,0:T(8,128)S(1)} collective-permute-done((f32[8,1152]{1,0:T(8,128)S(1)}, f32[8,1152]{1,0:T(8,128)S(1)}, u32[]{:S(2)}, u32[]{:S(2)}) %collective-permute-start.19) | collective-permute-done | bytes 36896 | tf_op jit(solution)/shard_map/ppermute | solution.py:688
  182.8 4.0 %collective-permute-done.20 = f32[8,3072]{1,0:T(8,128)S(1)} collective-permute-done((f32[8,3072]{1,0:T(8,128)S(1)}, f32[8,3072]{1,0:T(8,128)S(1)}, u32[]{:S(2)}, u32[]{:S(2)}) %collective-permute-start.20) | collective-permute-done | bytes 98336 | tf_op jit(solution)/shard_map/ppermute | solution.py:814
  186.8 2.1 collective-permute-start.21
  188.9 4.7 %collective-permute-done.21 = f32[8,3072]{1,0:T(8,128)S(1)} collective-permute-done((f32[8,3072]{1,0:T(8,128)S(1)}, f32[8,3072]{1,0:T(8,128)S(1)}, u32[]{:S(2)}, u32[]{:S(2)}) %collective-permute-start.21) | collective-permute-done | bytes 98336 | tf_op jit(solution)/shard_map/ppermute | solution.py:695
  193.8 5.5 %collective-permute-done.22 = f32[16,3072]{1,0:T(8,128)S(1)} collective-permute-done((f32[16,3072]{1,0:T(8,128)S(1)}, f32[16,3072]{1,0:T(8,128)S(1)}, u32[]{:S(2)}, u32[]{:S(2)}) %collective-permute-start.22) | collective-permute-done | bytes 196640 | tf_op jit(solution)/shard_map/ppermute | solution.py:695
  199.9 7.3 %collective-permute-done.23 = f32[32,3072]{1,0:T(8,128)S(1)} collective-permute-done((f32[32,3072]{1,0:T(8,128)S(1)}, f32[32,3072]{1,0:T(8,128)S(1)}, u32[]{:S(2)}, u32[]{:S(2)}) %collective-permute-start.23) | collective-permute-done | bytes 393248 | tf_op jit(solution)/shard_map/ppermute | solution.py:695
  207.3 2.3 %collective-permute-done.24 = f32[64,3072]{1,0:T(8,128)S(1)} collective-permute-done((f32[64,3072]{1,0:T(8,128)S(1)}, f32[64,3072]{1,0:T(8,128)S(1)}, u32[]{:S(2)}, u32[]{:S(2)}) %collective-permute-start.24) | collective-permute-done | bytes 786464 | tf_op jit(solution)/shard_map/ppermute | solution.py:695
  209.8 1.1 copy.33
  212.9 1.1 copy.36
  (109 shorter events, 18.7 us)
Async XLA Ops:
  0.7 3.5 %copy-start = (bf16[1,6,16,128,128]{4,3,2,1,0:T(8,128)(2,1)S(1)}, bf16[1,6,16,128,128]{4,3,2,1,0:T(8,128)(2,1)}, u32[]{:S(2)}) copy-start(bf16[1,6,16,128,128]{4,3,2,1,0:T(8,128)(2,1)} %param.9) | copy-start | bytes 9437188
  3.7 1.7 copy-start.6
  3.7 4.3 %collective-permute-start = (bf16[6,6,128,128]{3,2,1,0:T(8,128)(2,1)S(1)}, bf16[6,6,128,128]{3,2,1,0:T(8,128)(2,1)}, u32[]{:S(2)}, u32[]{:S(2)}) collective-permute-start(bf16[6,6,128,128]{3,2,1,0:T(8,128)(2,1)S(1)} %get-tuple-element.99), channel_id=1, source_target_pairs={{0,1},{1,0},{2,3},{3,2},{4,5},{5,4},{6,7},{7,6},{8,9},{9,8},{10,11... | collective-permute-start | bytes 3538952 | tf_op jit(solution)/shard_map/ppermute | solution.py:755
  5.4 6.7 %copy-start.19 = (s32[2]{0:T(128)S(1)}, s32[2]{0:T(128)}, u32[]{:S(2)}) copy-start(s32[2]{0:T(128)} %param.15) | copy-start | bytes 28
  5.4 3.0 %collective-permute-start.1 = (bf16[6,6,128,128]{3,2,1,0:T(8,128)(2,1)S(1)}, bf16[6,6,128,128]{3,2,1,0:T(8,128)(2,1)S(1)}, u32[]{:S(2)}, u32[]{:S(2)}) collective-permute-start(bf16[6,6,128,128]{3,2,1,0:T(8,128)(2,1)S(1)} %get-tuple-element.97), channel_id=1, source_target_pairs={{0,1},{1,0},{2,3},{3,2},{4,5},{5,4},{6,7},{7,6},{8,9},{9,8},{10,11... | collective-permute-start | bytes 3538952 | tf_op jit(solution)/shard_map/ppermute | solution.py:755
  8.3 4.3 %copy-start.5 = (bf16[6,6,128,128]{3,2,1,0:T(8,128)(2,1)}, bf16[6,6,128,128]{3,2,1,0:T(8,128)(2,1)S(1)}, u32[]{:S(2)}) copy-start(bf16[6,6,128,128]{3,2,1,0:T(8,128)(2,1)S(1)} %collective-permute-done.1.refs_3_) | copy-start | bytes 3538948
  8.3 22.1 %collective-permute-start.3 = (bf16[6,6,128,128]{3,2,1,0:T(8,128)(2,1)}, bf16[6,6,128,128]{3,2,1,0:T(8,128)(2,1)S(1)}, u32[]{:S(2)}, u32[]{:S(2)}) collective-permute-start(bf16[6,6,128,128]{3,2,1,0:T(8,128)(2,1)} %get-tuple-element.53), channel_id=1, source_target_pairs={{0,1},{1,0},{2,3},{3,2},{4,5},{5,4},{6,7},{7,6},{8,9},{9,8},{10,11... | collective-permute-start | bytes 3538952 | tf_op jit(solution)/shard_map/ppermute | solution.py:755
  8.7 21.8 %collective-permute-start.4 = (bf16[6,6,128,128]{3,2,1,0:T(8,128)(2,1)}, bf16[6,6,128,128]{3,2,1,0:T(8,128)(2,1)S(1)}, u32[]{:S(2)}, u32[]{:S(2)}) collective-permute-start(bf16[6,6,128,128]{3,2,1,0:T(8,128)(2,1)} %get-tuple-element.54), channel_id=1, source_target_pairs={{0,1},{1,0},{2,3},{3,2},{4,5},{5,4},{6,7},{7,6},{8,9},{9,8},{10,11... | collective-permute-start | bytes 3538952 | tf_op jit(solution)/shard_map/ppermute | solution.py:755
  26.9 26.1 %collective-permute-start.2 = (bf16[8,4,128,128]{3,2,1,0:T(8,128)(2,1)S(1)}, bf16[8,4,128,128]{3,2,1,0:T(8,128)(2,1)}, u32[]{:S(2)}, u32[]{:S(2)}) collective-permute-start(bf16[8,4,128,128]{3,2,1,0:T(8,128)(2,1)S(1)} %slice_select_fusion.1), channel_id=1, source_target_pairs={{0,2},{2,0},{1,3},{3,1},{4,6},{6,4},{5,7},{7,5},{8,10},{10,8},{9,1... | collective-permute-start | bytes 3145736 | tf_op jit(solution)/shard_map/ppermute | solution.py:768
  30.5 1.0 copy-start.3
  31.5 1.1 copy-start.4
  44.8 10.6 %copy-start.16 = (bf16[3,128,128]{2,1,0:T(8,128)(2,1)S(1)}, bf16[3,128,128]{2,1,0:T(8,128)(2,1)}, u32[]{:S(2)}) copy-start(bf16[3,128,128]{2,1,0:T(8,128)(2,1)} %param.13) | copy-start | bytes 294916
  44.8 11.4 %copy-start.12 = (bf16[3,128,128]{2,1,0:T(8,128)(2,1)S(1)}, bf16[3,128,128]{2,1,0:T(8,128)(2,1)}, u32[]{:S(2)}) copy-start(bf16[3,128,128]{2,1,0:T(8,128)(2,1)} %param.12) | copy-start | bytes 294916
  53.1 24.5 %collective-permute-start.5 = (bf16[8,4,128,128]{3,2,1,0:T(8,128)(2,1)}, bf16[8,4,128,128]{3,2,1,0:T(8,128)(2,1)S(1)}, u32[]{:S(2)}, u32[]{:S(2)}) collective-permute-start(bf16[8,4,128,128]{3,2,1,0:T(8,128)(2,1)} %slice_select_fusion), channel_id=1, source_target_pairs={{0,2},{2,0},{1,3},{3,1},{4,6},{6,4},{5,7},{7,5},{8,10},{10,8},{9,1... | collective-permute-start | bytes 3145736 | tf_op jit(solution)/shard_map/ppermute | solution.py:768
  57.0 11.9 %copy-start.8 = (bf16[3,3,128,128]{3,2,1,0:T(8,128)(2,1)S(1)}, bf16[3,3,128,128]{3,2,1,0:T(8,128)(2,1)}, u32[]{:S(2)}) copy-start(bf16[3,3,128,128]{3,2,1,0:T(8,128)(2,1)} %param.10) | copy-start | bytes 884740
  57.0 21.9 %copy-start.7 = (bf16[3,3,128,128]{3,2,1,0:T(8,128)(2,1)S(1)}, bf16[3,3,128,128]{3,2,1,0:T(8,128)(2,1)}, u32[]{:S(2)}) copy-start(bf16[3,3,128,128]{3,2,1,0:T(8,128)(2,1)} %param.11) | copy-start | bytes 884740
  68.8 11.6 %collective-permute-start.7 = (bf16[6,4,128,128]{3,2,1,0:T(8,128)(2,1)}, bf16[6,4,128,128]{3,2,1,0:T(8,128)(2,1)S(1)}, u32[]{:S(2)}, u32[]{:S(2)}) collective-permute-start(bf16[6,4,128,128]{3,2,1,0:T(8,128)(2,1)} %get-tuple-element.64), channel_id=1, source_target_pairs={{0,1},{1,0},{2,3},{3,2},{4,5},{5,4},{6,7},{7,6},{8,9},{9,8},{10,11... | collective-permute-start | bytes 2359304 | tf_op jit(solution)/shard_map/ppermute | solution.py:778
  77.5 12.5 %copy-start.11 = (bf16[8,4,128,128]{3,2,1,0:T(8,128)(2,1)}, bf16[8,4,128,128]{3,2,1,0:T(8,128)(2,1)S(1)}, u32[]{:S(2)}) copy-start(bf16[8,4,128,128]{3,2,1,0:T(8,128)(2,1)S(1)} %collective-permute-done.5.halo) | copy-start | bytes 3145732
  77.5 26.4 %collective-permute-start.6 = (bf16[8,4,128,128]{3,2,1,0:T(8,128)(2,1)}, bf16[8,4,128,128]{3,2,1,0:T(8,128)(2,1)S(1)}, u32[]{:S(2)}, u32[]{:S(2)}) collective-permute-start(bf16[8,4,128,128]{3,2,1,0:T(8,128)(2,1)} %get-tuple-element.58), channel_id=1, source_target_pairs={{0,2},{2,0},{1,3},{3,1},{4,6},{6,4},{5,7},{7,5},{8,10},{10,8},{9,1... | collective-permute-start | bytes 3145736 | tf_op jit(solution)/shard_map/ppermute | solution.py:774
  80.4 1.1 copy-start.2
  90.0 11.9 %copy-start.18 = (f32[128,384]{1,0:T(8,128)S(1)}, f32[128,384]{1,0:T(8,128)}, u32[]{:S(2)}) copy-start(f32[128,384]{1,0:T(8,128)} %get-tuple-element.86) | copy-start | bytes 589828
  90.0 12.9 %copy-start.17 = (f32[128,384]{1,0:T(8,128)S(1)}, f32[128,384]{1,0:T(8,128)}, u32[]{:S(2)}) copy-start(f32[128,384]{1,0:T(8,128)} %get-tuple-element.84) | copy-start | bytes 589828
  101.9 4.0 %collective-permute-start.9 = (bf16[6,4,128,128]{3,2,1,0:T(8,128)(2,1)}, bf16[6,4,128,128]{3,2,1,0:T(8,128)(2,1)S(1)}, u32[]{:S(2)}, u32[]{:S(2)}) collective-permute-start(bf16[6,4,128,128]{3,2,1,0:T(8,128)(2,1)} %get-tuple-element.69), channel_id=1, source_target_pairs={{0,1},{1,0},{2,3},{3,2},{4,5},{5,4},{6,7},{7,6},{8,9},{9,8},{10,11... | collective-permute-start | bytes 2359304 | tf_op jit(solution)/shard_map/ppermute | solution.py:778
  103.9 1.0 copy-start.10
  104.9 25.8 %collective-permute-start.8 = (bf16[8,4,128,128]{3,2,1,0:T(8,128)(2,1)}, bf16[8,4,128,128]{3,2,1,0:T(8,128)(2,1)S(1)}, u32[]{:S(2)}, u32[]{:S(2)}) collective-permute-start(bf16[8,4,128,128]{3,2,1,0:T(8,128)(2,1)} %get-tuple-element.66), channel_id=1, source_target_pairs={{0,2},{2,0},{1,3},{3,1},{4,6},{6,4},{5,7},{7,5},{8,10},{10,8},{9,1... | collective-permute-start | bytes 3145736 | tf_op jit(solution)/shard_map/ppermute | solution.py:774
  105.9 0.9 copy-start.13
  120.4 17.4 %collective-permute-start.12 = (f32[64,1920]{1,0:T(8,128)S(1)}, f32[64,1920]{1,0:T(8,128)}, u32[]{:S(2)}, u32[]{:S(2)}) collective-permute-start(f32[64,1920]{1,0:T(8,128)S(1)} %constant_dynamic-slice_fusion.7), channel_id=1, source_target_pairs={{0,1},{1,0},{2,3},{3,2},{4,5},{5,4},{6,7},{7,6},{8,9},{9,8},{10,11... | collective-permute-start | bytes 1474568 | tf_op jit(solution)/shard_map/ppermute | solution.py:688
  126.7 13.7 %collective-permute-start.10 = (bf16[6,4,128,128]{3,2,1,0:T(8,128)(2,1)}, bf16[6,4,128,128]{3,2,1,0:T(8,128)(2,1)S(1)}, u32[]{:S(2)}, u32[]{:S(2)}) collective-permute-start(bf16[6,4,128,128]{3,2,1,0:T(8,128)(2,1)} %get-tuple-element.75), channel_id=1, source_target_pairs={{0,1},{1,0},{2,3},{3,2},{4,5},{5,4},{6,7},{7,6},{8,9},{9,8},{10,11... | collective-permute-start | bytes 2359304 | tf_op jit(solution)/shard_map/ppermute | solution.py:789
  130.6 1.0 copy-start.9
  137.8 12.1 %collective-permute-start.11 = (bf16[6,4,128,128]{3,2,1,0:T(8,128)(2,1)}, bf16[6,4,128,128]{3,2,1,0:T(8,128)(2,1)S(1)}, u32[]{:S(2)}, u32[]{:S(2)}) collective-permute-start(bf16[6,4,128,128]{3,2,1,0:T(8,128)(2,1)} %get-tuple-element.76), channel_id=1, source_target_pairs={{0,1},{1,0},{2,3},{3,2},{4,5},{5,4},{6,7},{7,6},{8,9},{9,8},{10,11... | collective-permute-start | bytes 2359304 | tf_op jit(solution)/shard_map/ppermute | solution.py:789
  138.9 25.5 %collective-permute-start.13 = (f32[32,1920]{1,0:T(8,128)S(1)}, f32[32,1920]{1,0:T(8,128)S(1)}, u32[]{:S(2)}, u32[]{:S(2)}) collective-permute-start(f32[32,1920]{1,0:T(8,128)S(1)} %constant_dynamic-slice_fusion.6), channel_id=1, source_target_pairs={{0,4},{1,5},{2,6},{3,7},{4,0},{5,1},{6,2},{7,3},{8,12},{9,13},{10,... | collective-permute-start | bytes 737288 | tf_op jit(solution)/shard_map/ppermute | solution.py:688
  140.5 0.9 copy-start.1
  149.9 0.9 copy-start.14
  163.0 3.1 %copy-start.15 = (f32[128,1152]{1,0:T(8,128)S(1)}, f32[128,1152]{1,0:T(8,128)}, u32[]{:S(2)}) copy-start(f32[128,1152]{1,0:T(8,128)} %get-tuple-element.89) | copy-start | bytes 1769476
  164.1 2.0 collective-permute-start.16
  164.4 5.6 %collective-permute-start.14 = (f32[16,1920]{1,0:T(8,128)S(1)}, f32[16,1920]{1,0:T(8,128)S(1)}, u32[]{:S(2)}, u32[]{:S(2)}) collective-permute-start(f32[16,1920]{1,0:T(8,128)S(1)} %constant_dynamic-slice_fusion.5), channel_id=1, source_target_pairs={{0,8},{1,9},{2,10},{3,11},{4,12},{5,13},{6,14},{7,15},{8,0},{9,1},... | collective-permute-start | bytes 368648 | tf_op jit(solution)/shard_map/ppermute | solution.py:688
  166.1 5.8 %collective-permute-start.17 = (f32[32,1152]{1,0:T(8,128)S(1)}, f32[32,1152]{1,0:T(8,128)S(1)}, u32[]{:S(2)}, u32[]{:S(2)}) collective-permute-start(f32[32,1152]{1,0:T(8,128)S(1)} %constant_dynamic-slice_fusion.2), channel_id=1, source_target_pairs={{0,4},{1,5},{2,6},{3,7},{4,0},{5,1},{6,2},{7,3},{8,12},{9,13},{10,... | collective-permute-start | bytes 442376 | tf_op jit(solution)/shard_map/ppermute | solution.py:688
  172.0 5.0 %collective-permute-start.18 = (f32[16,1152]{1,0:T(8,128)S(1)}, f32[16,1152]{1,0:T(8,128)S(1)}, u32[]{:S(2)}, u32[]{:S(2)}) collective-permute-start(f32[16,1152]{1,0:T(8,128)S(1)} %constant_dynamic-slice_fusion.1), channel_id=1, source_target_pairs={{0,8},{1,9},{2,10},{3,11},{4,12},{5,13},{6,14},{7,15},{8,0},{9,1},... | collective-permute-start | bytes 221192 | tf_op jit(solution)/shard_map/ppermute | solution.py:688
  173.5 6.3 %collective-permute-start.15 = (f32[8,1920]{1,0:T(8,128)S(1)}, f32[8,1920]{1,0:T(8,128)S(1)}, u32[]{:S(2)}, u32[]{:S(2)}) collective-permute-start(f32[8,1920]{1,0:T(8,128)S(1)} %constant_dynamic-slice_fusion.4), channel_id=1, source_target_pairs={{0,16},{1,17},{2,18},{3,19},{4,20},{5,21},{6,22},{7,23},{8,24},{9,... | collective-permute-start | bytes 184328 | tf_op jit(solution)/shard_map/ppermute | solution.py:688
  177.1 4.9 %collective-permute-start.19 = (f32[8,1152]{1,0:T(8,128)S(1)}, f32[8,1152]{1,0:T(8,128)S(1)}, u32[]{:S(2)}, u32[]{:S(2)}) collective-permute-start(f32[8,1152]{1,0:T(8,128)S(1)} %constant_dynamic-slice_fusion), channel_id=1, source_target_pairs={{0,16},{1,17},{2,18},{3,19},{4,20},{5,21},{6,22},{7,23},{8,24},{9,... | collective-permute-start | bytes 110600 | tf_op jit(solution)/shard_map/ppermute | solution.py:688
  182.0 4.7 %collective-permute-start.20 = (f32[8,3072]{1,0:T(8,128)S(1)}, f32[8,3072]{1,0:T(8,128)S(1)}, u32[]{:S(2)}, u32[]{:S(2)}) collective-permute-start(f32[8,3072]{1,0:T(8,128)S(1)} %pad_maximum_fusion.1), channel_id=1, source_target_pairs={{0,2},{1,3},{2,0},{3,1},{4,6},{5,7},{6,4},{7,5},{8,10},{9,11},{10,... | collective-permute-start | bytes 294920 | tf_op jit(solution)/shard_map/ppermute | solution.py:814
  186.8 6.7 %collective-permute-start.21 = (f32[8,3072]{1,0:T(8,128)S(1)}, f32[8,3072]{1,0:T(8,128)S(1)}, u32[]{:S(2)}, u32[]{:S(2)}) collective-permute-start(f32[8,3072]{1,0:T(8,128)S(1)} %maximum_select_fusion.4), channel_id=1, source_target_pairs={{0,16},{1,17},{2,18},{3,19},{4,20},{5,21},{6,22},{7,23},{8,24},{9,... | collective-permute-start | bytes 294920 | tf_op jit(solution)/shard_map/ppermute | solution.py:695
  193.6 5.7 %collective-permute-start.22 = (f32[16,3072]{1,0:T(8,128)S(1)}, f32[16,3072]{1,0:T(8,128)S(1)}, u32[]{:S(2)}, u32[]{:S(2)}) collective-permute-start(f32[16,3072]{1,0:T(8,128)S(1)} %maximum_select_fusion.3), channel_id=1, source_target_pairs={{0,8},{1,9},{2,10},{3,11},{4,12},{5,13},{6,14},{7,15},{8,0},{9,1},... | collective-permute-start | bytes 589832 | tf_op jit(solution)/shard_map/ppermute | solution.py:695
  199.3 7.8 %collective-permute-start.23 = (f32[32,3072]{1,0:T(8,128)S(1)}, f32[32,3072]{1,0:T(8,128)S(1)}, u32[]{:S(2)}, u32[]{:S(2)}) collective-permute-start(f32[32,3072]{1,0:T(8,128)S(1)} %maximum_select_fusion.2), channel_id=1, source_target_pairs={{0,4},{1,5},{2,6},{3,7},{4,0},{5,1},{6,2},{7,3},{8,12},{9,13},{10,... | collective-permute-start | bytes 1179656 | tf_op jit(solution)/shard_map/ppermute | solution.py:695
  207.2 2.4 %collective-permute-start.24 = (f32[64,3072]{1,0:T(8,128)S(1)}, f32[64,3072]{1,0:T(8,128)S(1)}, u32[]{:S(2)}, u32[]{:S(2)}) collective-permute-start(f32[64,3072]{1,0:T(8,128)S(1)} %maximum_select_fusion.1), channel_id=1, source_target_pairs={{0,1},{1,0},{2,3},{3,2},{4,5},{5,4},{6,7},{7,6},{8,9},{9,8},{10,11... | collective-permute-start | bytes 2359304 | tf_op jit(solution)/shard_map/ppermute | solution.py:695

commit v3 on v2

--- a/solution.py
+++ b/solution.py
@@ -196,7 +196,7 @@
     )
 
 
-COST = 0.1
+COST = 0.02
 
 
 def cost(micros):
@@ -743,7 +743,7 @@
     w_other = jnp.where(at_zero, w_in_back, w_out)
 
     band = rows // CHUNKS // 2
-    got = []
+    entries, slopes = [], []
     for chunk in range(CHUNKS):
         start = chunk * 2 * band + (1 - core) * band - 1
         sent = [
@@ -751,54 +751,53 @@
             for value in (latents, cotangent)
         ]
         if chunk > 0:
-            sent = [after(value, *got[0]) for value in sent]
-        got.append([lax.ppermute(value, "tm", swap_cores) for value in sent])
-    middles, slopes = [], []
-    for chunk in range(CHUNKS):
+            sent = [after(value, act) for value in sent]
+        got = [lax.ppermute(value, "tm", swap_cores) for value in sent]
         start = chunk * 2 * band + core * band - 1
         kept = jnp.clip(start, 0, rows - band - 2)
         front_ids = jnp.concatenate([ids, jnp.stack([kept, start - kept]).astype(jnp.int32)])
         act, back, slope = front(
-            front_ids, [latents, got[chunk][0]], [cotangent, got[chunk][1]], w_in, w_out_back
+            front_ids, [latents, got[0]], [cotangent, got[1]], w_in, w_out_back
         )
         slopes.append(slope)
         leaving = jnp.where(at_zero, act[2 * slots - REACH :], back[:REACH])
         if chunk > 0:
             leaving = after(leaving, halo)
         halo = lax.ppermute(leaving, "tm", swap_sides)
-        middles.append(middle(ids, act, back, slope, halo, w_one, w_two_back, w_first))
-    halos, own, got = [], [], []
+        entries.append([act, back, slope, halo])
+    middles, halos, own, got = [], [], [], []
     outs = None
     sums_first = jnp.zeros((chans, 9 * chans), F32)
-    for chunk, made in enumerate(middles):
+    for chunk in range(CHUNKS):
+        act, back, slope, arrived = entries[chunk]
+        made = middle(ids, act, back, slope, arrived, w_one, w_two_back, w_first)
+        middles.append(made)
+        own.append(made[2])
+        got.append(lax.ppermute(made[3], "tm", swap_cores))
+        *outs, sums_first = ending(
+            chunk, factor, ids, own, got, latents, cotangent, w_ending, sums_first, outs
+        )
         halo = lax.ppermute(after(made[0], halo, sums_first), "tm", swap_sides)
         halos.append(halo)
-        own.append(made[2])
-        leaving = made[3] if chunk == 0 else after(made[3], sums_first)
-        got.append(lax.ppermute(leaving, "tm", swap_cores))
-        *outs, sums_first = ending(
-            chunk, factor, ids, own, got, latents, cotangent, w_ending, sums_first, outs
-        )
-
-    halos[-1] = after(halos[-1], sums_first)
-    seconds = [
-        second(ids, made[1], slope, halo, w_second)
-        for made, slope, halo in zip(middles, slopes, halos)
-    ]
-    own = [made[0] for made in seconds]
-    got = [lax.ppermute(made[1], "tm", swap_cores) for made in seconds]
-    ids = ids_for(1 - side)
-    sums_second = jnp.zeros((chans, 9 * chans), F32)
-    for chunk in range(CHUNKS):
-        *outs, sums_second = ending(
-            chunk, factor, ids, own, got, latents, cotangent, w_other, sums_second, outs
-        )
-    decoded, latent_grad = outs
 
     pairs = flips(dp_size, 4)
     place = lax.axis_index("dp") * 4 + tm_index
     digits = [0] + list(range(2, len(pairs)))
     span = 9 * chans
+    ids = ids_for(1 - side)
+    own, got = [], []
+    sums_second = jnp.zeros((chans, span), F32)
+    for chunk, made in enumerate(middles):
+        keep, leaving = second(ids, made[1], slopes[chunk], halos[chunk], w_second)
+        own.append(keep)
+        got.append(lax.ppermute(leaving, "tm", swap_cores))
+        *outs, sums_second = ending(
+            chunk, factor, ids, own, got, latents, cotangent, w_other, sums_second, outs
+        )
+        if chunk < CHUNKS - 1:
+            halos[chunk + 1] = after(halos[chunk + 1], sums_second)
+    decoded, latent_grad = outs
+
     early = jnp.concatenate(
         [
             sums_first,
@@ -807,7 +806,7 @@
         ],
         1,
     )
-    early = after(early, halos[-2])
+    early = after(early, halos[-1])
     early = halve(early, digits, pairs, place)
     late = halve(sums_second, digits, pairs, place)
     both = jnp.concatenate([early, late], 1)
@@ -817,7 +816,7 @@
     both = jnp.where(
         at_zero, both, jnp.concatenate([both[:, -span:], both[:, span:-span], both[:, :span]], 1)
     )
-    both = double(both, digits[::-1], pairs, place)
+    both = double(both.astype(BF), digits[::-1], pairs, place).astype(F32)
     spatial_sums = (both[:, :span], both[:, -span:])
     temporal_sums = both[:, span:-span]
 

time: 215 us -> 202 us (0.940)
  waiting for transfers between devices: 50.1 us -> 37.6 us
  starting transfers between devices: 22.6 us -> 25.7 us
    ppermute x2, waiting for transfers between devices: 13.9 us -> 4.61 us  [on_chip_pair(): halo = lax.ppermute(leaving, 'tm', swap_sides)]
    ppermute x4, waiting for transfers between devices: 19.8 us -> 12.5 us  [double(): other = lax.ppermute(values, ('dp', 'tm'), pairs[digit])]
    ppermute x6, waiting for transfers between devices: 0.34 us -> 3.49 us  [the longest x2 3.31 us: on_chip_pair(): got.append(lax.ppermute(made[3], 'tm', swap_cores))]
    transpose x4, local copies, waits for them, and re-layouts: 2.82 us -> 0.48 us  [turned(): return jnp.transpose(kernel[::-1, ::-1], (0, 1, 3, 2))]
    unnamed x43 -> x39, local copies, waits for them, and re-layouts: 9 us -> 8.91 us
  transfers between devices with their start and end apart: 25 -> 25, of which waited for: 14 -> 16; matrix products, arithmetic and copies ran while one was open for 11% -> 10% of each run, Pallas kernels for 48% -> 44%
where the time goes in v3:
time: 202 us
  Pallas kernels  102 us (50%)
  waiting for transfers between devices  37.6 us (19%)
  starting transfers between devices  25.7 us (13%)
  local copies, waits for them, and re-layouts  22.1 us (11%)
  other arithmetic  12.5 us (6%)
    pallas_call x4, Pallas kernels, ending(): pl.pallas_call(functools.partial(ending_kernel, chunk, rows, factor, outs...  41.8 us
    pallas_call x2, Pallas kernels, front(): pl.pallas_call(front_kernel, grid_spec=pltpu.PrefetchScalarGridSpec(num_s...  24.8 us
    pallas_call x2, Pallas kernels, middle(): pl.pallas_call(middle_kernel, grid_spec=pltpu.PrefetchScalarGridSpec(num_...  23.3 us
    ppermute x4, waiting for transfers between devices, double(): other = lax.ppermute(values, ('dp', 'tm'), pairs[digit])  12.5 us
    pallas_call x2, Pallas kernels, second(): pl.pallas_call(second_kernel, grid_spec=pltpu.PrefetchScalarGridSpec(num_...  12.2 us
    ppermute x8, starting transfers between devices, halve(): values = keep + lax.ppermute(send, ('dp', 'tm'), pairs[digit])  11.2 us
    unnamed x39, local copies, waits for them, and re-layouts  8.91 us
    ppermute x8, waiting for transfers between devices, halve(): values = keep + lax.ppermute(send, ('dp', 'tm'), pairs[digit])  8.36 us
  transfers between devices with their start and end apart: 25, of which 16 were waited for; matrix products, arithmetic and copies ran while one was open for 10% of the time, Pallas kernels for 44%

profile of v3, /device:TPU:0, one launch (start us, length us, event | category | flops | bytes accessed | tf_op | source)
XLA Modules:
  0.0 201.7 jit_solution(11018910018516650773)
XLA Ops:
  0.7 3.5 %dynamic-slice_bitcast_fusion.1 = (bf16[6,6,128,128]{3,2,1,0:T(8,128)(2,1)}, bf16[6,6,128,128]{3,2,1,0:T(8,128)(2,1)}) fusion(bf16[1,6,16,128,128]{4,3,2,1,0:T(8,128)(2,1)} %param.8, s32[]{:T(128)S(6)} %min.18, s32[]{:T(128)S(6)} %min.16), kind=kLoop, calls=%fused_computation.11 | loop fusion | bytes 4718600 | tf_op jit(solution)/shard_map/dynamic_slice | solution.py:750
  4.7 1.6 dynamic-slice_bitcast_fusion
  7.8 1.3 fusion.8
  9.3 1.0 copy-done.3
  10.3 12.6 %front.2 = (bf16[2,6,4,128,128]{4,3,2,1,0:T(8,128)(2,1)}, bf16[2,6,4,128,128]{4,3,2,1,0:T(8,128)(2,1)}, bf16[2,6,4,128,128]{4,3,2,1,0:T(8,128)(2,1)}) custom-call(s32[8]{0:T(128)} %concatenate.56.ids, bf16[6,16,128,128]{3,2,1,0:T(8,128)(2,1)} %bitcast.56, bf16[6,6,128,128]{3,2,1,0:T(8,128)(2,1)} %collective-permute-done.refs_1_, ...), custom_call_target="tpu_custom_call" | custom-call | flops 220000000 | bytes 1000 | tf_op jit(solution)/shard_map/front/pallas_call | solution.py:312
  23.4 2.7 %slice_select_fusion.1 = bf16[8,4,128,128]{3,2,1,0:T(8,128)(2,1)} fusion(bf16[12,4,128,128]{3,2,1,0:T(8,128)(2,1)} %bitcast.76, bf16[12,4,128,128]{3,2,1,0:T(8,128)(2,1)} %bitcast.74, pred[]{:T(512)S(6)} %eq.17), kind=kLoop, calls=%fused_computation.15 | loop fusion | flops 524288 | bytes 3145729 | tf_op jit(solution)/shard_map/jit(_where)/select_n | solution.py:763
  26.1 2.8 %collective-permute-start.2 = (bf16[8,4,128,128]{3,2,1,0:T(8,128)(2,1)}, bf16[8,4,128,128]{3,2,1,0:T(8,128)(2,1)}, u32[]{:S(2)}, u32[]{:S(2)}) collective-permute-start(bf16[8,4,128,128]{3,2,1,0:T(8,128)(2,1)} %slice_select_fusion.1), channel_id=1, source_target_pairs={{0,2},{2,0},{1,3},{3,1},{4,6},{6,4},{5,7},{7,5},{8,10},{10,8},{9,1... | collective-permute-start | bytes 3145736 | tf_op jit(solution)/shard_map/ppermute | solution.py:766
  32.1 1.1 copy-done.5
  33.1 12.2 %front.3 = (bf16[2,6,4,128,128]{4,3,2,1,0:T(8,128)(2,1)}, bf16[2,6,4,128,128]{4,3,2,1,0:T(8,128)(2,1)}, bf16[2,6,4,128,128]{4,3,2,1,0:T(8,128)(2,1)}) custom-call(s32[8]{0:T(128)} %concatenate.59.ids, bf16[6,16,128,128]{3,2,1,0:T(8,128)(2,1)} %bitcast.57, bf16[6,6,128,128]{3,2,1,0:T(8,128)(2,1)} %copy-done.4, bf16[6,16,128,128]{3,2,1,0:T(8,128)(2,1)} %bitcast.63, ...), custom_call_target="tpu_custom_call" | custom-call | flops 220000000 | bytes 1000 | tf_op jit(solution)/shard_map/front/pallas_call | solution.py:312
  45.4 2.6 %slice_select_fusion = bf16[8,4,128,128]{3,2,1,0:T(8,128)(2,1)} fusion(bf16[12,4,128,128]{3,2,1,0:T(8,128)(2,1)} %bitcast.80, bf16[12,4,128,128]{3,2,1,0:T(8,128)(2,1)} %bitcast.78, pred[]{:T(512)S(6)} %eq.17), kind=kLoop, calls=%fused_computation.14 | loop fusion | flops 524288 | bytes 3145729 | tf_op jit(solution)/shard_map/jit(_where)/select_n | solution.py:763
  48.0 4.6 %collective-permute-done.2.halo = bf16[8,4,128,128]{3,2,1,0:T(8,128)(2,1)} collective-permute-done((bf16[8,4,128,128]{3,2,1,0:T(8,128)(2,1)}, bf16[8,4,128,128]{3,2,1,0:T(8,128)(2,1)}, u32[]{:S(2)}, u32[]{:S(2)}) %collective-permute-start.2) | collective-permute-done | bytes 1048608 | tf_op jit(solution)/shard_map/ppermute | solution.py:766
  52.6 1.7 collective-permute-start.5
  55.0 11.6 %middle.2 = (bf16[8,4,128,128]{3,2,1,0:T(8,128)(2,1)}, bf16[12,4,128,128]{3,2,1,0:T(8,128)(2,1)}, bf16[6,4,128,128]{3,2,1,0:T(8,128)(2,1)}, bf16[6,4,128,128]{3,...) custom-call(s32[6]{0:T(128)} %stack.39.ids, bf16[12,4,128,128]{3,2,1,0:T(8,128)(2,1)} %bitcast.75, ...), custom_call_target="tpu_custom_call" | custom-call | flops 240000000 | bytes 1000 | tf_op jit(solution)/shard_map/middle/pallas_call | solution.py:430
  67.0 1.4 broadcast_select_fusion
  70.4 8.6 %ending.4 = (bf16[6,16,128,128]{3,2,1,0:T(8,128)(2,1)}, bf16[6,16,128,128]{3,2,1,0:T(8,128)(2,1)}, f32[128,1152]{1,0:T(8,128)}) custom-call(s32[6]{0:T(128)} %stack.39.ids, bf16[6,4,128,128]{3,2,1,0:T(8,128)(2,1)} %get-tuple-element.57.refs_0_, bf16[6,4,128,128]{3,2,1,0:T(8,128)(2,1)} %copy-done.2, bf16[6,16,128,128]{3,2,1,0:T(8,128)(2,1)} %bitcast.58, ...), custom_call_target="tpu_custom_call" | custom-call | flops 260000000 | bytes 1000 | tf_op jit(solution)/shard_map/ending/pallas_call | solution.py:627
  79.8 11.7 %middle.3 = (bf16[8,4,128,128]{3,2,1,0:T(8,128)(2,1)}, bf16[12,4,128,128]{3,2,1,0:T(8,128)(2,1)}, bf16[6,4,128,128]{3,2,1,0:T(8,128)(2,1)}, bf16[6,4,128,128]{3,...) custom-call(s32[6]{0:T(128)} %stack.39.ids, bf16[12,4,128,128]{3,2,1,0:T(8,128)(2,1)} %bitcast.79, ...), custom_call_target="tpu_custom_call" | custom-call | flops 240000000 | bytes 1000 | tf_op jit(solution)/shard_map/middle/pallas_call | solution.py:430
  91.5 2.5 %collective-permute-done.8.refs_3_ = bf16[6,4,128,128]{3,2,1,0:T(8,128)(2,1)S(1)} collective-permute-done((bf16[6,4,128,128]{3,2,1,0:T(8,128)(2,1)}, bf16[6,4,128,128]{3,2,1,0:T(8,128)(2,1)S(1)}, u32[]{:S(2)}, u32[]{:S(2)}) %collective-permute-start.8) | collective-permute-done | bytes 786464 | tf_op jit(solution)/shard_map/ppermute | solution.py:776
  94.9 12.4 %ending.5 = (bf16[6,16,128,128]{3,2,1,0:T(8,128)(2,1)}, bf16[6,16,128,128]{3,2,1,0:T(8,128)(2,1)}, f32[128,1152]{1,0:T(8,128)}) custom-call(s32[6]{0:T(128)} %stack.39.ids, bf16[6,4,128,128]{3,2,1,0:T(8,128)(2,1)} %get-tuple-element.57.refs_0_, bf16[6,4,128,128]{3,2,1,0:T(8,128)(2,1)} %get-tuple-element.65.refs_1_, ...), custom_call_target="tpu_custom_call", output_to_operand_aliasing={{0}: (9, {}), {1}: (10, {})} | custom-call | flops 260000000 | bytes 1000 | tf_op jit(solution)/shard_map/ending/pallas_call | solution.py:627
  107.3 1.8 collective-permute-start.9
  109.8 6.1 %second.2 = (bf16[6,4,128,128]{3,2,1,0:T(8,128)(2,1)}, bf16[6,4,128,128]{3,2,1,0:T(8,128)(2,1)}) custom-call(s32[6]{0:T(128)} %stack.38.ids, bf16[12,4,128,128]{3,2,1,0:T(8,128)(2,1)} %get-tuple-element.50.mid, bf16[12,4,128,128]{3,2,1,0:T(8,128)(2,1)} %bitcast.73, bf16[8,4,128,128]{3,2,1,0:T(8,128)(2,1)} %copy-done.9, bf16[384,128]{1,0:T(8,128)(2,1)} %bitcast.91), custom_call_target="tpu_custom_call" | custom-call | flops 100000000 | bytes 1000 | tf_op jit(solution)/shard_map/second/pallas_call | solution.py:500
  115.9 1.1 add_multiply_fusion
  117.0 1.0 add_multiply_fusion.1
  119.3 8.5 %ending.6 = (bf16[6,16,128,128]{3,2,1,0:T(8,128)(2,1)}, bf16[6,16,128,128]{3,2,1,0:T(8,128)(2,1)}, f32[128,1152]{1,0:T(8,128)}) custom-call(s32[6]{0:T(128)} %stack.38.ids, bf16[6,4,128,128]{3,2,1,0:T(8,128)(2,1)} %get-tuple-element.61.refs_0_, bf16[6,4,128,128]{3,2,1,0:T(8,128)(2,1)} %copy-done.1, ...), custom_call_target="tpu_custom_call", output_to_operand_aliasing={{0}: (7, {}), {1}: (8, {})} | custom-call | flops 260000000 | bytes 1000 | tf_op jit(solution)/shard_map/ending/pallas_call | solution.py:627
  127.8 5.0 %collective-permute-done.9.halo = bf16[8,4,128,128]{3,2,1,0:T(8,128)(2,1)S(1)} collective-permute-done((bf16[8,4,128,128]{3,2,1,0:T(8,128)(2,1)}, bf16[8,4,128,128]{3,2,1,0:T(8,128)(2,1)S(1)}, u32[]{:S(2)}, u32[]{:S(2)}) %collective-permute-start.9) | collective-permute-done | bytes 1048608 | tf_op jit(solution)/shard_map/ppermute | solution.py:780
  133.8 6.1 %second.3 = (bf16[6,4,128,128]{3,2,1,0:T(8,128)(2,1)}, bf16[6,4,128,128]{3,2,1,0:T(8,128)(2,1)}) custom-call(s32[6]{0:T(128)} %stack.38.ids, bf16[12,4,128,128]{3,2,1,0:T(8,128)(2,1)} %get-tuple-element.63.mid, bf16[12,4,128,128]{3,2,1,0:T(8,128)(2,1)} %bitcast.71, bf16[8,4,128,128]{3,2,1,0:T(8,128)(2,1)} %copy-done.8, bf16[384,128]{1,0:T(8,128)(2,1)} %bitcast.92), custom_call_target="tpu_custom_call" | custom-call | flops 100000000 | bytes 1000 | tf_op jit(solution)/shard_map/second/pallas_call | solution.py:500
  139.9 1.1 dynamic-slice_add_fusion
  141.0 1.8 collective-permute-start.13
  143.7 12.2 %ending.7 = (bf16[6,16,128,128]{3,2,1,0:T(8,128)(2,1)}, bf16[6,16,128,128]{3,2,1,0:T(8,128)(2,1)}, f32[128,1152]{1,0:T(8,128)}) custom-call(s32[6]{0:T(128)} %stack.38.ids, bf16[6,4,128,128]{3,2,1,0:T(8,128)(2,1)} %get-tuple-element.61.refs_0_, bf16[6,4,128,128]{3,2,1,0:T(8,128)(2,1)} %get-tuple-element.76.refs_1_, ...), custom_call_target="tpu_custom_call", output_to_operand_aliasing={{0}: (9, {}), {1}: (10, {})} | custom-call | flops 260000000 | bytes 1000 | tf_op jit(solution)/shard_map/ending/pallas_call | solution.py:627
  156.0 1.0 constant_dynamic-slice_fusion.3
  157.4 1.6 collective-permute-start.14
  159.1 1.3 collective-permute-start.17
  160.4 2.6 %collective-permute-done.14 = f32[16,1920]{1,0:T(8,128)S(1)} collective-permute-done((f32[16,1920]{1,0:T(8,128)S(1)}, f32[16,1920]{1,0:T(8,128)S(1)}, u32[]{:S(2)}, u32[]{:S(2)}) %collective-permute-start.14) | collective-permute-done | bytes 122912 | tf_op jit(solution)/shard_map/ppermute | solution.py:688
  163.0 1.9 collective-permute-done.17
  165.0 1.5 collective-permute-start.18
  166.5 2.6 %collective-permute-start.15 = (f32[8,1920]{1,0:T(8,128)S(1)}, f32[8,1920]{1,0:T(8,128)S(1)}, u32[]{:S(2)}, u32[]{:S(2)}) collective-permute-start(f32[8,1920]{1,0:T(8,128)S(1)} %constant_dynamic-slice_fusion.4), channel_id=1, source_target_pairs={{0,16},{1,17},{2,18},{3,19},{4,20},{5,21},{6,22},{7,23},{8,24},{9,... | collective-permute-start | bytes 184328 | tf_op jit(solution)/shard_map/ppermute | solution.py:688
  170.0 2.0 %collective-permute-start.19 = (f32[8,1152]{1,0:T(8,128)S(1)}, f32[8,1152]{1,0:T(8,128)S(1)}, u32[]{:S(2)}, u32[]{:S(2)}) collective-permute-start(f32[8,1152]{1,0:T(8,128)S(1)} %constant_dynamic-slice_fusion), channel_id=1, source_target_pairs={{0,16},{1,17},{2,18},{3,19},{4,20},{5,21},{6,22},{7,23},{8,24},{9,... | collective-permute-start | bytes 110600 | tf_op jit(solution)/shard_map/ppermute | solution.py:688
  172.8 2.1 %collective-permute-done.19 = f32[8,1152]{1,0:T(8,128)S(1)} collective-permute-done((f32[8,1152]{1,0:T(8,128)S(1)}, f32[8,1152]{1,0:T(8,128)S(1)}, u32[]{:S(2)}, u32[]{:S(2)}) %collective-permute-start.19) | collective-permute-done | bytes 36896 | tf_op jit(solution)/shard_map/ppermute | solution.py:688
  175.0 1.3 collective-permute-start.20
  176.3 3.4 %collective-permute-done.20 = f32[8,3072]{1,0:T(8,128)S(1)} collective-permute-done((f32[8,3072]{1,0:T(8,128)S(1)}, f32[8,3072]{1,0:T(8,128)S(1)}, u32[]{:S(2)}, u32[]{:S(2)}) %collective-permute-start.20) | collective-permute-done | bytes 98336 | tf_op jit(solution)/shard_map/ppermute | solution.py:813
  179.8 2.1 %collective-permute-start.21 = (bf16[8,3072]{1,0:T(8,128)(2,1)S(1)}, bf16[8,3072]{1,0:T(8,128)(2,1)S(1)}, u32[]{:S(2)}, u32[]{:S(2)}) collective-permute-start(bf16[8,3072]{1,0:T(8,128)(2,1)S(1)} %fusion.13), channel_id=1, source_target_pairs={{0,16},{1,17},{2,18},{3,19},{4,20},{5,21},{6,22},{7,23},{8,24},{9,... | collective-permute-start | bytes 147464 | tf_op jit(solution)/shard_map/ppermute | solution.py:695
  181.8 3.1 %collective-permute-done.21 = bf16[8,3072]{1,0:T(8,128)(2,1)S(1)} collective-permute-done((bf16[8,3072]{1,0:T(8,128)(2,1)S(1)}, bf16[8,3072]{1,0:T(8,128)(2,1)S(1)}, u32[]{:S(2)}, u32[]{:S(2)}) %collective-permute-start.21) | collective-permute-done | bytes 49184 | tf_op jit(solution)/shard_map/ppermute | solution.py:695
  185.0 1.4 collective-permute-start.22
  186.4 3.3 %collective-permute-done.22 = bf16[16,3072]{1,0:T(8,128)(2,1)S(1)} collective-permute-done((bf16[16,3072]{1,0:T(8,128)(2,1)S(1)}, bf16[16,3072]{1,0:T(8,128)(2,1)S(1)}, u32[]{:S(2)}, u32[]{:S(2)}) %collective-permute-start.22) | collective-permute-done | bytes 98336 | tf_op jit(solution)/shard_map/ppermute | solution.py:695
  189.7 1.4 collective-permute-start.23
  191.1 4.3 %collective-permute-done.23 = bf16[32,3072]{1,0:T(8,128)(2,1)S(1)} collective-permute-done((bf16[32,3072]{1,0:T(8,128)(2,1)S(1)}, bf16[32,3072]{1,0:T(8,128)(2,1)S(1)}, u32[]{:S(2)}, u32[]{:S(2)}) %collective-permute-start.23) | collective-permute-done | bytes 196640 | tf_op jit(solution)/shard_map/ppermute | solution.py:695
  195.6 1.7 collective-permute-done.24
  197.9 1.1 copy.36
  198.9 1.0 copy.33
  (105 shorter events, 18.4 us)
Async XLA Ops:
  0.7 4.0 %copy-start = (bf16[1,6,16,128,128]{4,3,2,1,0:T(8,128)(2,1)S(1)}, bf16[1,6,16,128,128]{4,3,2,1,0:T(8,128)(2,1)}, u32[]{:S(2)}) copy-start(bf16[1,6,16,128,128]{4,3,2,1,0:T(8,128)(2,1)} %param.9) | copy-start | bytes 9437188
  4.1 2.8 %copy-start.6 = (bf16[3,3,128,128]{3,2,1,0:T(8,128)(2,1)S(1)}, bf16[3,3,128,128]{3,2,1,0:T(8,128)(2,1)}, u32[]{:S(2)}) copy-start(bf16[3,3,128,128]{3,2,1,0:T(8,128)(2,1)} %param.11) | copy-start | bytes 884740
  4.1 3.1 %copy-start.16 = (s32[2]{0:T(128)S(1)}, s32[2]{0:T(128)}, u32[]{:S(2)}) copy-start(s32[2]{0:T(128)} %param.15) | copy-start | bytes 28
  4.1 3.7 %copy-start.7 = (bf16[3,3,128,128]{3,2,1,0:T(8,128)(2,1)S(1)}, bf16[3,3,128,128]{3,2,1,0:T(8,128)(2,1)}, u32[]{:S(2)}) copy-start(bf16[3,3,128,128]{3,2,1,0:T(8,128)(2,1)} %param.10) | copy-start | bytes 884740
  4.2 5.0 %collective-permute-start = (bf16[6,6,128,128]{3,2,1,0:T(8,128)(2,1)}, bf16[6,6,128,128]{3,2,1,0:T(8,128)(2,1)}, u32[]{:S(2)}, u32[]{:S(2)}) collective-permute-start(bf16[6,6,128,128]{3,2,1,0:T(8,128)(2,1)} %get-tuple-element.97), channel_id=1, source_target_pairs={{0,1},{1,0},{2,3},{3,2},{4,5},{5,4},{6,7},{7,6},{8,9},{9,8},{10,11... | collective-permute-start | bytes 3538952 | tf_op jit(solution)/shard_map/ppermute | solution.py:755
  6.2 3.1 %collective-permute-start.1 = (bf16[6,6,128,128]{3,2,1,0:T(8,128)(2,1)}, bf16[6,6,128,128]{3,2,1,0:T(8,128)(2,1)S(1)}, u32[]{:S(2)}, u32[]{:S(2)}) collective-permute-start(bf16[6,6,128,128]{3,2,1,0:T(8,128)(2,1)} %get-tuple-element.95), channel_id=1, source_target_pairs={{0,1},{1,0},{2,3},{3,2},{4,5},{5,4},{6,7},{7,6},{8,9},{9,8},{10,11... | collective-permute-start | bytes 3538952 | tf_op jit(solution)/shard_map/ppermute | solution.py:755
  9.3 1.0 copy-start.3
  22.9 8.1 %collective-permute-start.3 = (bf16[6,6,128,128]{3,2,1,0:T(8,128)(2,1)}, bf16[6,6,128,128]{3,2,1,0:T(8,128)(2,1)S(1)}, u32[]{:S(2)}, u32[]{:S(2)}) collective-permute-start(bf16[6,6,128,128]{3,2,1,0:T(8,128)(2,1)} %get-tuple-element.52), channel_id=1, source_target_pairs={{0,1},{1,0},{2,3},{3,2},{4,5},{5,4},{6,7},{7,6},{8,9},{9,8},{10,11... | collective-permute-start | bytes 3538952 | tf_op jit(solution)/shard_map/ppermute | solution.py:755
  22.9 8.1 %collective-permute-start.4 = (bf16[6,6,128,128]{3,2,1,0:T(8,128)(2,1)}, bf16[6,6,128,128]{3,2,1,0:T(8,128)(2,1)S(1)}, u32[]{:S(2)}, u32[]{:S(2)}) collective-permute-start(bf16[6,6,128,128]{3,2,1,0:T(8,128)(2,1)} %get-tuple-element.53), channel_id=1, source_target_pairs={{0,1},{1,0},{2,3},{3,2},{4,5},{5,4},{6,7},{7,6},{8,9},{9,8},{10,11... | collective-permute-start | bytes 3538952 | tf_op jit(solution)/shard_map/ppermute | solution.py:755
  23.4 6.1 %copy-start.15 = (bf16[3,128,128]{2,1,0:T(8,128)(2,1)S(1)}, bf16[3,128,128]{2,1,0:T(8,128)(2,1)}, u32[]{:S(2)}) copy-start(bf16[3,128,128]{2,1,0:T(8,128)(2,1)} %param.13) | copy-start | bytes 294916
  23.4 6.9 %copy-start.10 = (bf16[3,128,128]{2,1,0:T(8,128)(2,1)S(1)}, bf16[3,128,128]{2,1,0:T(8,128)(2,1)}, u32[]{:S(2)}) copy-start(bf16[3,128,128]{2,1,0:T(8,128)(2,1)} %param.12) | copy-start | bytes 294916
  26.1 26.5 %collective-permute-start.2 = (bf16[8,4,128,128]{3,2,1,0:T(8,128)(2,1)}, bf16[8,4,128,128]{3,2,1,0:T(8,128)(2,1)}, u32[]{:S(2)}, u32[]{:S(2)}) collective-permute-start(bf16[8,4,128,128]{3,2,1,0:T(8,128)(2,1)} %slice_select_fusion.1), channel_id=1, source_target_pairs={{0,2},{2,0},{1,3},{3,1},{4,6},{6,4},{5,7},{7,5},{8,10},{10,8},{9,1... | collective-permute-start | bytes 3145736 | tf_op jit(solution)/shard_map/ppermute | solution.py:766
  31.0 1.0 copy-start.4
  32.1 1.1 copy-start.5
  52.6 26.4 %collective-permute-start.5 = (bf16[8,4,128,128]{3,2,1,0:T(8,128)(2,1)}, bf16[8,4,128,128]{3,2,1,0:T(8,128)(2,1)}, u32[]{:S(2)}, u32[]{:S(2)}) collective-permute-start(bf16[8,4,128,128]{3,2,1,0:T(8,128)(2,1)} %slice_select_fusion), channel_id=1, source_target_pairs={{0,2},{2,0},{1,3},{3,1},{4,6},{6,4},{5,7},{7,5},{8,10},{10,8},{9,1... | collective-permute-start | bytes 3145736 | tf_op jit(solution)/shard_map/ppermute | solution.py:766
  66.7 2.6 %collective-permute-start.6 = (bf16[6,4,128,128]{3,2,1,0:T(8,128)(2,1)}, bf16[6,4,128,128]{3,2,1,0:T(8,128)(2,1)S(1)}, u32[]{:S(2)}, u32[]{:S(2)}) collective-permute-start(bf16[6,4,128,128]{3,2,1,0:T(8,128)(2,1)} %get-tuple-element.58), channel_id=1, source_target_pairs={{0,1},{1,0},{2,3},{3,2},{4,5},{5,4},{6,7},{7,6},{8,9},{9,8},{10,11... | collective-permute-start | bytes 2359304 | tf_op jit(solution)/shard_map/ppermute | solution.py:776
  69.2 1.1 copy-start.2
  70.4 8.7 %copy-start.17 = (bf16[8,4,128,128]{3,2,1,0:T(8,128)(2,1)S(1)}, bf16[8,4,128,128]{3,2,1,0:T(8,128)(2,1)}, u32[]{:S(2)}) copy-start(bf16[8,4,128,128]{3,2,1,0:T(8,128)(2,1)} %get-tuple-element.60) | copy-start | bytes 3145732
  79.0 28.3 %collective-permute-start.7 = (bf16[8,4,128,128]{3,2,1,0:T(8,128)(2,1)S(1)}, bf16[8,4,128,128]{3,2,1,0:T(8,128)(2,1)S(1)}, u32[]{:S(2)}, u32[]{:S(2)}) collective-permute-start(bf16[8,4,128,128]{3,2,1,0:T(8,128)(2,1)S(1)} %copy-done.17), channel_id=1, source_target_pairs={{0,2},{2,0},{1,3},{3,1},{4,6},{6,4},{5,7},{7,5},{8,10},{10,8},{9,1... | collective-permute-start | bytes 3145736 | tf_op jit(solution)/shard_map/ppermute | solution.py:780
  91.5 2.6 %collective-permute-start.8 = (bf16[6,4,128,128]{3,2,1,0:T(8,128)(2,1)}, bf16[6,4,128,128]{3,2,1,0:T(8,128)(2,1)S(1)}, u32[]{:S(2)}, u32[]{:S(2)}) collective-permute-start(bf16[6,4,128,128]{3,2,1,0:T(8,128)(2,1)} %get-tuple-element.66), channel_id=1, source_target_pairs={{0,1},{1,0},{2,3},{3,2},{4,5},{5,4},{6,7},{7,6},{8,9},{9,8},{10,11... | collective-permute-start | bytes 2359304 | tf_op jit(solution)/shard_map/ppermute | solution.py:776
  94.0 0.9 copy-start.12
  107.3 2.4 %copy-start.9 = (bf16[8,4,128,128]{3,2,1,0:T(8,128)(2,1)}, bf16[8,4,128,128]{3,2,1,0:T(8,128)(2,1)S(1)}, u32[]{:S(2)}) copy-start(bf16[8,4,128,128]{3,2,1,0:T(8,128)(2,1)S(1)} %collective-permute-done.7.halo) | copy-start | bytes 3145732
  107.3 25.5 %collective-permute-start.9 = (bf16[8,4,128,128]{3,2,1,0:T(8,128)(2,1)}, bf16[8,4,128,128]{3,2,1,0:T(8,128)(2,1)S(1)}, u32[]{:S(2)}, u32[]{:S(2)}) collective-permute-start(bf16[8,4,128,128]{3,2,1,0:T(8,128)(2,1)} %get-tuple-element.70), channel_id=1, source_target_pairs={{0,2},{2,0},{1,3},{3,1},{4,6},{6,4},{5,7},{7,5},{8,10},{10,8},{9,1... | collective-permute-start | bytes 3145736 | tf_op jit(solution)/shard_map/ppermute | solution.py:780
  115.9 2.2 %copy-start.14 = (f32[128,1152]{1,0:T(8,128)S(1)}, f32[128,1152]{1,0:T(8,128)}, u32[]{:S(2)}) copy-start(f32[128,1152]{1,0:T(8,128)} %get-tuple-element.69) | copy-start | bytes 1769476
  115.9 2.5 %collective-permute-start.10 = (bf16[6,4,128,128]{3,2,1,0:T(8,128)(2,1)}, bf16[6,4,128,128]{3,2,1,0:T(8,128)(2,1)S(1)}, u32[]{:S(2)}, u32[]{:S(2)}) collective-permute-start(bf16[6,4,128,128]{3,2,1,0:T(8,128)(2,1)} %get-tuple-element.71), channel_id=1, source_target_pairs={{0,1},{1,0},{2,3},{3,2},{4,5},{5,4},{6,7},{7,6},{8,9},{9,8},{10,11... | collective-permute-start | bytes 2359304 | tf_op jit(solution)/shard_map/ppermute | solution.py:793
  118.4 0.9 copy-start.1
  132.8 1.0 copy-start.8
  132.9 7.0 %collective-permute-start.12 = (f32[64,1920]{1,0:T(8,128)S(1)}, f32[64,1920]{1,0:T(8,128)}, u32[]{:S(2)}, u32[]{:S(2)}) collective-permute-start(f32[64,1920]{1,0:T(8,128)S(1)} %constant_dynamic-slice_fusion.7), channel_id=1, source_target_pairs={{0,1},{1,0},{2,3},{3,2},{4,5},{5,4},{6,7},{7,6},{8,9},{9,8},{10,11... | collective-permute-start | bytes 1474568 | tf_op jit(solution)/shard_map/ppermute | solution.py:688
  139.9 3.0 %collective-permute-start.11 = (bf16[6,4,128,128]{3,2,1,0:T(8,128)(2,1)}, bf16[6,4,128,128]{3,2,1,0:T(8,128)(2,1)S(1)}, u32[]{:S(2)}, u32[]{:S(2)}) collective-permute-start(bf16[6,4,128,128]{3,2,1,0:T(8,128)(2,1)} %get-tuple-element.77), channel_id=1, source_target_pairs={{0,1},{1,0},{2,3},{3,2},{4,5},{5,4},{6,7},{7,6},{8,9},{9,8},{10,11... | collective-permute-start | bytes 2359304 | tf_op jit(solution)/shard_map/ppermute | solution.py:793
  141.0 16.3 %collective-permute-start.13 = (f32[32,1920]{1,0:T(8,128)S(1)}, f32[32,1920]{1,0:T(8,128)S(1)}, u32[]{:S(2)}, u32[]{:S(2)}) collective-permute-start(f32[32,1920]{1,0:T(8,128)S(1)} %constant_dynamic-slice_fusion.6), channel_id=1, source_target_pairs={{0,4},{1,5},{2,6},{3,7},{4,0},{5,1},{6,2},{7,3},{8,12},{9,13},{10,... | collective-permute-start | bytes 737288 | tf_op jit(solution)/shard_map/ppermute | solution.py:688
  142.9 0.9 copy-start.11
  156.0 3.1 %copy-start.13 = (f32[128,1152]{1,0:T(8,128)S(1)}, f32[128,1152]{1,0:T(8,128)}, u32[]{:S(2)}) copy-start(f32[128,1152]{1,0:T(8,128)} %get-tuple-element.87) | copy-start | bytes 1769476
  157.0 2.0 collective-permute-start.16
  157.4 5.6 %collective-permute-start.14 = (f32[16,1920]{1,0:T(8,128)S(1)}, f32[16,1920]{1,0:T(8,128)S(1)}, u32[]{:S(2)}, u32[]{:S(2)}) collective-permute-start(f32[16,1920]{1,0:T(8,128)S(1)} %constant_dynamic-slice_fusion.5), channel_id=1, source_target_pairs={{0,8},{1,9},{2,10},{3,11},{4,12},{5,13},{6,14},{7,15},{8,0},{9,1},... | collective-permute-start | bytes 368648 | tf_op jit(solution)/shard_map/ppermute | solution.py:688
  159.1 5.8 %collective-permute-start.17 = (f32[32,1152]{1,0:T(8,128)S(1)}, f32[32,1152]{1,0:T(8,128)S(1)}, u32[]{:S(2)}, u32[]{:S(2)}) collective-permute-start(f32[32,1152]{1,0:T(8,128)S(1)} %constant_dynamic-slice_fusion.2), channel_id=1, source_target_pairs={{0,4},{1,5},{2,6},{3,7},{4,0},{5,1},{6,2},{7,3},{8,12},{9,13},{10,... | collective-permute-start | bytes 442376 | tf_op jit(solution)/shard_map/ppermute | solution.py:688
  165.0 5.0 %collective-permute-start.18 = (f32[16,1152]{1,0:T(8,128)S(1)}, f32[16,1152]{1,0:T(8,128)S(1)}, u32[]{:S(2)}, u32[]{:S(2)}) collective-permute-start(f32[16,1152]{1,0:T(8,128)S(1)} %constant_dynamic-slice_fusion.1), channel_id=1, source_target_pairs={{0,8},{1,9},{2,10},{3,11},{4,12},{5,13},{6,14},{7,15},{8,0},{9,1},... | collective-permute-start | bytes 221192 | tf_op jit(solution)/shard_map/ppermute | solution.py:688
  166.5 6.3 %collective-permute-start.15 = (f32[8,1920]{1,0:T(8,128)S(1)}, f32[8,1920]{1,0:T(8,128)S(1)}, u32[]{:S(2)}, u32[]{:S(2)}) collective-permute-start(f32[8,1920]{1,0:T(8,128)S(1)} %constant_dynamic-slice_fusion.4), channel_id=1, source_target_pairs={{0,16},{1,17},{2,18},{3,19},{4,20},{5,21},{6,22},{7,23},{8,24},{9,... | collective-permute-start | bytes 184328 | tf_op jit(solution)/shard_map/ppermute | solution.py:688
  170.0 4.9 %collective-permute-start.19 = (f32[8,1152]{1,0:T(8,128)S(1)}, f32[8,1152]{1,0:T(8,128)S(1)}, u32[]{:S(2)}, u32[]{:S(2)}) collective-permute-start(f32[8,1152]{1,0:T(8,128)S(1)} %constant_dynamic-slice_fusion), channel_id=1, source_target_pairs={{0,16},{1,17},{2,18},{3,19},{4,20},{5,21},{6,22},{7,23},{8,24},{9,... | collective-permute-start | bytes 110600 | tf_op jit(solution)/shard_map/ppermute | solution.py:688
  175.0 4.7 %collective-permute-start.20 = (f32[8,3072]{1,0:T(8,128)S(1)}, f32[8,3072]{1,0:T(8,128)S(1)}, u32[]{:S(2)}, u32[]{:S(2)}) collective-permute-start(f32[8,3072]{1,0:T(8,128)S(1)} %pad_maximum_fusion.1), channel_id=1, source_target_pairs={{0,2},{1,3},{2,0},{3,1},{4,6},{5,7},{6,4},{7,5},{8,10},{9,11},{10,... | collective-permute-start | bytes 294920 | tf_op jit(solution)/shard_map/ppermute | solution.py:813
  179.8 5.2 %collective-permute-start.21 = (bf16[8,3072]{1,0:T(8,128)(2,1)S(1)}, bf16[8,3072]{1,0:T(8,128)(2,1)S(1)}, u32[]{:S(2)}, u32[]{:S(2)}) collective-permute-start(bf16[8,3072]{1,0:T(8,128)(2,1)S(1)} %fusion.13), channel_id=1, source_target_pairs={{0,16},{1,17},{2,18},{3,19},{4,20},{5,21},{6,22},{7,23},{8,24},{9,... | collective-permute-start | bytes 147464 | tf_op jit(solution)/shard_map/ppermute | solution.py:695
  185.0 4.7 %collective-permute-start.22 = (bf16[16,3072]{1,0:T(8,128)(2,1)S(1)}, bf16[16,3072]{1,0:T(8,128)(2,1)S(1)}, u32[]{:S(2)}, u32[]{:S(2)}) collective-permute-start(bf16[16,3072]{1,0:T(8,128)(2,1)S(1)} %maximum_select_fusion.4), channel_id=1, source_target_pairs={{0,8},{1,9},{2,10},{3,11},{4,12},{5,13},{6,14},{7,15},{8,0},{9,1},... | collective-permute-start | bytes 294920 | tf_op jit(solution)/shard_map/ppermute | solution.py:695
  189.7 5.7 %collective-permute-start.23 = (bf16[32,3072]{1,0:T(8,128)(2,1)S(1)}, bf16[32,3072]{1,0:T(8,128)(2,1)S(1)}, u32[]{:S(2)}, u32[]{:S(2)}) collective-permute-start(bf16[32,3072]{1,0:T(8,128)(2,1)S(1)} %maximum_select_fusion.2), channel_id=1, source_target_pairs={{0,4},{1,5},{2,6},{3,7},{4,0},{5,1},{6,2},{7,3},{8,12},{9,13},{10,... | collective-permute-start | bytes 589832 | tf_op jit(solution)/shard_map/ppermute | solution.py:695
  195.5 1.8 collective-permute-start.24

commit v4 on v3

--- a/solution.py
+++ b/solution.py
@@ -242,21 +242,20 @@
                 pairs[frame, at, :, lane : lane + chans] = seen
 
 
-def front_kernel(ids, *refs):
+def front_kernel(slots, ids, *refs):
     latents, cotangent = refs[0:2], refs[2:4]
-    w_in, w_back, act, back, slope, pad, pairs = refs[4:]
+    w_in, w_back, act, back, slope, leaving, pads, windows = refs[4:]
     at = pl.program_id(0)
-    core, shift_rows = ids[1], ids[7]
+    side, core, shift_rows = ids[0], ids[1], ids[7]
     spread, width, chans = latents[0].shape[1:]
     count = spread // 2 - 1
     lanes = 6 * chans
-    slots = pl.num_programs(0)
 
     @pl.when(at == 0)
     def _():
-        pad[...] = jnp.zeros(pad.shape, F32)
-
-    def conv(blocks, weights):
+        pads[...] = jnp.zeros(pads.shape, F32)
+
+    def conv(blocks, weights, pad, pairs):
         for index in range(2):
             for row in range(spread):
                 place = index * (spread + 2) + 1 + row
@@ -288,15 +287,33 @@
                 lane = row % 2 * chans
                 target[owner, 0, row] = values[index * count + row // 2, :, lane : lane + chans]
 
-    pre = conv(latents, w_in)
+    pre = conv(latents, w_in, pads.at[0], windows.at[0])
+    summed = conv(cotangent, w_back, pads.at[1], windows.at[1])
     sigma = jax.nn.sigmoid(pre)
     store(act, (pre * sigma).astype(BF))
     store(slope, (sigma * (1.0 + pre * (1.0 - sigma))).astype(BF))
-    summed = conv(cotangent, w_back)
     half = count * width
     mine = jnp.where(core * slots + at < ids[2], 1.0, 0.0).astype(F32)
     other = jnp.where((1 - core) * slots + at < ids[2], 1.0, 0.0).astype(F32)
     store(back, jnp.concatenate([summed[:half] * mine, summed[half:] * other], 0).astype(BF))
+
+    tail = leaving.shape[0] - slots
+
+    @pl.when(side == 0)
+    def _():
+        leaving[at + tail] = act[1, 0]
+
+    @pl.when((side == 0) & (at >= slots - tail))
+    def _():
+        leaving[at - (slots - tail)] = act[0, 0]
+
+    @pl.when(side == 1)
+    def _():
+        leaving[at] = back[0, 0]
+
+    @pl.when((side == 1) & (at < tail))
+    def _():
+        leaving[slots + at] = back[1, 0]
 
 
 def front(ids, latents, cotangent, w_in, w_back):
@@ -310,23 +327,27 @@
     target = pl.BlockSpec((2, 1, rows, width, chans), lambda i, ids: (0, i, 0, 0, 0))
     fixed = pl.BlockSpec(w_in.shape, lambda i, ids: (0, 0))
     made = pl.pallas_call(
-        front_kernel,
+        functools.partial(front_kernel, slots),
         grid_spec=pltpu.PrefetchScalarGridSpec(
             num_scalar_prefetch=1,
             grid=(slots,),
             in_specs=[own, got, own, got, fixed, fixed],
-            out_specs=[target] * 3,
+            out_specs=[
+                target, target, target,
+                pl.BlockSpec((REACH, rows, width, chans), lambda i, ids: (0, 0, 0, 0)),
+            ],
             scratch_shapes=[
-                pltpu.VMEM((2 * (spread + 2), width + 16, chans), F32),
-                pltpu.VMEM((spread, width, 6 * chans), BF),
+                pltpu.VMEM((2, 2 * (spread + 2), width + 16, chans), F32),
+                pltpu.VMEM((2, spread, width, 6 * chans), BF),
             ],
         ),
-        out_shape=[jax.ShapeDtypeStruct((2, slots, rows, width, chans), BF)] * 3,
+        out_shape=[jax.ShapeDtypeStruct((2, slots, rows, width, chans), BF)] * 3
+        + [jax.ShapeDtypeStruct((REACH, rows, width, chans), BF)],
         compiler_params=params(),
         cost_estimate=cost(22.0 / CHUNKS),
         name="front",
     )(ids, *latents, *cotangent, w_in, w_back)
-    return [value.reshape(2 * slots, rows, width, chans) for value in made]
+    return [value.reshape(-1, rows, width, chans) for value in made]
 
 
 def taps_of(held, start, step, count):
@@ -357,8 +378,6 @@
     @pl.when(at == 0)
     def _():
         blank = jnp.zeros((REACH,) + held_in.shape[1:], BF)
-        held_in[0:REACH] = blank
-        held_back[frames : frames + REACH] = blank
         held_mid[0:REACH] = blank
         held_mid[REACH + frames : 2 * REACH + frames] = blank
         grad_first[...] = jnp.zeros_like(grad_first)
@@ -367,13 +386,9 @@
     held_in[REACH : REACH + frames] = act_in[:, 0]
     held_back[0:frames] = act_back[:, 0]
 
-    @pl.when(side == 0)
-    def _():
-        held_back[frames : frames + REACH] = halo[:, 0]
-
-    @pl.when(side == 1)
-    def _():
-        held_in[0:REACH] = halo[:, 0]
+    one = side.astype(F32)
+    held_in[0:REACH] = (halo[:, 0].astype(F32) * one).astype(BF)
+    held_back[frames : frames + REACH] = (halo[:, 0].astype(F32) * (1.0 - one)).astype(BF)
 
     size, chans = held_in.shape[1:]
     taps_in = taps_of(held_in, REACH, -near, frames)
@@ -388,28 +403,16 @@
     act = act.reshape(frames, size, chans)
     grad = grad.reshape(frames, size, chans)
 
-    @pl.when(side == 0)
-    def _():
-        held_mid[REACH : REACH + frames] = act
-        mid_keep[:, 0] = grad
-        mid_send[:, 0] = act[frames - REACH :]
-
-    @pl.when(side == 1)
-    def _():
-        held_mid[REACH : REACH + frames] = grad
-        mid_keep[:, 0] = act
-        mid_send[:, 0] = grad[:REACH]
-
+    ours = jnp.where(side == 0, act, grad)
+    held_mid[REACH : REACH + frames] = ours
+    mid_keep[:, 0] = jnp.where(side == 0, grad, act)
+    mid_send[:, 0] = held_mid[pl.ds(REACH + (1 - side) * (frames - REACH), REACH)]
     step = jnp.where(side == 0, -far, near)
     first = jnp.dot(
         taps_of(held_mid, REACH, step, frames), w_first[...], preferred_element_type=F32
     )
-    result[...] = first.astype(BF).reshape(frames, size, chans)
-
-    @pl.when(side == 1)
-    def _():
-        result[...] = (result[...].astype(F32) * slope[:, 0].astype(F32)).astype(BF)
-
+    first = first.astype(BF).reshape(frames, size, chans).astype(F32)
+    result[...] = (first * (slope[:, 0].astype(F32) * one + (1.0 - one))).astype(BF)
     first_keep[:, 0] = result[pl.ds(mine, slots)]
     first_send[:, 0] = result[pl.ds(other, slots)]
 
@@ -453,63 +456,48 @@
 
 
 def second_kernel(ids, mid, slope, halo, w_second, keep, send, held, result):
-    at = pl.program_id(0)
     side, core, near, far = ids[0], ids[1], ids[3], ids[4]
-    frames = mid.shape[0]
+    frames, each = mid.shape[:2]
     slots = frames // 2
     mine = core * slots
-
-    @pl.when(at == 0)
-    def _():
-        blank = jnp.zeros((REACH,) + held.shape[1:], BF)
-        held[0:REACH] = blank
-        held[REACH + frames : 2 * REACH + frames] = blank
-
-    held[REACH : REACH + frames] = mid[:, 0]
-
-    @pl.when(side == 0)
-    def _():
-        held[REACH + frames : 2 * REACH + frames] = halo[:, 0]
-
-    @pl.when(side == 1)
-    def _():
-        held[0:REACH] = halo[:, 0]
-
+    size, chans = held.shape[2:]
+    one = side.astype(F32)
     step = jnp.where(side == 0, near, -far)
-    made = jnp.dot(
-        taps_of(held, REACH, step, frames), w_second[...], preferred_element_type=F32
-    )
-    result[...] = made.astype(BF).reshape(result.shape)
-
-    @pl.when(side == 0)
-    def _():
-        result[...] = (result[...].astype(F32) * slope[:, 0].astype(F32)).astype(BF)
-
-    keep[:, 0] = result[pl.ds(mine, slots)]
-    send[:, 0] = result[pl.ds(slots - mine, slots)]
+    for row in range(each):
+        held[row, 0:REACH] = (halo[:, row].astype(F32) * one).astype(BF)
+        held[row, REACH : REACH + frames] = mid[:, row]
+        held[row, REACH + frames :] = (halo[:, row].astype(F32) * (1.0 - one)).astype(BF)
+        made = jnp.dot(
+            taps_of(held.at[row], REACH, step, frames), w_second[...], preferred_element_type=F32
+        )
+        made = made.astype(BF).reshape(frames, size, chans).astype(F32)
+        result[row] = (made * (slope[:, row].astype(F32) * (1.0 - one) + one)).astype(BF)
+        keep[:, row] = result[row, pl.ds(mine, slots)]
+        send[:, row] = result[row, pl.ds(slots - mine, slots)]
 
 
 def second(ids, mid, slope, halo, w_second):
     frames, rows, width, chans = mid.shape
     slots = frames // 2
+    each = 2
 
     def rowwise(count):
-        return pl.BlockSpec((count, 1, width, chans), lambda i, ids: (0, i, 0, 0))
+        return pl.BlockSpec((count, each, width, chans), lambda i, ids: (0, i, 0, 0))
 
     shape = jax.ShapeDtypeStruct((slots, rows, width, chans), BF)
     return pl.pallas_call(
         second_kernel,
         grid_spec=pltpu.PrefetchScalarGridSpec(
             num_scalar_prefetch=1,
-            grid=(rows,),
+            grid=(rows // each,),
             in_specs=[
                 rowwise(frames), rowwise(frames), rowwise(REACH),
                 pl.BlockSpec(w_second.shape, lambda i, ids: (0, 0)),
             ],
             out_specs=[rowwise(slots), rowwise(slots)],
             scratch_shapes=[
-                pltpu.VMEM((2 * REACH + frames, width, chans), BF),
-                pltpu.VMEM((frames, width, chans), BF),
+                pltpu.VMEM((each, 2 * REACH + frames, width, chans), BF),
+                pltpu.VMEM((each, frames, width, chans), BF),
             ],
         ),
         out_shape=[shape, shape],
@@ -756,11 +744,10 @@
         start = chunk * 2 * band + core * band - 1
         kept = jnp.clip(start, 0, rows - band - 2)
         front_ids = jnp.concatenate([ids, jnp.stack([kept, start - kept]).astype(jnp.int32)])
-        act, back, slope = front(
+        act, back, slope, leaving = front(
             front_ids, [latents, got[0]], [cotangent, got[1]], w_in, w_out_back
         )
         slopes.append(slope)
-        leaving = jnp.where(at_zero, act[2 * slots - REACH :], back[:REACH])
         if chunk > 0:
             leaving = after(leaving, halo)
         halo = lax.ppermute(leaving, "tm", swap_sides)

time: 202 us -> 197 us (0.975)
  other arithmetic: 12.5 us -> 7.18 us
  waiting for transfers between devices: 37.6 us -> 41.7 us
  Pallas kernels: 102 us -> 98.6 us
    select_n x2 -> x0, other arithmetic: 5.33 us -> none  [on_chip_pair(): leaving = jnp.where(at_zero, act[2 * slots - REACH:], back[:REACH])]
    ppermute x2, waiting for transfers between devices: 4.61 us -> 7.35 us  [on_chip_pair(): halo = lax.ppermute(leaving, 'tm', swap_sides)]
    pallas_call x2, Pallas kernels: 23.3 us -> 21.2 us  [middle(): pl.pallas_call(middle_kernel, grid_spec=pltpu.PrefetchScalarGridSpec(num_...]
  transfers between devices with their start and end apart: 25 -> 25, of which waited for: 16 -> 16; matrix products, arithmetic and copies ran while one was open for 10% -> 7% of each run, Pallas kernels for 44% -> 44%
where the time goes in v4:
time: 197 us; the launch traced here: 196 us
  Pallas kernels  98.6 us (50%)
  waiting for transfers between devices  41.7 us (21%)
  starting transfers between devices  25 us (13%)
  local copies, waits for them, and re-layouts  22.1 us (11%)
  other arithmetic  7.18 us (4%)
    pallas_call x4, Pallas kernels, ending(): pl.pallas_call(functools.partial(ending_kernel, chunk, rows, factor, outs...  41.8 us
    pallas_call x2, Pallas kernels, front(): pl.pallas_call(functools.partial(front_kernel, slots), grid_spec=pltpu.Pr...  24.9 us
    pallas_call x2, Pallas kernels, middle(): pl.pallas_call(middle_kernel, grid_spec=pltpu.PrefetchScalarGridSpec(num_...  21.2 us
    ppermute x4, waiting for transfers between devices, double(): other = lax.ppermute(values, ('dp', 'tm'), pairs[digit])  12.5 us
    ppermute x8, starting transfers between devices, halve(): values = keep + lax.ppermute(send, ('dp', 'tm'), pairs[digit])  11 us
    pallas_call x2, Pallas kernels, second(): pl.pallas_call(second_kernel, grid_spec=pltpu.PrefetchScalarGridSpec(num_...  10.8 us
    unnamed x39, local copies, waits for them, and re-layouts  8.93 us
    ppermute x8, waiting for transfers between devices, halve(): values = keep + lax.ppermute(send, ('dp', 'tm'), pairs[digit])  8.37 us
  transfers between devices with their start and end apart: 25, of which 16 were waited for; matrix products, arithmetic and copies ran while one was open for 7% of the time, Pallas kernels for 44%

profile of v4, /device:TPU:0, one launch (start us, length us, event | category | flops | bytes accessed | tf_op | source)
XLA Modules:
  0.0 196.4 jit_solution(17764567674908730416)
XLA Ops:
  0.7 3.5 %dynamic-slice_bitcast_fusion.1 = (bf16[6,6,128,128]{3,2,1,0:T(8,128)(2,1)}, bf16[6,6,128,128]{3,2,1,0:T(8,128)(2,1)}) fusion(bf16[1,6,16,128,128]{4,3,2,1,0:T(8,128)(2,1)} %param.8, s32[]{:T(128)S(6)} %min.18, s32[]{:T(128)S(6)} %min.16), kind=kLoop, calls=%fused_computation.11 | loop fusion | bytes 4718600 | tf_op jit(solution)/shard_map/dynamic_slice | solution.py:738
  4.7 1.6 dynamic-slice_bitcast_fusion
  7.8 1.3 fusion.8
  9.3 1.0 copy-done.3
  10.3 12.7 %front.2 = (bf16[2,6,4,128,128]{4,3,2,1,0:T(8,128)(2,1)}, bf16[2,6,4,128,128]{4,3,2,1,0:T(8,128)(2,1)}, bf16[2,6,4,128,128]{4,3,2,1,0:T(8,128)(2,1)}, bf16[8,4,128,128]{3,2,1,0:T(8,128)(2,1)}) custom-call(s32[8]{0:T(128)} %concatenate.56.ids, bf16[6,16,128,128]{3,2,1,0:T(8,128)(2,1)} %bitcast.56, bf16[6,6,128,128]{3,2,1,0:T(8,128)(2,1)} %collective-permute-done.refs_1_, ...), custom_call_target="tpu_custom_call" | custom-call | flops 220000000 | bytes 1000 | tf_op jit(solution)/shard_map/front/pallas_call | solution.py:329
  23.6 2.8 %collective-permute-start.2 = (bf16[8,4,128,128]{3,2,1,0:T(8,128)(2,1)}, bf16[8,4,128,128]{3,2,1,0:T(8,128)(2,1)}, u32[]{:S(2)}, u32[]{:S(2)}) collective-permute-start(bf16[8,4,128,128]{3,2,1,0:T(8,128)(2,1)} %get-tuple-element.52), channel_id=1, source_target_pairs={{0,2},{2,0},{1,3},{3,1},{4,6},{6,4},{5,7},{7,5},{8,10},{10,8},{9,1... | collective-permute-start | bytes 3145736 | tf_op jit(solution)/shard_map/ppermute | solution.py:753
  28.6 1.1 copy-done.4
  29.6 1.0 copy-done.5
  30.7 12.1 %front.3 = (bf16[2,6,4,128,128]{4,3,2,1,0:T(8,128)(2,1)}, bf16[2,6,4,128,128]{4,3,2,1,0:T(8,128)(2,1)}, bf16[2,6,4,128,128]{4,3,2,1,0:T(8,128)(2,1)}, bf16[8,4,128,128]{3,2,1,0:T(8,128)(2,1)}) custom-call(s32[8]{0:T(128)} %concatenate.59.ids, bf16[6,16,128,128]{3,2,1,0:T(8,128)(2,1)} %bitcast.57, bf16[6,6,128,128]{3,2,1,0:T(8,128)(2,1)} %copy-done.4, ...), custom_call_target="tpu_custom_call" | custom-call | flops 220000000 | bytes 1000 | tf_op jit(solution)/shard_map/front/pallas_call | solution.py:329
  42.8 7.3 %collective-permute-done.2.halo = bf16[8,4,128,128]{3,2,1,0:T(8,128)(2,1)} collective-permute-done((bf16[8,4,128,128]{3,2,1,0:T(8,128)(2,1)}, bf16[8,4,128,128]{3,2,1,0:T(8,128)(2,1)}, u32[]{:S(2)}, u32[]{:S(2)}) %collective-permute-start.2) | collective-permute-done | bytes 1048608 | tf_op jit(solution)/shard_map/ppermute | solution.py:753
  50.1 1.7 collective-permute-start.5
  52.6 10.6 %middle.2 = (bf16[8,4,128,128]{3,2,1,0:T(8,128)(2,1)}, bf16[12,4,128,128]{3,2,1,0:T(8,128)(2,1)}, bf16[6,4,128,128]{3,2,1,0:T(8,128)(2,1)}, bf16[6,4,128,128]{3,...) custom-call(s32[6]{0:T(128)} %stack.39.ids, bf16[12,4,128,128]{3,2,1,0:T(8,128)(2,1)} %bitcast.75, ...), custom_call_target="tpu_custom_call" | custom-call | flops 240000000 | bytes 1000 | tf_op jit(solution)/shard_map/middle/pallas_call | solution.py:433
  63.5 1.4 broadcast_select_fusion
  66.9 8.6 %ending.4 = (bf16[6,16,128,128]{3,2,1,0:T(8,128)(2,1)}, bf16[6,16,128,128]{3,2,1,0:T(8,128)(2,1)}, f32[128,1152]{1,0:T(8,128)}) custom-call(s32[6]{0:T(128)} %stack.39.ids, bf16[6,4,128,128]{3,2,1,0:T(8,128)(2,1)} %get-tuple-element.59.refs_0_, bf16[6,4,128,128]{3,2,1,0:T(8,128)(2,1)} %copy-done.2, bf16[6,16,128,128]{3,2,1,0:T(8,128)(2,1)} %bitcast.58, ...), custom_call_target="tpu_custom_call" | custom-call | flops 260000000 | bytes 1000 | tf_op jit(solution)/shard_map/ending/pallas_call | solution.py:615
  75.5 1.0 collective-permute-start.7
  76.5 10.6 %middle.3 = (bf16[8,4,128,128]{3,2,1,0:T(8,128)(2,1)}, bf16[12,4,128,128]{3,2,1,0:T(8,128)(2,1)}, bf16[6,4,128,128]{3,2,1,0:T(8,128)(2,1)}, bf16[6,4,128,128]{3,...) custom-call(s32[6]{0:T(128)} %stack.39.ids, bf16[12,4,128,128]{3,2,1,0:T(8,128)(2,1)} %bitcast.77, ...), custom_call_target="tpu_custom_call" | custom-call | flops 240000000 | bytes 1000 | tf_op jit(solution)/shard_map/middle/pallas_call | solution.py:433
  87.2 2.5 %collective-permute-done.8.refs_3_ = bf16[6,4,128,128]{3,2,1,0:T(8,128)(2,1)S(1)} collective-permute-done((bf16[6,4,128,128]{3,2,1,0:T(8,128)(2,1)}, bf16[6,4,128,128]{3,2,1,0:T(8,128)(2,1)S(1)}, u32[]{:S(2)}, u32[]{:S(2)}) %collective-permute-start.8) | collective-permute-done | bytes 786464 | tf_op jit(solution)/shard_map/ppermute | solution.py:763
  90.6 12.4 %ending.5 = (bf16[6,16,128,128]{3,2,1,0:T(8,128)(2,1)}, bf16[6,16,128,128]{3,2,1,0:T(8,128)(2,1)}, f32[128,1152]{1,0:T(8,128)}) custom-call(s32[6]{0:T(128)} %stack.39.ids, bf16[6,4,128,128]{3,2,1,0:T(8,128)(2,1)} %get-tuple-element.59.refs_0_, bf16[6,4,128,128]{3,2,1,0:T(8,128)(2,1)} %get-tuple-element.69.refs_1_, ...), custom_call_target="tpu_custom_call", output_to_operand_aliasing={{0}: (9, {}), {1}: (10, {})} | custom-call | flops 260000000 | bytes 1000 | tf_op jit(solution)/shard_map/ending/pallas_call | solution.py:615
  103.0 1.2 collective-permute-start.9
  104.8 5.4 %second.2 = (bf16[6,4,128,128]{3,2,1,0:T(8,128)(2,1)}, bf16[6,4,128,128]{3,2,1,0:T(8,128)(2,1)}) custom-call(s32[6]{0:T(128)} %stack.38.ids, bf16[12,4,128,128]{3,2,1,0:T(8,128)(2,1)} %get-tuple-element.53.mid, bf16[12,4,128,128]{3,2,1,0:T(8,128)(2,1)} %bitcast.73, bf16[8,4,128,128]{3,2,1,0:T(8,128)(2,1)} %copy-done.9, bf16[384,128]{1,0:T(8,128)(2,1)} %bitcast.87), custom_call_target="tpu_custom_call" | custom-call | flops 100000000 | bytes 1000 | tf_op jit(solution)/shard_map/second/pallas_call | solution.py:488
  110.3 1.1 add_multiply_fusion
  111.4 1.0 add_multiply_fusion.1
  113.7 8.5 %ending.6 = (bf16[6,16,128,128]{3,2,1,0:T(8,128)(2,1)}, bf16[6,16,128,128]{3,2,1,0:T(8,128)(2,1)}, f32[128,1152]{1,0:T(8,128)}) custom-call(s32[6]{0:T(128)} %stack.38.ids, bf16[6,4,128,128]{3,2,1,0:T(8,128)(2,1)} %get-tuple-element.63.refs_0_, bf16[6,4,128,128]{3,2,1,0:T(8,128)(2,1)} %copy-done.1, ...), custom_call_target="tpu_custom_call", output_to_operand_aliasing={{0}: (7, {}), {1}: (8, {})} | custom-call | flops 260000000 | bytes 1000 | tf_op jit(solution)/shard_map/ending/pallas_call | solution.py:615
  122.2 6.3 %collective-permute-done.9.halo = bf16[8,4,128,128]{3,2,1,0:T(8,128)(2,1)S(1)} collective-permute-done((bf16[8,4,128,128]{3,2,1,0:T(8,128)(2,1)}, bf16[8,4,128,128]{3,2,1,0:T(8,128)(2,1)S(1)}, u32[]{:S(2)}, u32[]{:S(2)}) %collective-permute-start.9) | collective-permute-done | bytes 1048608 | tf_op jit(solution)/shard_map/ppermute | solution.py:767
  129.5 5.4 %second.3 = (bf16[6,4,128,128]{3,2,1,0:T(8,128)(2,1)}, bf16[6,4,128,128]{3,2,1,0:T(8,128)(2,1)}) custom-call(s32[6]{0:T(128)} %stack.38.ids, bf16[12,4,128,128]{3,2,1,0:T(8,128)(2,1)} %get-tuple-element.67.mid, bf16[12,4,128,128]{3,2,1,0:T(8,128)(2,1)} %bitcast.71, bf16[8,4,128,128]{3,2,1,0:T(8,128)(2,1)} %copy-done.8, bf16[384,128]{1,0:T(8,128)(2,1)} %bitcast.88), custom_call_target="tpu_custom_call" | custom-call | flops 100000000 | bytes 1000 | tf_op jit(solution)/shard_map/second/pallas_call | solution.py:488
  134.9 1.1 dynamic-slice_add_fusion
  136.0 1.6 collective-permute-start.13
  138.5 12.2 %ending.7 = (bf16[6,16,128,128]{3,2,1,0:T(8,128)(2,1)}, bf16[6,16,128,128]{3,2,1,0:T(8,128)(2,1)}, f32[128,1152]{1,0:T(8,128)}) custom-call(s32[6]{0:T(128)} %stack.38.ids, bf16[6,4,128,128]{3,2,1,0:T(8,128)(2,1)} %get-tuple-element.63.refs_0_, bf16[6,4,128,128]{3,2,1,0:T(8,128)(2,1)} %get-tuple-element.80.refs_1_, ...), custom_call_target="tpu_custom_call", output_to_operand_aliasing={{0}: (9, {}), {1}: (10, {})} | custom-call | flops 260000000 | bytes 1000 | tf_op jit(solution)/shard_map/ending/pallas_call | solution.py:615
  150.7 1.0 constant_dynamic-slice_fusion.3
  152.1 1.6 collective-permute-start.14
  153.8 1.3 collective-permute-start.17
  155.1 2.6 %collective-permute-done.14 = f32[16,1920]{1,0:T(8,128)S(1)} collective-permute-done((f32[16,1920]{1,0:T(8,128)S(1)}, f32[16,1920]{1,0:T(8,128)S(1)}, u32[]{:S(2)}, u32[]{:S(2)}) %collective-permute-start.14) | collective-permute-done | bytes 122912 | tf_op jit(solution)/shard_map/ppermute | solution.py:676
  157.7 1.9 collective-permute-done.17
  159.7 1.5 collective-permute-start.18
  161.2 2.6 %collective-permute-start.15 = (f32[8,1920]{1,0:T(8,128)S(1)}, f32[8,1920]{1,0:T(8,128)S(1)}, u32[]{:S(2)}, u32[]{:S(2)}) collective-permute-start(f32[8,1920]{1,0:T(8,128)S(1)} %constant_dynamic-slice_fusion.4), channel_id=1, source_target_pairs={{0,16},{1,17},{2,18},{3,19},{4,20},{5,21},{6,22},{7,23},{8,24},{9,... | collective-permute-start | bytes 184328 | tf_op jit(solution)/shard_map/ppermute | solution.py:676
  164.8 2.0 %collective-permute-start.19 = (f32[8,1152]{1,0:T(8,128)S(1)}, f32[8,1152]{1,0:T(8,128)S(1)}, u32[]{:S(2)}, u32[]{:S(2)}) collective-permute-start(f32[8,1152]{1,0:T(8,128)S(1)} %constant_dynamic-slice_fusion), channel_id=1, source_target_pairs={{0,16},{1,17},{2,18},{3,19},{4,20},{5,21},{6,22},{7,23},{8,24},{9,... | collective-permute-start | bytes 110600 | tf_op jit(solution)/shard_map/ppermute | solution.py:676
  167.6 2.1 %collective-permute-done.19 = f32[8,1152]{1,0:T(8,128)S(1)} collective-permute-done((f32[8,1152]{1,0:T(8,128)S(1)}, f32[8,1152]{1,0:T(8,128)S(1)}, u32[]{:S(2)}, u32[]{:S(2)}) %collective-permute-start.19) | collective-permute-done | bytes 36896 | tf_op jit(solution)/shard_map/ppermute | solution.py:676
  169.7 1.2 collective-permute-start.20
  170.9 3.5 %collective-permute-done.20 = f32[8,3072]{1,0:T(8,128)S(1)} collective-permute-done((f32[8,3072]{1,0:T(8,128)S(1)}, f32[8,3072]{1,0:T(8,128)S(1)}, u32[]{:S(2)}, u32[]{:S(2)}) %collective-permute-start.20) | collective-permute-done | bytes 98336 | tf_op jit(solution)/shard_map/ppermute | solution.py:800
  174.5 2.0 %collective-permute-start.21 = (bf16[8,3072]{1,0:T(8,128)(2,1)S(1)}, bf16[8,3072]{1,0:T(8,128)(2,1)S(1)}, u32[]{:S(2)}, u32[]{:S(2)}) collective-permute-start(bf16[8,3072]{1,0:T(8,128)(2,1)S(1)} %fusion.13), channel_id=1, source_target_pairs={{0,16},{1,17},{2,18},{3,19},{4,20},{5,21},{6,22},{7,23},{8,24},{9,... | collective-permute-start | bytes 147464 | tf_op jit(solution)/shard_map/ppermute | solution.py:683
  176.5 3.1 %collective-permute-done.21 = bf16[8,3072]{1,0:T(8,128)(2,1)S(1)} collective-permute-done((bf16[8,3072]{1,0:T(8,128)(2,1)S(1)}, bf16[8,3072]{1,0:T(8,128)(2,1)S(1)}, u32[]{:S(2)}, u32[]{:S(2)}) %collective-permute-start.21) | collective-permute-done | bytes 49184 | tf_op jit(solution)/shard_map/ppermute | solution.py:683
  179.7 1.4 collective-permute-start.22
  181.1 3.3 %collective-permute-done.22 = bf16[16,3072]{1,0:T(8,128)(2,1)S(1)} collective-permute-done((bf16[16,3072]{1,0:T(8,128)(2,1)S(1)}, bf16[16,3072]{1,0:T(8,128)(2,1)S(1)}, u32[]{:S(2)}, u32[]{:S(2)}) %collective-permute-start.22) | collective-permute-done | bytes 98336 | tf_op jit(solution)/shard_map/ppermute | solution.py:683
  184.4 1.4 collective-permute-start.23
  185.8 4.3 %collective-permute-done.23 = bf16[32,3072]{1,0:T(8,128)(2,1)S(1)} collective-permute-done((bf16[32,3072]{1,0:T(8,128)(2,1)S(1)}, bf16[32,3072]{1,0:T(8,128)(2,1)S(1)}, u32[]{:S(2)}, u32[]{:S(2)}) %collective-permute-start.23) | collective-permute-done | bytes 196640 | tf_op jit(solution)/shard_map/ppermute | solution.py:683
  190.3 1.7 collective-permute-done.24
  192.6 1.1 copy.36
  193.6 1.0 copy.33
  (103 shorter events, 16.7 us)
Async XLA Ops:
  0.7 4.0 %copy-start = (bf16[1,6,16,128,128]{4,3,2,1,0:T(8,128)(2,1)S(1)}, bf16[1,6,16,128,128]{4,3,2,1,0:T(8,128)(2,1)}, u32[]{:S(2)}) copy-start(bf16[1,6,16,128,128]{4,3,2,1,0:T(8,128)(2,1)} %param.9) | copy-start | bytes 9437188
  4.1 2.8 %copy-start.6 = (bf16[3,3,128,128]{3,2,1,0:T(8,128)(2,1)S(1)}, bf16[3,3,128,128]{3,2,1,0:T(8,128)(2,1)}, u32[]{:S(2)}) copy-start(bf16[3,3,128,128]{3,2,1,0:T(8,128)(2,1)} %param.11) | copy-start | bytes 884740
  4.1 3.1 %copy-start.16 = (s32[2]{0:T(128)S(1)}, s32[2]{0:T(128)}, u32[]{:S(2)}) copy-start(s32[2]{0:T(128)} %param.15) | copy-start | bytes 28
  4.1 3.7 %copy-start.7 = (bf16[3,3,128,128]{3,2,1,0:T(8,128)(2,1)S(1)}, bf16[3,3,128,128]{3,2,1,0:T(8,128)(2,1)}, u32[]{:S(2)}) copy-start(bf16[3,3,128,128]{3,2,1,0:T(8,128)(2,1)} %param.10) | copy-start | bytes 884740
  4.2 5.0 %collective-permute-start = (bf16[6,6,128,128]{3,2,1,0:T(8,128)(2,1)}, bf16[6,6,128,128]{3,2,1,0:T(8,128)(2,1)}, u32[]{:S(2)}, u32[]{:S(2)}) collective-permute-start(bf16[6,6,128,128]{3,2,1,0:T(8,128)(2,1)} %get-tuple-element.101), channel_id=1, source_target_pairs={{0,1},{1,0},{2,3},{3,2},{4,5},{5,4},{6,7},{7,6},{8,9},{9,8},{10,11... | collective-permute-start | bytes 3538952 | tf_op jit(solution)/shard_map/ppermute | solution.py:743
  6.2 3.1 %collective-permute-start.1 = (bf16[6,6,128,128]{3,2,1,0:T(8,128)(2,1)}, bf16[6,6,128,128]{3,2,1,0:T(8,128)(2,1)S(1)}, u32[]{:S(2)}, u32[]{:S(2)}) collective-permute-start(bf16[6,6,128,128]{3,2,1,0:T(8,128)(2,1)} %get-tuple-element.99), channel_id=1, source_target_pairs={{0,1},{1,0},{2,3},{3,2},{4,5},{5,4},{6,7},{7,6},{8,9},{9,8},{10,11... | collective-permute-start | bytes 3538952 | tf_op jit(solution)/shard_map/ppermute | solution.py:743
  9.3 1.0 copy-start.3
  10.3 16.7 %copy-start.15 = (bf16[3,128,128]{2,1,0:T(8,128)(2,1)S(1)}, bf16[3,128,128]{2,1,0:T(8,128)(2,1)}, u32[]{:S(2)}) copy-start(bf16[3,128,128]{2,1,0:T(8,128)(2,1)} %param.13) | copy-start | bytes 294916
  10.3 17.5 %copy-start.10 = (bf16[3,128,128]{2,1,0:T(8,128)(2,1)S(1)}, bf16[3,128,128]{2,1,0:T(8,128)(2,1)}, u32[]{:S(2)}) copy-start(bf16[3,128,128]{2,1,0:T(8,128)(2,1)} %param.12) | copy-start | bytes 294916
  23.1 5.5 %collective-permute-start.3 = (bf16[6,6,128,128]{3,2,1,0:T(8,128)(2,1)}, bf16[6,6,128,128]{3,2,1,0:T(8,128)(2,1)S(1)}, u32[]{:S(2)}, u32[]{:S(2)}) collective-permute-start(bf16[6,6,128,128]{3,2,1,0:T(8,128)(2,1)} %get-tuple-element.55), channel_id=1, source_target_pairs={{0,1},{1,0},{2,3},{3,2},{4,5},{5,4},{6,7},{7,6},{8,9},{9,8},{10,11... | collective-permute-start | bytes 3538952 | tf_op jit(solution)/shard_map/ppermute | solution.py:743
  23.1 5.4 %collective-permute-start.4 = (bf16[6,6,128,128]{3,2,1,0:T(8,128)(2,1)}, bf16[6,6,128,128]{3,2,1,0:T(8,128)(2,1)S(1)}, u32[]{:S(2)}, u32[]{:S(2)}) collective-permute-start(bf16[6,6,128,128]{3,2,1,0:T(8,128)(2,1)} %get-tuple-element.56), channel_id=1, source_target_pairs={{0,1},{1,0},{2,3},{3,2},{4,5},{5,4},{6,7},{7,6},{8,9},{9,8},{10,11... | collective-permute-start | bytes 3538952 | tf_op jit(solution)/shard_map/ppermute | solution.py:743
  23.6 26.5 %collective-permute-start.2 = (bf16[8,4,128,128]{3,2,1,0:T(8,128)(2,1)}, bf16[8,4,128,128]{3,2,1,0:T(8,128)(2,1)}, u32[]{:S(2)}, u32[]{:S(2)}) collective-permute-start(bf16[8,4,128,128]{3,2,1,0:T(8,128)(2,1)} %get-tuple-element.52), channel_id=1, source_target_pairs={{0,2},{2,0},{1,3},{3,1},{4,6},{6,4},{5,7},{7,5},{8,10},{10,8},{9,1... | collective-permute-start | bytes 3145736 | tf_op jit(solution)/shard_map/ppermute | solution.py:753
  28.6 1.1 copy-start.4
  29.6 1.0 copy-start.5
  50.1 25.4 %collective-permute-start.5 = (bf16[8,4,128,128]{3,2,1,0:T(8,128)(2,1)}, bf16[8,4,128,128]{3,2,1,0:T(8,128)(2,1)}, u32[]{:S(2)}, u32[]{:S(2)}) collective-permute-start(bf16[8,4,128,128]{3,2,1,0:T(8,128)(2,1)} %get-tuple-element.58), channel_id=1, source_target_pairs={{0,2},{2,0},{1,3},{3,1},{4,6},{6,4},{5,7},{7,5},{8,10},{10,8},{9,1... | collective-permute-start | bytes 3145736 | tf_op jit(solution)/shard_map/ppermute | solution.py:753
  63.2 2.6 %collective-permute-start.6 = (bf16[6,4,128,128]{3,2,1,0:T(8,128)(2,1)}, bf16[6,4,128,128]{3,2,1,0:T(8,128)(2,1)S(1)}, u32[]{:S(2)}, u32[]{:S(2)}) collective-permute-start(bf16[6,4,128,128]{3,2,1,0:T(8,128)(2,1)} %get-tuple-element.60), channel_id=1, source_target_pairs={{0,1},{1,0},{2,3},{3,2},{4,5},{5,4},{6,7},{7,6},{8,9},{9,8},{10,11... | collective-permute-start | bytes 2359304 | tf_op jit(solution)/shard_map/ppermute | solution.py:763
  65.7 1.1 copy-start.2
  66.8 8.7 %copy-start.17 = (bf16[8,4,128,128]{3,2,1,0:T(8,128)(2,1)S(1)}, bf16[8,4,128,128]{3,2,1,0:T(8,128)(2,1)}, u32[]{:S(2)}) copy-start(bf16[8,4,128,128]{3,2,1,0:T(8,128)(2,1)} %get-tuple-element.62) | copy-start | bytes 3145732
  75.5 27.5 %collective-permute-start.7 = (bf16[8,4,128,128]{3,2,1,0:T(8,128)(2,1)S(1)}, bf16[8,4,128,128]{3,2,1,0:T(8,128)(2,1)S(1)}, u32[]{:S(2)}, u32[]{:S(2)}) collective-permute-start(bf16[8,4,128,128]{3,2,1,0:T(8,128)(2,1)S(1)} %copy-done.17), channel_id=1, source_target_pairs={{0,2},{2,0},{1,3},{3,1},{4,6},{6,4},{5,7},{7,5},{8,10},{10,8},{9,1... | collective-permute-start | bytes 3145736 | tf_op jit(solution)/shard_map/ppermute | solution.py:767
  87.1 2.6 %collective-permute-start.8 = (bf16[6,4,128,128]{3,2,1,0:T(8,128)(2,1)}, bf16[6,4,128,128]{3,2,1,0:T(8,128)(2,1)S(1)}, u32[]{:S(2)}, u32[]{:S(2)}) collective-permute-start(bf16[6,4,128,128]{3,2,1,0:T(8,128)(2,1)} %get-tuple-element.70), channel_id=1, source_target_pairs={{0,1},{1,0},{2,3},{3,2},{4,5},{5,4},{6,7},{7,6},{8,9},{9,8},{10,11... | collective-permute-start | bytes 2359304 | tf_op jit(solution)/shard_map/ppermute | solution.py:763
  89.7 0.9 copy-start.12
  103.0 1.8 copy-start.9
  103.0 25.5 %collective-permute-start.9 = (bf16[8,4,128,128]{3,2,1,0:T(8,128)(2,1)}, bf16[8,4,128,128]{3,2,1,0:T(8,128)(2,1)S(1)}, u32[]{:S(2)}, u32[]{:S(2)}) collective-permute-start(bf16[8,4,128,128]{3,2,1,0:T(8,128)(2,1)} %get-tuple-element.74), channel_id=1, source_target_pairs={{0,2},{2,0},{1,3},{3,1},{4,6},{6,4},{5,7},{7,5},{8,10},{10,8},{9,1... | collective-permute-start | bytes 3145736 | tf_op jit(solution)/shard_map/ppermute | solution.py:767
  110.2 2.2 %copy-start.14 = (f32[128,1152]{1,0:T(8,128)S(1)}, f32[128,1152]{1,0:T(8,128)}, u32[]{:S(2)}) copy-start(f32[128,1152]{1,0:T(8,128)} %get-tuple-element.73) | copy-start | bytes 1769476
  110.2 2.5 %collective-permute-start.10 = (bf16[6,4,128,128]{3,2,1,0:T(8,128)(2,1)}, bf16[6,4,128,128]{3,2,1,0:T(8,128)(2,1)S(1)}, u32[]{:S(2)}, u32[]{:S(2)}) collective-permute-start(bf16[6,4,128,128]{3,2,1,0:T(8,128)(2,1)} %get-tuple-element.75), channel_id=1, source_target_pairs={{0,1},{1,0},{2,3},{3,2},{4,5},{5,4},{6,7},{7,6},{8,9},{9,8},{10,11... | collective-permute-start | bytes 2359304 | tf_op jit(solution)/shard_map/ppermute | solution.py:780
  112.7 0.9 copy-start.1
  128.5 1.0 copy-start.8
  128.5 6.3 %collective-permute-start.12 = (f32[64,1920]{1,0:T(8,128)S(1)}, f32[64,1920]{1,0:T(8,128)}, u32[]{:S(2)}, u32[]{:S(2)}) collective-permute-start(f32[64,1920]{1,0:T(8,128)S(1)} %constant_dynamic-slice_fusion.7), channel_id=1, source_target_pairs={{0,1},{1,0},{2,3},{3,2},{4,5},{5,4},{6,7},{7,6},{8,9},{9,8},{10,11... | collective-permute-start | bytes 1474568 | tf_op jit(solution)/shard_map/ppermute | solution.py:676
  134.9 2.7 %collective-permute-start.11 = (bf16[6,4,128,128]{3,2,1,0:T(8,128)(2,1)}, bf16[6,4,128,128]{3,2,1,0:T(8,128)(2,1)S(1)}, u32[]{:S(2)}, u32[]{:S(2)}) collective-permute-start(bf16[6,4,128,128]{3,2,1,0:T(8,128)(2,1)} %get-tuple-element.81), channel_id=1, source_target_pairs={{0,1},{1,0},{2,3},{3,2},{4,5},{5,4},{6,7},{7,6},{8,9},{9,8},{10,11... | collective-permute-start | bytes 2359304 | tf_op jit(solution)/shard_map/ppermute | solution.py:780
  136.0 16.0 %collective-permute-start.13 = (f32[32,1920]{1,0:T(8,128)S(1)}, f32[32,1920]{1,0:T(8,128)S(1)}, u32[]{:S(2)}, u32[]{:S(2)}) collective-permute-start(f32[32,1920]{1,0:T(8,128)S(1)} %constant_dynamic-slice_fusion.6), channel_id=1, source_target_pairs={{0,4},{1,5},{2,6},{3,7},{4,0},{5,1},{6,2},{7,3},{8,12},{9,13},{10,... | collective-permute-start | bytes 737288 | tf_op jit(solution)/shard_map/ppermute | solution.py:676
  137.6 0.9 copy-start.11
  150.7 3.1 %copy-start.13 = (f32[128,1152]{1,0:T(8,128)S(1)}, f32[128,1152]{1,0:T(8,128)}, u32[]{:S(2)}) copy-start(f32[128,1152]{1,0:T(8,128)} %get-tuple-element.91) | copy-start | bytes 1769476
  151.8 2.0 %collective-permute-start.16 = (f32[64,1152]{1,0:T(8,128)S(1)}, f32[64,1152]{1,0:T(8,128)S(1)}, u32[]{:S(2)}, u32[]{:S(2)}) collective-permute-start(f32[64,1152]{1,0:T(8,128)S(1)} %constant_dynamic-slice_fusion.3), channel_id=1, source_target_pairs={{0,1},{1,0},{2,3},{3,2},{4,5},{5,4},{6,7},{7,6},{8,9},{9,8},{10,11... | collective-permute-start | bytes 884744 | tf_op jit(solution)/shard_map/ppermute | solution.py:676
  152.1 5.6 %collective-permute-start.14 = (f32[16,1920]{1,0:T(8,128)S(1)}, f32[16,1920]{1,0:T(8,128)S(1)}, u32[]{:S(2)}, u32[]{:S(2)}) collective-permute-start(f32[16,1920]{1,0:T(8,128)S(1)} %constant_dynamic-slice_fusion.5), channel_id=1, source_target_pairs={{0,8},{1,9},{2,10},{3,11},{4,12},{5,13},{6,14},{7,15},{8,0},{9,1},... | collective-permute-start | bytes 368648 | tf_op jit(solution)/shard_map/ppermute | solution.py:676
  153.8 5.8 %collective-permute-start.17 = (f32[32,1152]{1,0:T(8,128)S(1)}, f32[32,1152]{1,0:T(8,128)S(1)}, u32[]{:S(2)}, u32[]{:S(2)}) collective-permute-start(f32[32,1152]{1,0:T(8,128)S(1)} %constant_dynamic-slice_fusion.2), channel_id=1, source_target_pairs={{0,4},{1,5},{2,6},{3,7},{4,0},{5,1},{6,2},{7,3},{8,12},{9,13},{10,... | collective-permute-start | bytes 442376 | tf_op jit(solution)/shard_map/ppermute | solution.py:676
  159.7 5.0 %collective-permute-start.18 = (f32[16,1152]{1,0:T(8,128)S(1)}, f32[16,1152]{1,0:T(8,128)S(1)}, u32[]{:S(2)}, u32[]{:S(2)}) collective-permute-start(f32[16,1152]{1,0:T(8,128)S(1)} %constant_dynamic-slice_fusion.1), channel_id=1, source_target_pairs={{0,8},{1,9},{2,10},{3,11},{4,12},{5,13},{6,14},{7,15},{8,0},{9,1},... | collective-permute-start | bytes 221192 | tf_op jit(solution)/shard_map/ppermute | solution.py:676
  161.2 6.4 %collective-permute-start.15 = (f32[8,1920]{1,0:T(8,128)S(1)}, f32[8,1920]{1,0:T(8,128)S(1)}, u32[]{:S(2)}, u32[]{:S(2)}) collective-permute-start(f32[8,1920]{1,0:T(8,128)S(1)} %constant_dynamic-slice_fusion.4), channel_id=1, source_target_pairs={{0,16},{1,17},{2,18},{3,19},{4,20},{5,21},{6,22},{7,23},{8,24},{9,... | collective-permute-start | bytes 184328 | tf_op jit(solution)/shard_map/ppermute | solution.py:676
  164.8 4.9 %collective-permute-start.19 = (f32[8,1152]{1,0:T(8,128)S(1)}, f32[8,1152]{1,0:T(8,128)S(1)}, u32[]{:S(2)}, u32[]{:S(2)}) collective-permute-start(f32[8,1152]{1,0:T(8,128)S(1)} %constant_dynamic-slice_fusion), channel_id=1, source_target_pairs={{0,16},{1,17},{2,18},{3,19},{4,20},{5,21},{6,22},{7,23},{8,24},{9,... | collective-permute-start | bytes 110600 | tf_op jit(solution)/shard_map/ppermute | solution.py:676
  169.7 4.7 %collective-permute-start.20 = (f32[8,3072]{1,0:T(8,128)S(1)}, f32[8,3072]{1,0:T(8,128)S(1)}, u32[]{:S(2)}, u32[]{:S(2)}) collective-permute-start(f32[8,3072]{1,0:T(8,128)S(1)} %pad_maximum_fusion.1), channel_id=1, source_target_pairs={{0,2},{1,3},{2,0},{3,1},{4,6},{5,7},{6,4},{7,5},{8,10},{9,11},{10,... | collective-permute-start | bytes 294920 | tf_op jit(solution)/shard_map/ppermute | solution.py:800
  174.5 5.2 %collective-permute-start.21 = (bf16[8,3072]{1,0:T(8,128)(2,1)S(1)}, bf16[8,3072]{1,0:T(8,128)(2,1)S(1)}, u32[]{:S(2)}, u32[]{:S(2)}) collective-permute-start(bf16[8,3072]{1,0:T(8,128)(2,1)S(1)} %fusion.13), channel_id=1, source_target_pairs={{0,16},{1,17},{2,18},{3,19},{4,20},{5,21},{6,22},{7,23},{8,24},{9,... | collective-permute-start | bytes 147464 | tf_op jit(solution)/shard_map/ppermute | solution.py:683
  179.7 4.7 %collective-permute-start.22 = (bf16[16,3072]{1,0:T(8,128)(2,1)S(1)}, bf16[16,3072]{1,0:T(8,128)(2,1)S(1)}, u32[]{:S(2)}, u32[]{:S(2)}) collective-permute-start(bf16[16,3072]{1,0:T(8,128)(2,1)S(1)} %maximum_select_fusion.4), channel_id=1, source_target_pairs={{0,8},{1,9},{2,10},{3,11},{4,12},{5,13},{6,14},{7,15},{8,0},{9,1},... | collective-permute-start | bytes 294920 | tf_op jit(solution)/shard_map/ppermute | solution.py:683
  184.4 5.7 %collective-permute-start.23 = (bf16[32,3072]{1,0:T(8,128)(2,1)S(1)}, bf16[32,3072]{1,0:T(8,128)(2,1)S(1)}, u32[]{:S(2)}, u32[]{:S(2)}) collective-permute-start(bf16[32,3072]{1,0:T(8,128)(2,1)S(1)} %maximum_select_fusion.2), channel_id=1, source_target_pairs={{0,4},{1,5},{2,6},{3,7},{4,0},{5,1},{6,2},{7,3},{8,12},{9,13},{10,... | collective-permute-start | bytes 589832 | tf_op jit(solution)/shard_map/ppermute | solution.py:683
  190.2 1.8 collective-permute-start.24

commit v5 on v4

--- a/solution.py
+++ b/solution.py
@@ -185,7 +185,7 @@
 
 REACH = (TAPS - 1) * DILATION_MAX
 CHUNKS = 2
-VMEM_LIMIT = 56 * 1024 * 1024
+VMEM_LIMIT = 52 * 1024 * 1024
 BF = jnp.bfloat16
 F32 = jnp.float32
 

time: 197 us -> 192 us (0.975)
  waiting for transfers between devices: 41.7 us -> 56.3 us
  Pallas kernels: 98.6 us -> 90.4 us
  local copies, waits for them, and re-layouts: 22.1 us -> 15.4 us
  other arithmetic: 7.18 us -> 4.34 us
    ppermute x2, waiting for transfers between devices: 7.35 us -> 13.6 us  [on_chip_pair(): halo = lax.ppermute(leaving, 'tm', swap_sides)]
    pallas_call x4, Pallas kernels: 41.8 us -> 36.9 us  [ending(): pl.pallas_call(functools.partial(ending_kernel, chunk, rows, factor, outs...]
    ppermute x2, waiting for transfers between devices: 6.31 us -> 9.69 us  [on_chip_pair(): halo = lax.ppermute(after(made[0], halo, sums_first), 'tm', swap_sides)]
    unnamed x39 -> x31, local copies, waits for them, and re-layouts: 8.93 us -> 6.17 us
    ppermute x2, waiting for transfers between devices: 0.23 us -> 2.48 us  [on_chip_pair(): got.append(lax.ppermute(leaving, 'tm', swap_cores))]
  transfers between devices with their start and end apart: 25 -> 25, of which waited for: 16 -> 18; matrix products, arithmetic and copies ran while one was open for 7% -> 4% of each run, Pallas kernels for 44% -> 41%
where the time goes in v5:
time: 192 us
  Pallas kernels  90.4 us (47%)
  waiting for transfers between devices  56.3 us (29%)
  starting transfers between devices  23.3 us (12%)
  local copies, waits for them, and re-layouts  15.4 us (8%)
  other arithmetic  4.34 us (2%)
    pallas_call x4, Pallas kernels, ending(): pl.pallas_call(functools.partial(ending_kernel, chunk, rows, factor, outs...  36.9 us
    pallas_call x2, Pallas kernels, front(): pl.pallas_call(functools.partial(front_kernel, slots), grid_spec=pltpu.Pr...  23.4 us
    pallas_call x2, Pallas kernels, middle(): pl.pallas_call(middle_kernel, grid_spec=pltpu.PrefetchScalarGridSpec(num_...  20.5 us
    ppermute x4, waiting for transfers between devices, double(): other = lax.ppermute(values, ('dp', 'tm'), pairs[digit])  13.7 us
    ppermute x2, waiting for transfers between devices, on_chip_pair(): halo = lax.ppermute(leaving, 'tm', swap_sides)  13.6 us
    ppermute x8, starting transfers between devices, halve(): values = keep + lax.ppermute(send, ('dp', 'tm'), pairs[digit])  10.6 us
    pallas_call x2, Pallas kernels, second(): pl.pallas_call(second_kernel, grid_spec=pltpu.PrefetchScalarGridSpec(num_...  9.69 us
    ppermute x2, waiting for transfers between devices, on_chip_pair(): halo = lax.ppermute(after(made[0], halo, sums_first), 'tm', swap_sides)  9.69 us
  transfers between devices with their start and end apart: 25, of which 18 were waited for; matrix products, arithmetic and copies ran while one was open for 4% of the time, Pallas kernels for 41%

profile of v5, /device:TPU:0, one launch (start us, length us, event | category | flops | bytes accessed | tf_op | source)
XLA Modules:
  0.0 191.5 jit_solution(5155547123290929339)
XLA Ops:
  0.7 3.5 %dynamic-slice_bitcast_fusion.1 = (bf16[6,6,128,128]{3,2,1,0:T(8,128)(2,1)}, bf16[6,6,128,128]{3,2,1,0:T(8,128)(2,1)}) fusion(bf16[1,6,16,128,128]{4,3,2,1,0:T(8,128)(2,1)} %param.8, s32[]{:T(128)S(6)} %min.18, s32[]{:T(128)S(6)} %min.16), kind=kLoop, calls=%fused_computation.11 | loop fusion | bytes 4718600 | tf_op jit(solution)/shard_map/dynamic_slice | solution.py:738
  4.7 1.6 dynamic-slice_bitcast_fusion
  7.0 0.9 copy.28
  8.0 1.2 fusion.8
  9.4 0.8 copy-done.5
  10.3 12.0 %front.2 = (bf16[2,6,4,128,128]{4,3,2,1,0:T(8,128)(2,1)}, bf16[2,6,4,128,128]{4,3,2,1,0:T(8,128)(2,1)}, bf16[2,6,4,128,128]{4,3,2,1,0:T(8,128)(2,1)}, bf16[8,4,128,128]{3,2,1,0:T(8,128)(2,1)}) custom-call(s32[8]{0:T(128)S(1)} %concatenate.56.ids, bf16[6,16,128,128]{3,2,1,0:T(8,128)(2,1)} %bitcast.64, bf16[6,6,128,128]{3,2,1,0:T(8,128)(2,1)} %copy-done.5, ...), custom_call_target="tpu_custom_call" | custom-call | flops 220000000 | bytes 1000 | tf_op jit(solution)/shard_map/front/pallas_call | solution.py:329
  22.8 2.9 %collective-permute-start.2 = (bf16[8,4,128,128]{3,2,1,0:T(8,128)(2,1)}, bf16[8,4,128,128]{3,2,1,0:T(8,128)(2,1)S(1)}, u32[]{:S(2)}, u32[]{:S(2)}) collective-permute-start(bf16[8,4,128,128]{3,2,1,0:T(8,128)(2,1)} %get-tuple-element.52), channel_id=1, source_target_pairs={{0,2},{2,0},{1,3},{3,1},{4,6},{6,4},{5,7},{7,5},{8,10},{10,8},{9,1... | collective-permute-start | bytes 3145736 | tf_op jit(solution)/shard_map/ppermute | solution.py:753
  27.2 11.5 %front.3 = (bf16[2,6,4,128,128]{4,3,2,1,0:T(8,128)(2,1)}, bf16[2,6,4,128,128]{4,3,2,1,0:T(8,128)(2,1)}, bf16[2,6,4,128,128]{4,3,2,1,0:T(8,128)(2,1)}, bf16[8,4,128,128]{3,2,1,0:T(8,128)(2,1)}) custom-call(s32[8]{0:T(128)S(1)} %concatenate.59.ids, bf16[6,16,128,128]{3,2,1,0:T(8,128)(2,1)} %bitcast.65, ...), custom_call_target="tpu_custom_call" | custom-call | flops 220000000 | bytes 1000 | tf_op jit(solution)/shard_map/front/pallas_call | solution.py:329
  38.6 10.7 %collective-permute-done.2.halo = bf16[8,4,128,128]{3,2,1,0:T(8,128)(2,1)S(1)} collective-permute-done((bf16[8,4,128,128]{3,2,1,0:T(8,128)(2,1)}, bf16[8,4,128,128]{3,2,1,0:T(8,128)(2,1)S(1)}, u32[]{:S(2)}, u32[]{:S(2)}) %collective-permute-start.2) | collective-permute-done | bytes 1048608 | tf_op jit(solution)/shard_map/ppermute | solution.py:753
  49.3 1.7 collective-permute-start.5
  51.1 10.3 %middle.2 = (bf16[8,4,128,128]{3,2,1,0:T(8,128)(2,1)}, bf16[12,4,128,128]{3,2,1,0:T(8,128)(2,1)}, bf16[6,4,128,128]{3,2,1,0:T(8,128)(2,1)S(1)}, bf16[6,4,128,128...) custom-call(s32[6]{0:T(128)S(1)} %stack.39.ids, bf16[12,4,128,128]{3,2,1,0:T(8,128)(2,1)} %bitcast.83, ...), custom_call_target="tpu_custom_call" | custom-call | flops 240000000 | bytes 1000 | tf_op jit(solution)/shard_map/middle/pallas_call | solution.py:433
  61.6 1.4 broadcast_select_fusion
  63.0 1.0 collective-permute-done.6.refs_1_.refs_2_
  64.1 7.3 %ending.4 = (bf16[6,16,128,128]{3,2,1,0:T(8,128)(2,1)}, bf16[6,16,128,128]{3,2,1,0:T(8,128)(2,1)}, f32[128,1152]{1,0:T(8,128)S(1)}) custom-call(s32[6]{0:T(128)S(1)} %stack.39.ids, bf16[6,4,128,128]{3,2,1,0:T(8,128)(2,1)S(1)} %get-tuple-element.59.refs_0_, bf16[6,4,128,128]{3,2,1,0:T(8,128)(2,1)} %collective-permute-done.6.refs_1_.refs_2_, ...), custom_call_target="tpu_custom_call" | custom-call | flops 260000000 | bytes 1000 | tf_op jit(solution)/shard_map/ending/pallas_call | solution.py:615
  71.4 2.9 %collective-permute-done.5.halo = bf16[8,4,128,128]{3,2,1,0:T(8,128)(2,1)} collective-permute-done((bf16[8,4,128,128]{3,2,1,0:T(8,128)(2,1)}, bf16[8,4,128,128]{3,2,1,0:T(8,128)(2,1)}, u32[]{:S(2)}, u32[]{:S(2)}) %collective-permute-start.5) | collective-permute-done | bytes 1048608 | tf_op jit(solution)/shard_map/ppermute | solution.py:753
  74.3 1.4 collective-permute-start.7
  75.7 10.2 %middle.3 = (bf16[8,4,128,128]{3,2,1,0:T(8,128)(2,1)}, bf16[12,4,128,128]{3,2,1,0:T(8,128)(2,1)}, bf16[6,4,128,128]{3,2,1,0:T(8,128)(2,1)S(1)}, bf16[6,4,128,128...) custom-call(s32[6]{0:T(128)S(1)} %stack.39.ids, bf16[12,4,128,128]{3,2,1,0:T(8,128)(2,1)} %bitcast.85, ...), custom_call_target="tpu_custom_call" | custom-call | flops 240000000 | bytes 1000 | tf_op jit(solution)/shard_map/middle/pallas_call | solution.py:433
  85.9 0.9 copy-done.2
  86.8 2.5 %collective-permute-done.8.refs_3_ = bf16[6,4,128,128]{3,2,1,0:T(8,128)(2,1)S(1)} collective-permute-done((bf16[6,4,128,128]{3,2,1,0:T(8,128)(2,1)}, bf16[6,4,128,128]{3,2,1,0:T(8,128)(2,1)S(1)}, u32[]{:S(2)}, u32[]{:S(2)}) %collective-permute-start.8) | collective-permute-done | bytes 786464 | tf_op jit(solution)/shard_map/ppermute | solution.py:763
  89.3 0.9 copy-done.9
  90.2 11.2 %ending.5 = (bf16[6,16,128,128]{3,2,1,0:T(8,128)(2,1)}, bf16[6,16,128,128]{3,2,1,0:T(8,128)(2,1)}, f32[128,1152]{1,0:T(8,128)S(1)}) custom-call(s32[6]{0:T(128)S(1)} %stack.39.ids, bf16[6,4,128,128]{3,2,1,0:T(8,128)(2,1)S(1)} %get-tuple-element.59.refs_0_, bf16[6,4,128,128]{3,2,1,0:T(8,128)(2,1)} %copy-done.2, ...), custom_call_target="tpu_custom_call", output_to_operand_aliasing={{0}: (9, {}), {1}: (10, {})} | custom-call | flops 260000000 | bytes 1000 | tf_op jit(solution)/shard_map/ending/pallas_call | solution.py:615
  102.2 5.2 %second.2 = (bf16[6,4,128,128]{3,2,1,0:T(8,128)(2,1)S(1)}, bf16[6,4,128,128]{3,2,1,0:T(8,128)(2,1)}) custom-call(s32[6]{0:T(128)S(1)} %stack.38.ids, bf16[12,4,128,128]{3,2,1,0:T(8,128)(2,1)} %get-tuple-element.53.mid, bf16[12,4,128,128]{3,2,1,0:T(8,128)(2,1)} %bitcast.81, bf16[8,4,128,128]{3,2,1,0:T(8,128)(2,1)} %collective-permute-done.7.halo, ...), custom_call_target="tpu_custom_call" | custom-call | flops 100000000 | bytes 1000 | tf_op jit(solution)/shard_map/second/pallas_call | solution.py:488
  107.6 2.5 %collective-permute-done.10.refs_1_.refs_2_ = bf16[6,4,128,128]{3,2,1,0:T(8,128)(2,1)} collective-permute-done((bf16[6,4,128,128]{3,2,1,0:T(8,128)(2,1)}, bf16[6,4,128,128]{3,2,1,0:T(8,128)(2,1)}, u32[]{:S(2)}, u32[]{:S(2)}) %collective-permute-start.10) | collective-permute-done | bytes 786464 | tf_op jit(solution)/shard_map/ppermute | solution.py:780
  110.0 7.3 %ending.6 = (bf16[6,16,128,128]{3,2,1,0:T(8,128)(2,1)}, bf16[6,16,128,128]{3,2,1,0:T(8,128)(2,1)}, f32[128,1152]{1,0:T(8,128)S(1)}) custom-call(s32[6]{0:T(128)S(1)} %stack.38.ids, bf16[6,4,128,128]{3,2,1,0:T(8,128)(2,1)S(1)} %get-tuple-element.63.refs_0_, ...), custom_call_target="tpu_custom_call", output_to_operand_aliasing={{0}: (7, {}), {1}: (8, {})} | custom-call | flops 260000000 | bytes 1000 | tf_op jit(solution)/shard_map/ending/pallas_call | solution.py:615
  117.3 9.7 %collective-permute-done.9.halo = bf16[8,4,128,128]{3,2,1,0:T(8,128)(2,1)} collective-permute-done((bf16[8,4,128,128]{3,2,1,0:T(8,128)(2,1)}, bf16[8,4,128,128]{3,2,1,0:T(8,128)(2,1)}, u32[]{:S(2)}, u32[]{:S(2)}) %collective-permute-start.9) | collective-permute-done | bytes 1048608 | tf_op jit(solution)/shard_map/ppermute | solution.py:767
  127.2 4.5 %second.3 = (bf16[6,4,128,128]{3,2,1,0:T(8,128)(2,1)S(1)}, bf16[6,4,128,128]{3,2,1,0:T(8,128)(2,1)S(1)}) custom-call(s32[6]{0:T(128)S(1)} %stack.38.ids, bf16[12,4,128,128]{3,2,1,0:T(8,128)(2,1)} %get-tuple-element.67.mid, bf16[12,4,128,128]{3,2,1,0:T(8,128)(2,1)} %bitcast.79, bf16[8,4,128,128]{3,2,1,0:T(8,128)(2,1)} %collective-permute-done.9.halo, ...), custom_call_target="tpu_custom_call" | custom-call | flops 100000000 | bytes 1000 | tf_op jit(solution)/shard_map/second/pallas_call | solution.py:488
  131.7 0.9 copy-done.1
  133.0 1.1 dynamic-slice_add_fusion
  134.2 1.6 collective-permute-start.13
  135.7 11.0 %ending.7 = (bf16[6,16,128,128]{3,2,1,0:T(8,128)(2,1)}, bf16[6,16,128,128]{3,2,1,0:T(8,128)(2,1)}, f32[128,1152]{1,0:T(8,128)S(1)}) custom-call(s32[6]{0:T(128)S(1)} %stack.38.ids, bf16[6,4,128,128]{3,2,1,0:T(8,128)(2,1)S(1)} %get-tuple-element.63.refs_0_, bf16[6,4,128,128]{3,2,1,0:T(8,128)(2,1)} %copy-done.1, ...), custom_call_target="tpu_custom_call", output_to_operand_aliasing={{0}: (9, {}), {1}: (10, {})} | custom-call | flops 260000000 | bytes 1000 | tf_op jit(solution)/shard_map/ending/pallas_call | solution.py:615
  147.0 1.6 collective-permute-start.14
  148.7 1.3 collective-permute-start.17
  149.9 2.8 %collective-permute-done.14 = f32[16,1920]{1,0:T(8,128)S(1)} collective-permute-done((f32[16,1920]{1,0:T(8,128)S(1)}, f32[16,1920]{1,0:T(8,128)S(1)}, u32[]{:S(2)}, u32[]{:S(2)}) %collective-permute-start.14) | collective-permute-done | bytes 122912 | tf_op jit(solution)/shard_map/ppermute | solution.py:676
  152.7 1.9 %collective-permute-done.17 = f32[32,1152]{1,0:T(8,128)S(1)} collective-permute-done((f32[32,1152]{1,0:T(8,128)S(1)}, f32[32,1152]{1,0:T(8,128)S(1)}, u32[]{:S(2)}, u32[]{:S(2)}) %collective-permute-start.17) | collective-permute-done | bytes 147488 | tf_op jit(solution)/shard_map/ppermute | solution.py:676
  154.7 1.4 collective-permute-start.18
  156.2 2.6 %collective-permute-start.15 = (f32[8,1920]{1,0:T(8,128)S(1)}, f32[8,1920]{1,0:T(8,128)S(1)}, u32[]{:S(2)}, u32[]{:S(2)}) collective-permute-start(f32[8,1920]{1,0:T(8,128)S(1)} %constant_dynamic-slice_fusion.4), channel_id=1, source_target_pairs={{0,16},{1,17},{2,18},{3,19},{4,20},{5,21},{6,22},{7,23},{8,24},{9,... | collective-permute-start | bytes 184328 | tf_op jit(solution)/shard_map/ppermute | solution.py:676
  158.8 1.1 collective-permute-done.18
  159.8 2.0 %collective-permute-start.19 = (f32[8,1152]{1,0:T(8,128)S(1)}, f32[8,1152]{1,0:T(8,128)S(1)}, u32[]{:S(2)}, u32[]{:S(2)}) collective-permute-start(f32[8,1152]{1,0:T(8,128)S(1)} %constant_dynamic-slice_fusion), channel_id=1, source_target_pairs={{0,16},{1,17},{2,18},{3,19},{4,20},{5,21},{6,22},{7,23},{8,24},{9,... | collective-permute-start | bytes 110600 | tf_op jit(solution)/shard_map/ppermute | solution.py:676
  162.6 2.2 %collective-permute-done.19 = f32[8,1152]{1,0:T(8,128)S(1)} collective-permute-done((f32[8,1152]{1,0:T(8,128)S(1)}, f32[8,1152]{1,0:T(8,128)S(1)}, u32[]{:S(2)}, u32[]{:S(2)}) %collective-permute-start.19) | collective-permute-done | bytes 36896 | tf_op jit(solution)/shard_map/ppermute | solution.py:676
  165.4 4.1 %collective-permute-done.20 = f32[8,3072]{1,0:T(8,128)S(1)} collective-permute-done((f32[8,3072]{1,0:T(8,128)S(1)}, f32[8,3072]{1,0:T(8,128)S(1)}, u32[]{:S(2)}, u32[]{:S(2)}) %collective-permute-start.20) | collective-permute-done | bytes 98336 | tf_op jit(solution)/shard_map/ppermute | solution.py:800
  169.6 2.0 %collective-permute-start.21 = (bf16[8,3072]{1,0:T(8,128)(2,1)S(1)}, bf16[8,3072]{1,0:T(8,128)(2,1)S(1)}, u32[]{:S(2)}, u32[]{:S(2)}) collective-permute-start(bf16[8,3072]{1,0:T(8,128)(2,1)S(1)} %fusion.13), channel_id=1, source_target_pairs={{0,16},{1,17},{2,18},{3,19},{4,20},{5,21},{6,22},{7,23},{8,24},{9,... | collective-permute-start | bytes 147464 | tf_op jit(solution)/shard_map/ppermute | solution.py:683
  171.6 3.2 %collective-permute-done.21 = bf16[8,3072]{1,0:T(8,128)(2,1)S(1)} collective-permute-done((bf16[8,3072]{1,0:T(8,128)(2,1)S(1)}, bf16[8,3072]{1,0:T(8,128)(2,1)S(1)}, u32[]{:S(2)}, u32[]{:S(2)}) %collective-permute-start.21) | collective-permute-done | bytes 49184 | tf_op jit(solution)/shard_map/ppermute | solution.py:683
  174.8 1.4 collective-permute-start.22
  176.2 3.3 %collective-permute-done.22 = bf16[16,3072]{1,0:T(8,128)(2,1)S(1)} collective-permute-done((bf16[16,3072]{1,0:T(8,128)(2,1)S(1)}, bf16[16,3072]{1,0:T(8,128)(2,1)S(1)}, u32[]{:S(2)}, u32[]{:S(2)}) %collective-permute-start.22) | collective-permute-done | bytes 98336 | tf_op jit(solution)/shard_map/ppermute | solution.py:683
  179.7 5.5 %collective-permute-done.23 = bf16[32,3072]{1,0:T(8,128)(2,1)S(1)} collective-permute-done((bf16[32,3072]{1,0:T(8,128)(2,1)S(1)}, bf16[32,3072]{1,0:T(8,128)(2,1)S(1)}, u32[]{:S(2)}, u32[]{:S(2)}) %collective-permute-start.23) | collective-permute-done | bytes 196640 | tf_op jit(solution)/shard_map/ppermute | solution.py:683
  185.4 1.7 collective-permute-done.24
  187.7 1.1 copy.36
  188.7 1.0 copy.33
  (95 shorter events, 9.1 us)
Async XLA Ops:
  0.7 4.0 %copy-start.3 = (bf16[1,6,16,128,128]{4,3,2,1,0:T(8,128)(2,1)S(1)}, bf16[1,6,16,128,128]{4,3,2,1,0:T(8,128)(2,1)}, u32[]{:S(2)}) copy-start(bf16[1,6,16,128,128]{4,3,2,1,0:T(8,128)(2,1)} %param.9) | copy-start | bytes 9437188
  4.1 2.8 %copy-start.6 = (bf16[3,3,128,128]{3,2,1,0:T(8,128)(2,1)S(1)}, bf16[3,3,128,128]{3,2,1,0:T(8,128)(2,1)}, u32[]{:S(2)}) copy-start(bf16[3,3,128,128]{3,2,1,0:T(8,128)(2,1)} %param.11) | copy-start | bytes 884740
  4.1 3.7 %copy-start.12 = (s32[2]{0:T(128)S(1)}, s32[2]{0:T(128)}, u32[]{:S(2)}) copy-start(s32[2]{0:T(128)} %param.15) | copy-start | bytes 28
  4.1 3.8 %copy-start.7 = (bf16[3,3,128,128]{3,2,1,0:T(8,128)(2,1)S(1)}, bf16[3,3,128,128]{3,2,1,0:T(8,128)(2,1)}, u32[]{:S(2)}) copy-start(bf16[3,3,128,128]{3,2,1,0:T(8,128)(2,1)} %param.10) | copy-start | bytes 884740
  4.2 5.1 %collective-permute-start = (bf16[6,6,128,128]{3,2,1,0:T(8,128)(2,1)}, bf16[6,6,128,128]{3,2,1,0:T(8,128)(2,1)S(1)}, u32[]{:S(2)}, u32[]{:S(2)}) collective-permute-start(bf16[6,6,128,128]{3,2,1,0:T(8,128)(2,1)} %get-tuple-element.101), channel_id=1, source_target_pairs={{0,1},{1,0},{2,3},{3,2},{4,5},{5,4},{6,7},{7,6},{8,9},{9,8},{10,11... | collective-permute-start | bytes 3538952 | tf_op jit(solution)/shard_map/ppermute | solution.py:743
  6.2 3.2 %collective-permute-start.1 = (bf16[6,6,128,128]{3,2,1,0:T(8,128)(2,1)}, bf16[6,6,128,128]{3,2,1,0:T(8,128)(2,1)}, u32[]{:S(2)}, u32[]{:S(2)}) collective-permute-start(bf16[6,6,128,128]{3,2,1,0:T(8,128)(2,1)} %get-tuple-element.99), channel_id=1, source_target_pairs={{0,1},{1,0},{2,3},{3,2},{4,5},{5,4},{6,7},{7,6},{8,9},{9,8},{10,11... | collective-permute-start | bytes 3538952 | tf_op jit(solution)/shard_map/ppermute | solution.py:743
  9.2 1.1 copy-start.5
  10.3 15.5 %copy-start.10 = (bf16[3,128,128]{2,1,0:T(8,128)(2,1)S(1)}, bf16[3,128,128]{2,1,0:T(8,128)(2,1)}, u32[]{:S(2)}) copy-start(bf16[3,128,128]{2,1,0:T(8,128)(2,1)} %param.13) | copy-start | bytes 294916
  10.3 15.7 %copy-start = (bf16[3,128,128]{2,1,0:T(8,128)(2,1)S(1)}, bf16[3,128,128]{2,1,0:T(8,128)(2,1)}, u32[]{:S(2)}) copy-start(bf16[3,128,128]{2,1,0:T(8,128)(2,1)} %param.12) | copy-start | bytes 294916
  22.2 4.6 %collective-permute-start.3 = (bf16[6,6,128,128]{3,2,1,0:T(8,128)(2,1)}, bf16[6,6,128,128]{3,2,1,0:T(8,128)(2,1)}, u32[]{:S(2)}, u32[]{:S(2)}) collective-permute-start(bf16[6,6,128,128]{3,2,1,0:T(8,128)(2,1)} %get-tuple-element.55), channel_id=1, source_target_pairs={{0,1},{1,0},{2,3},{3,2},{4,5},{5,4},{6,7},{7,6},{8,9},{9,8},{10,11... | collective-permute-start | bytes 3538952 | tf_op jit(solution)/shard_map/ppermute | solution.py:743
  22.3 4.9 %collective-permute-start.4 = (bf16[6,6,128,128]{3,2,1,0:T(8,128)(2,1)}, bf16[6,6,128,128]{3,2,1,0:T(8,128)(2,1)}, u32[]{:S(2)}, u32[]{:S(2)}) collective-permute-start(bf16[6,6,128,128]{3,2,1,0:T(8,128)(2,1)} %get-tuple-element.56), channel_id=1, source_target_pairs={{0,1},{1,0},{2,3},{3,2},{4,5},{5,4},{6,7},{7,6},{8,9},{9,8},{10,11... | collective-permute-start | bytes 3538952 | tf_op jit(solution)/shard_map/ppermute | solution.py:743
  22.8 26.5 %collective-permute-start.2 = (bf16[8,4,128,128]{3,2,1,0:T(8,128)(2,1)}, bf16[8,4,128,128]{3,2,1,0:T(8,128)(2,1)S(1)}, u32[]{:S(2)}, u32[]{:S(2)}) collective-permute-start(bf16[8,4,128,128]{3,2,1,0:T(8,128)(2,1)} %get-tuple-element.52), channel_id=1, source_target_pairs={{0,2},{2,0},{1,3},{3,1},{4,6},{6,4},{5,7},{7,5},{8,10},{10,8},{9,1... | collective-permute-start | bytes 3145736 | tf_op jit(solution)/shard_map/ppermute | solution.py:753
  26.8 24.3 %copy-start.11 = (bf16[3,128,128]{1,2,0:T(8,128)(2,1)S(1)}, bf16[3,128,128]{1,2,0:T(8,128)(2,1)}, u32[]{:S(2)}) copy-start(bf16[3,128,128]{1,2,0:T(8,128)(2,1)} %copy.30) | copy-start | bytes 294916
  49.3 1.8 copy-start.8
  49.3 24.9 %collective-permute-start.5 = (bf16[8,4,128,128]{3,2,1,0:T(8,128)(2,1)}, bf16[8,4,128,128]{3,2,1,0:T(8,128)(2,1)}, u32[]{:S(2)}, u32[]{:S(2)}) collective-permute-start(bf16[8,4,128,128]{3,2,1,0:T(8,128)(2,1)} %get-tuple-element.58), channel_id=1, source_target_pairs={{0,2},{2,0},{1,3},{3,1},{4,6},{6,4},{5,7},{7,5},{8,10},{10,8},{9,1... | collective-permute-start | bytes 3145736 | tf_op jit(solution)/shard_map/ppermute | solution.py:753
  61.4 2.6 %collective-permute-start.6 = (bf16[6,4,128,128]{3,2,1,0:T(8,128)(2,1)}, bf16[6,4,128,128]{3,2,1,0:T(8,128)(2,1)}, u32[]{:S(2)}, u32[]{:S(2)}) collective-permute-start(bf16[6,4,128,128]{3,2,1,0:T(8,128)(2,1)} %get-tuple-element.60), channel_id=1, source_target_pairs={{0,1},{1,0},{2,3},{3,2},{4,5},{5,4},{6,7},{7,6},{8,9},{9,8},{10,11... | collective-permute-start | bytes 2359304 | tf_op jit(solution)/shard_map/ppermute | solution.py:763
  64.0 10.2 %copy-start.13 = (bf16[8,4,128,128]{3,2,1,0:T(8,128)(2,1)S(1)}, bf16[8,4,128,128]{3,2,1,0:T(8,128)(2,1)}, u32[]{:S(2)}) copy-start(bf16[8,4,128,128]{3,2,1,0:T(8,128)(2,1)} %get-tuple-element.62) | copy-start | bytes 3145732
  74.3 27.2 %collective-permute-start.7 = (bf16[8,4,128,128]{3,2,1,0:T(8,128)(2,1)S(1)}, bf16[8,4,128,128]{3,2,1,0:T(8,128)(2,1)}, u32[]{:S(2)}, u32[]{:S(2)}) collective-permute-start(bf16[8,4,128,128]{3,2,1,0:T(8,128)(2,1)S(1)} %copy-done.13), channel_id=1, source_target_pairs={{0,2},{2,0},{1,3},{3,1},{4,6},{6,4},{5,7},{7,5},{8,10},{10,8},{9,1... | collective-permute-start | bytes 3145736 | tf_op jit(solution)/shard_map/ppermute | solution.py:767
  85.9 0.9 copy-start.2
  86.8 2.5 %collective-permute-start.8 = (bf16[6,4,128,128]{3,2,1,0:T(8,128)(2,1)}, bf16[6,4,128,128]{3,2,1,0:T(8,128)(2,1)S(1)}, u32[]{:S(2)}, u32[]{:S(2)}) collective-permute-start(bf16[6,4,128,128]{3,2,1,0:T(8,128)(2,1)} %get-tuple-element.70), channel_id=1, source_target_pairs={{0,1},{1,0},{2,3},{3,2},{4,5},{5,4},{6,7},{7,6},{8,9},{9,8},{10,11... | collective-permute-start | bytes 2359304 | tf_op jit(solution)/shard_map/ppermute | solution.py:763
  89.3 0.9 copy-start.9
  101.5 25.6 %collective-permute-start.9 = (bf16[8,4,128,128]{3,2,1,0:T(8,128)(2,1)}, bf16[8,4,128,128]{3,2,1,0:T(8,128)(2,1)}, u32[]{:S(2)}, u32[]{:S(2)}) collective-permute-start(bf16[8,4,128,128]{3,2,1,0:T(8,128)(2,1)} %get-tuple-element.74), channel_id=1, source_target_pairs={{0,2},{2,0},{1,3},{3,1},{4,6},{6,4},{5,7},{7,5},{8,10},{10,8},{9,1... | collective-permute-start | bytes 3145736 | tf_op jit(solution)/shard_map/ppermute | solution.py:767
  107.4 2.6 %collective-permute-start.10 = (bf16[6,4,128,128]{3,2,1,0:T(8,128)(2,1)}, bf16[6,4,128,128]{3,2,1,0:T(8,128)(2,1)}, u32[]{:S(2)}, u32[]{:S(2)}) collective-permute-start(bf16[6,4,128,128]{3,2,1,0:T(8,128)(2,1)} %get-tuple-element.75), channel_id=1, source_target_pairs={{0,1},{1,0},{2,3},{3,2},{4,5},{5,4},{6,7},{7,6},{8,9},{9,8},{10,11... | collective-permute-start | bytes 2359304 | tf_op jit(solution)/shard_map/ppermute | solution.py:780
  107.5 19.5 %copy-start.4 = (f32[128,1920]{1,0:T(8,128)}, f32[128,1920]{1,0:T(8,128)S(1)}, u32[]{:S(2)}) copy-start(f32[128,1920]{1,0:T(8,128)S(1)} %pad_maximum_fusion) | copy-start | bytes 2949124
  127.1 6.0 %collective-permute-start.12 = (f32[64,1920]{1,0:T(8,128)S(1)}, f32[64,1920]{1,0:T(8,128)S(1)}, u32[]{:S(2)}, u32[]{:S(2)}) collective-permute-start(f32[64,1920]{1,0:T(8,128)S(1)} %constant_dynamic-slice_fusion.7), channel_id=1, source_target_pairs={{0,1},{1,0},{2,3},{3,2},{4,5},{5,4},{6,7},{7,6},{8,9},{9,8},{10,11... | collective-permute-start | bytes 1474568 | tf_op jit(solution)/shard_map/ppermute | solution.py:676
  131.7 0.9 copy-start.1
  132.5 3.2 %collective-permute-start.11 = (bf16[6,4,128,128]{3,2,1,0:T(8,128)(2,1)S(1)}, bf16[6,4,128,128]{3,2,1,0:T(8,128)(2,1)}, u32[]{:S(2)}, u32[]{:S(2)}) collective-permute-start(bf16[6,4,128,128]{3,2,1,0:T(8,128)(2,1)S(1)} %get-tuple-element.81), channel_id=1, source_target_pairs={{0,1},{1,0},{2,3},{3,2},{4,5},{5,4},{6,7},{7,6},{8,9},{9,8},{10,11... | collective-permute-start | bytes 2359304 | tf_op jit(solution)/shard_map/ppermute | solution.py:780
  134.2 12.7 %collective-permute-start.13 = (f32[32,1920]{1,0:T(8,128)S(1)}, f32[32,1920]{1,0:T(8,128)S(1)}, u32[]{:S(2)}, u32[]{:S(2)}) collective-permute-start(f32[32,1920]{1,0:T(8,128)S(1)} %constant_dynamic-slice_fusion.6), channel_id=1, source_target_pairs={{0,4},{1,5},{2,6},{3,7},{4,0},{5,1},{6,2},{7,3},{8,12},{9,13},{10,... | collective-permute-start | bytes 737288 | tf_op jit(solution)/shard_map/ppermute | solution.py:676
  146.8 1.8 collective-permute-start.16
  147.0 5.8 %collective-permute-start.14 = (f32[16,1920]{1,0:T(8,128)S(1)}, f32[16,1920]{1,0:T(8,128)S(1)}, u32[]{:S(2)}, u32[]{:S(2)}) collective-permute-start(f32[16,1920]{1,0:T(8,128)S(1)} %constant_dynamic-slice_fusion.5), channel_id=1, source_target_pairs={{0,8},{1,9},{2,10},{3,11},{4,12},{5,13},{6,14},{7,15},{8,0},{9,1},... | collective-permute-start | bytes 368648 | tf_op jit(solution)/shard_map/ppermute | solution.py:676
  148.7 6.0 %collective-permute-start.17 = (f32[32,1152]{1,0:T(8,128)S(1)}, f32[32,1152]{1,0:T(8,128)S(1)}, u32[]{:S(2)}, u32[]{:S(2)}) collective-permute-start(f32[32,1152]{1,0:T(8,128)S(1)} %constant_dynamic-slice_fusion.2), channel_id=1, source_target_pairs={{0,4},{1,5},{2,6},{3,7},{4,0},{5,1},{6,2},{7,3},{8,12},{9,13},{10,... | collective-permute-start | bytes 442376 | tf_op jit(solution)/shard_map/ppermute | solution.py:676
  154.7 5.1 %collective-permute-start.18 = (f32[16,1152]{1,0:T(8,128)S(1)}, f32[16,1152]{1,0:T(8,128)S(1)}, u32[]{:S(2)}, u32[]{:S(2)}) collective-permute-start(f32[16,1152]{1,0:T(8,128)S(1)} %constant_dynamic-slice_fusion.1), channel_id=1, source_target_pairs={{0,8},{1,9},{2,10},{3,11},{4,12},{5,13},{6,14},{7,15},{8,0},{9,1},... | collective-permute-start | bytes 221192 | tf_op jit(solution)/shard_map/ppermute | solution.py:676
  156.2 6.4 %collective-permute-start.15 = (f32[8,1920]{1,0:T(8,128)S(1)}, f32[8,1920]{1,0:T(8,128)S(1)}, u32[]{:S(2)}, u32[]{:S(2)}) collective-permute-start(f32[8,1920]{1,0:T(8,128)S(1)} %constant_dynamic-slice_fusion.4), channel_id=1, source_target_pairs={{0,16},{1,17},{2,18},{3,19},{4,20},{5,21},{6,22},{7,23},{8,24},{9,... | collective-permute-start | bytes 184328 | tf_op jit(solution)/shard_map/ppermute | solution.py:676
  159.8 4.9 %collective-permute-start.19 = (f32[8,1152]{1,0:T(8,128)S(1)}, f32[8,1152]{1,0:T(8,128)S(1)}, u32[]{:S(2)}, u32[]{:S(2)}) collective-permute-start(f32[8,1152]{1,0:T(8,128)S(1)} %constant_dynamic-slice_fusion), channel_id=1, source_target_pairs={{0,16},{1,17},{2,18},{3,19},{4,20},{5,21},{6,22},{7,23},{8,24},{9,... | collective-permute-start | bytes 110600 | tf_op jit(solution)/shard_map/ppermute | solution.py:676
  164.8 4.7 %collective-permute-start.20 = (f32[8,3072]{1,0:T(8,128)S(1)}, f32[8,3072]{1,0:T(8,128)S(1)}, u32[]{:S(2)}, u32[]{:S(2)}) collective-permute-start(f32[8,3072]{1,0:T(8,128)S(1)} %pad_maximum_fusion.1), channel_id=1, source_target_pairs={{0,2},{1,3},{2,0},{3,1},{4,6},{5,7},{6,4},{7,5},{8,10},{9,11},{10,... | collective-permute-start | bytes 294920 | tf_op jit(solution)/shard_map/ppermute | solution.py:800
  169.6 5.2 %collective-permute-start.21 = (bf16[8,3072]{1,0:T(8,128)(2,1)S(1)}, bf16[8,3072]{1,0:T(8,128)(2,1)S(1)}, u32[]{:S(2)}, u32[]{:S(2)}) collective-permute-start(bf16[8,3072]{1,0:T(8,128)(2,1)S(1)} %fusion.13), channel_id=1, source_target_pairs={{0,16},{1,17},{2,18},{3,19},{4,20},{5,21},{6,22},{7,23},{8,24},{9,... | collective-permute-start | bytes 147464 | tf_op jit(solution)/shard_map/ppermute | solution.py:683
  174.8 4.7 %collective-permute-start.22 = (bf16[16,3072]{1,0:T(8,128)(2,1)S(1)}, bf16[16,3072]{1,0:T(8,128)(2,1)S(1)}, u32[]{:S(2)}, u32[]{:S(2)}) collective-permute-start(bf16[16,3072]{1,0:T(8,128)(2,1)S(1)} %maximum_select_fusion.4), channel_id=1, source_target_pairs={{0,8},{1,9},{2,10},{3,11},{4,12},{5,13},{6,14},{7,15},{8,0},{9,1},... | collective-permute-start | bytes 294920 | tf_op jit(solution)/shard_map/ppermute | solution.py:683
  179.5 5.7 %collective-permute-start.23 = (bf16[32,3072]{1,0:T(8,128)(2,1)S(1)}, bf16[32,3072]{1,0:T(8,128)(2,1)S(1)}, u32[]{:S(2)}, u32[]{:S(2)}) collective-permute-start(bf16[32,3072]{1,0:T(8,128)(2,1)S(1)} %maximum_select_fusion.2), channel_id=1, source_target_pairs={{0,4},{1,5},{2,6},{3,7},{4,0},{5,1},{6,2},{7,3},{8,12},{9,13},{10,... | collective-permute-start | bytes 589832 | tf_op jit(solution)/shard_map/ppermute | solution.py:683
  185.3 1.8 collective-permute-start.24

commit v6 on v5

--- a/solution.py
+++ b/solution.py
@@ -803,7 +803,7 @@
     both = jnp.where(
         at_zero, both, jnp.concatenate([both[:, -span:], both[:, span:-span], both[:, :span]], 1)
     )
-    both = double(both.astype(BF), digits[::-1], pairs, place).astype(F32)
+    both = double(both.astype(BF), digits[::-1], pairs, place)
     spatial_sums = (both[:, :span], both[:, -span:])
     temporal_sums = both[:, span:-span]
 
@@ -812,7 +812,8 @@
     first_grad = first_grad[::-1, ::-1]
     near_grad = jnp.transpose(temporal_sums[:, : TAPS * chans].reshape(chans, TAPS, chans), (1, 2, 0))
     far_grad = jnp.transpose(temporal_sums[:, TAPS * chans :].reshape(chans, TAPS, chans), (1, 0, 2))
-    return (decoded[None], latent_grad[None], first_grad, last_grad, near_grad, far_grad)
+    sums = [value.astype(F32) for value in (first_grad, last_grad, near_grad, far_grad)]
+    return (decoded[None], latent_grad[None], *sums)
 
 
 def on_any_device(dp_size, tm_size, latents, cotangent, *rest):

time: 192 us -> 192 us (level)
    convert_element_type x0 -> x3, local copies, waits for them, and re-layouts: none -> 1.98 us  [on_chip_pair(): value.astype(F32)]
where the time goes in v6:
time: 192 us; the launch traced here: 191 us
  Pallas kernels  90.4 us (47%)
  waiting for transfers between devices  56.3 us (29%)
  starting transfers between devices  23.3 us (12%)
  local copies, waits for them, and re-layouts  15.2 us (8%)
  other arithmetic  4.48 us (2%)
    pallas_call x4, Pallas kernels, ending(): pl.pallas_call(functools.partial(ending_kernel, chunk, rows, factor, outs...  36.9 us
    pallas_call x2, Pallas kernels, front(): pl.pallas_call(functools.partial(front_kernel, slots), grid_spec=pltpu.Pr...  23.4 us
    pallas_call x2, Pallas kernels, middle(): pl.pallas_call(middle_kernel, grid_spec=pltpu.PrefetchScalarGridSpec(num_...  20.5 us
    ppermute x4, waiting for transfers between devices, double(): other = lax.ppermute(values, ('dp', 'tm'), pairs[digit])  13.7 us
    ppermute x2, waiting for transfers between devices, on_chip_pair(): halo = lax.ppermute(leaving, 'tm', swap_sides)  13.6 us
    ppermute x8, starting transfers between devices, halve(): values = keep + lax.ppermute(send, ('dp', 'tm'), pairs[digit])  10.6 us
    pallas_call x2, Pallas kernels, second(): pl.pallas_call(second_kernel, grid_spec=pltpu.PrefetchScalarGridSpec(num_...  9.69 us
    ppermute x2, waiting for transfers between devices, on_chip_pair(): halo = lax.ppermute(after(made[0], halo, sums_first), 'tm', swap_sides)  9.69 us
  transfers between devices with their start and end apart: 25, of which 18 were waited for; matrix products, arithmetic and copies ran while one was open for 4% of the time, Pallas kernels for 41%

profile of v6, /device:TPU:0, one launch (start us, length us, event | category | flops | bytes accessed | tf_op | source)
XLA Modules:
  0.0 191.5 jit_solution(22179502495069422)
XLA Ops:
  0.7 3.5 %dynamic-slice_bitcast_fusion.1 = (bf16[6,6,128,128]{3,2,1,0:T(8,128)(2,1)}, bf16[6,6,128,128]{3,2,1,0:T(8,128)(2,1)}) fusion(bf16[1,6,16,128,128]{4,3,2,1,0:T(8,128)(2,1)} %param.8, s32[]{:T(128)S(6)} %min.18, s32[]{:T(128)S(6)} %min.16), kind=kLoop, calls=%fused_computation.11 | loop fusion | bytes 4718600 | tf_op jit(solution)/shard_map/dynamic_slice | solution.py:738
  4.7 1.6 dynamic-slice_bitcast_fusion
  7.0 0.9 copy.28
  8.0 1.2 fusion.8
  9.4 0.8 copy-done.5
  10.3 12.0 %front.2 = (bf16[2,6,4,128,128]{4,3,2,1,0:T(8,128)(2,1)}, bf16[2,6,4,128,128]{4,3,2,1,0:T(8,128)(2,1)}, bf16[2,6,4,128,128]{4,3,2,1,0:T(8,128)(2,1)}, bf16[8,4,128,128]{3,2,1,0:T(8,128)(2,1)}) custom-call(s32[8]{0:T(128)S(1)} %concatenate.56.ids, bf16[6,16,128,128]{3,2,1,0:T(8,128)(2,1)} %bitcast.64, bf16[6,6,128,128]{3,2,1,0:T(8,128)(2,1)} %copy-done.5, ...), custom_call_target="tpu_custom_call" | custom-call | flops 220000000 | bytes 1000 | tf_op jit(solution)/shard_map/front/pallas_call | solution.py:329
  22.8 2.9 %collective-permute-start.2 = (bf16[8,4,128,128]{3,2,1,0:T(8,128)(2,1)}, bf16[8,4,128,128]{3,2,1,0:T(8,128)(2,1)S(1)}, u32[]{:S(2)}, u32[]{:S(2)}) collective-permute-start(bf16[8,4,128,128]{3,2,1,0:T(8,128)(2,1)} %get-tuple-element.52), channel_id=1, source_target_pairs={{0,2},{2,0},{1,3},{3,1},{4,6},{6,4},{5,7},{7,5},{8,10},{10,8},{9,1... | collective-permute-start | bytes 3145736 | tf_op jit(solution)/shard_map/ppermute | solution.py:753
  27.2 11.5 %front.3 = (bf16[2,6,4,128,128]{4,3,2,1,0:T(8,128)(2,1)}, bf16[2,6,4,128,128]{4,3,2,1,0:T(8,128)(2,1)}, bf16[2,6,4,128,128]{4,3,2,1,0:T(8,128)(2,1)}, bf16[8,4,128,128]{3,2,1,0:T(8,128)(2,1)}) custom-call(s32[8]{0:T(128)S(1)} %concatenate.59.ids, bf16[6,16,128,128]{3,2,1,0:T(8,128)(2,1)} %bitcast.65, ...), custom_call_target="tpu_custom_call" | custom-call | flops 220000000 | bytes 1000 | tf_op jit(solution)/shard_map/front/pallas_call | solution.py:329
  38.6 10.7 %collective-permute-done.2.halo = bf16[8,4,128,128]{3,2,1,0:T(8,128)(2,1)S(1)} collective-permute-done((bf16[8,4,128,128]{3,2,1,0:T(8,128)(2,1)}, bf16[8,4,128,128]{3,2,1,0:T(8,128)(2,1)S(1)}, u32[]{:S(2)}, u32[]{:S(2)}) %collective-permute-start.2) | collective-permute-done | bytes 1048608 | tf_op jit(solution)/shard_map/ppermute | solution.py:753
  49.3 1.7 collective-permute-start.5
  51.1 10.3 %middle.2 = (bf16[8,4,128,128]{3,2,1,0:T(8,128)(2,1)}, bf16[12,4,128,128]{3,2,1,0:T(8,128)(2,1)}, bf16[6,4,128,128]{3,2,1,0:T(8,128)(2,1)S(1)}, bf16[6,4,128,128...) custom-call(s32[6]{0:T(128)S(1)} %stack.39.ids, bf16[12,4,128,128]{3,2,1,0:T(8,128)(2,1)} %bitcast.82, ...), custom_call_target="tpu_custom_call" | custom-call | flops 240000000 | bytes 1000 | tf_op jit(solution)/shard_map/middle/pallas_call | solution.py:433
  61.6 1.4 broadcast_select_fusion
  63.0 1.0 collective-permute-done.6.refs_1_.refs_2_
  64.1 7.3 %ending.4 = (bf16[6,16,128,128]{3,2,1,0:T(8,128)(2,1)}, bf16[6,16,128,128]{3,2,1,0:T(8,128)(2,1)}, f32[128,1152]{1,0:T(8,128)S(1)}) custom-call(s32[6]{0:T(128)S(1)} %stack.39.ids, bf16[6,4,128,128]{3,2,1,0:T(8,128)(2,1)S(1)} %get-tuple-element.59.refs_0_, bf16[6,4,128,128]{3,2,1,0:T(8,128)(2,1)} %collective-permute-done.6.refs_1_.refs_2_, ...), custom_call_target="tpu_custom_call" | custom-call | flops 260000000 | bytes 1000 | tf_op jit(solution)/shard_map/ending/pallas_call | solution.py:615
  71.4 2.9 %collective-permute-done.5.halo = bf16[8,4,128,128]{3,2,1,0:T(8,128)(2,1)} collective-permute-done((bf16[8,4,128,128]{3,2,1,0:T(8,128)(2,1)}, bf16[8,4,128,128]{3,2,1,0:T(8,128)(2,1)}, u32[]{:S(2)}, u32[]{:S(2)}) %collective-permute-start.5) | collective-permute-done | bytes 1048608 | tf_op jit(solution)/shard_map/ppermute | solution.py:753
  74.3 1.4 collective-permute-start.7
  75.7 10.2 %middle.3 = (bf16[8,4,128,128]{3,2,1,0:T(8,128)(2,1)}, bf16[12,4,128,128]{3,2,1,0:T(8,128)(2,1)}, bf16[6,4,128,128]{3,2,1,0:T(8,128)(2,1)S(1)}, bf16[6,4,128,128...) custom-call(s32[6]{0:T(128)S(1)} %stack.39.ids, bf16[12,4,128,128]{3,2,1,0:T(8,128)(2,1)} %bitcast.84, ...), custom_call_target="tpu_custom_call" | custom-call | flops 240000000 | bytes 1000 | tf_op jit(solution)/shard_map/middle/pallas_call | solution.py:433
  85.9 0.9 copy-done.2
  86.8 2.5 %collective-permute-done.8.refs_3_ = bf16[6,4,128,128]{3,2,1,0:T(8,128)(2,1)S(1)} collective-permute-done((bf16[6,4,128,128]{3,2,1,0:T(8,128)(2,1)}, bf16[6,4,128,128]{3,2,1,0:T(8,128)(2,1)S(1)}, u32[]{:S(2)}, u32[]{:S(2)}) %collective-permute-start.8) | collective-permute-done | bytes 786464 | tf_op jit(solution)/shard_map/ppermute | solution.py:763
  89.3 0.9 copy-done.9
  90.2 11.2 %ending.5 = (bf16[6,16,128,128]{3,2,1,0:T(8,128)(2,1)}, bf16[6,16,128,128]{3,2,1,0:T(8,128)(2,1)}, f32[128,1152]{1,0:T(8,128)S(1)}) custom-call(s32[6]{0:T(128)S(1)} %stack.39.ids, bf16[6,4,128,128]{3,2,1,0:T(8,128)(2,1)S(1)} %get-tuple-element.59.refs_0_, bf16[6,4,128,128]{3,2,1,0:T(8,128)(2,1)} %copy-done.2, ...), custom_call_target="tpu_custom_call", output_to_operand_aliasing={{0}: (9, {}), {1}: (10, {})} | custom-call | flops 260000000 | bytes 1000 | tf_op jit(solution)/shard_map/ending/pallas_call | solution.py:615
  102.2 5.2 %second.2 = (bf16[6,4,128,128]{3,2,1,0:T(8,128)(2,1)S(1)}, bf16[6,4,128,128]{3,2,1,0:T(8,128)(2,1)}) custom-call(s32[6]{0:T(128)S(1)} %stack.38.ids, bf16[12,4,128,128]{3,2,1,0:T(8,128)(2,1)} %get-tuple-element.53.mid, bf16[12,4,128,128]{3,2,1,0:T(8,128)(2,1)} %bitcast.81, bf16[8,4,128,128]{3,2,1,0:T(8,128)(2,1)} %collective-permute-done.7.halo, ...), custom_call_target="tpu_custom_call" | custom-call | flops 100000000 | bytes 1000 | tf_op jit(solution)/shard_map/second/pallas_call | solution.py:488
  107.6 2.5 %collective-permute-done.10.refs_1_.refs_2_ = bf16[6,4,128,128]{3,2,1,0:T(8,128)(2,1)} collective-permute-done((bf16[6,4,128,128]{3,2,1,0:T(8,128)(2,1)}, bf16[6,4,128,128]{3,2,1,0:T(8,128)(2,1)}, u32[]{:S(2)}, u32[]{:S(2)}) %collective-permute-start.10) | collective-permute-done | bytes 786464 | tf_op jit(solution)/shard_map/ppermute | solution.py:780
  110.0 7.3 %ending.6 = (bf16[6,16,128,128]{3,2,1,0:T(8,128)(2,1)}, bf16[6,16,128,128]{3,2,1,0:T(8,128)(2,1)}, f32[128,1152]{1,0:T(8,128)S(1)}) custom-call(s32[6]{0:T(128)S(1)} %stack.38.ids, bf16[6,4,128,128]{3,2,1,0:T(8,128)(2,1)S(1)} %get-tuple-element.63.refs_0_, ...), custom_call_target="tpu_custom_call", output_to_operand_aliasing={{0}: (7, {}), {1}: (8, {})} | custom-call | flops 260000000 | bytes 1000 | tf_op jit(solution)/shard_map/ending/pallas_call | solution.py:615
  117.3 9.7 %collective-permute-done.9.halo = bf16[8,4,128,128]{3,2,1,0:T(8,128)(2,1)} collective-permute-done((bf16[8,4,128,128]{3,2,1,0:T(8,128)(2,1)}, bf16[8,4,128,128]{3,2,1,0:T(8,128)(2,1)}, u32[]{:S(2)}, u32[]{:S(2)}) %collective-permute-start.9) | collective-permute-done | bytes 1048608 | tf_op jit(solution)/shard_map/ppermute | solution.py:767
  127.2 4.5 %second.3 = (bf16[6,4,128,128]{3,2,1,0:T(8,128)(2,1)S(1)}, bf16[6,4,128,128]{3,2,1,0:T(8,128)(2,1)S(1)}) custom-call(s32[6]{0:T(128)S(1)} %stack.38.ids, bf16[12,4,128,128]{3,2,1,0:T(8,128)(2,1)} %get-tuple-element.67.mid, bf16[12,4,128,128]{3,2,1,0:T(8,128)(2,1)} %bitcast.79, bf16[8,4,128,128]{3,2,1,0:T(8,128)(2,1)} %collective-permute-done.9.halo, ...), custom_call_target="tpu_custom_call" | custom-call | flops 100000000 | bytes 1000 | tf_op jit(solution)/shard_map/second/pallas_call | solution.py:488
  131.7 0.9 copy-done.1
  133.0 1.1 dynamic-slice_add_fusion
  134.2 1.6 collective-permute-start.13
  135.7 11.0 %ending.7 = (bf16[6,16,128,128]{3,2,1,0:T(8,128)(2,1)}, bf16[6,16,128,128]{3,2,1,0:T(8,128)(2,1)}, f32[128,1152]{1,0:T(8,128)S(1)}) custom-call(s32[6]{0:T(128)S(1)} %stack.38.ids, bf16[6,4,128,128]{3,2,1,0:T(8,128)(2,1)S(1)} %get-tuple-element.63.refs_0_, bf16[6,4,128,128]{3,2,1,0:T(8,128)(2,1)} %copy-done.1, ...), custom_call_target="tpu_custom_call", output_to_operand_aliasing={{0}: (9, {}), {1}: (10, {})} | custom-call | flops 260000000 | bytes 1000 | tf_op jit(solution)/shard_map/ending/pallas_call | solution.py:615
  147.0 1.6 collective-permute-start.14
  148.7 1.3 collective-permute-start.17
  149.9 2.8 %collective-permute-done.14 = f32[16,1920]{1,0:T(8,128)S(1)} collective-permute-done((f32[16,1920]{1,0:T(8,128)S(1)}, f32[16,1920]{1,0:T(8,128)S(1)}, u32[]{:S(2)}, u32[]{:S(2)}) %collective-permute-start.14) | collective-permute-done | bytes 122912 | tf_op jit(solution)/shard_map/ppermute | solution.py:676
  152.7 1.9 %collective-permute-done.17 = f32[32,1152]{1,0:T(8,128)S(1)} collective-permute-done((f32[32,1152]{1,0:T(8,128)S(1)}, f32[32,1152]{1,0:T(8,128)S(1)}, u32[]{:S(2)}, u32[]{:S(2)}) %collective-permute-start.17) | collective-permute-done | bytes 147488 | tf_op jit(solution)/shard_map/ppermute | solution.py:676
  154.7 1.4 collective-permute-start.18
  156.2 2.6 %collective-permute-start.15 = (f32[8,1920]{1,0:T(8,128)S(1)}, f32[8,1920]{1,0:T(8,128)S(1)}, u32[]{:S(2)}, u32[]{:S(2)}) collective-permute-start(f32[8,1920]{1,0:T(8,128)S(1)} %constant_dynamic-slice_fusion.4), channel_id=1, source_target_pairs={{0,16},{1,17},{2,18},{3,19},{4,20},{5,21},{6,22},{7,23},{8,24},{9,... | collective-permute-start | bytes 184328 | tf_op jit(solution)/shard_map/ppermute | solution.py:676
  158.8 1.1 collective-permute-done.18
  159.8 2.0 %collective-permute-start.19 = (f32[8,1152]{1,0:T(8,128)S(1)}, f32[8,1152]{1,0:T(8,128)S(1)}, u32[]{:S(2)}, u32[]{:S(2)}) collective-permute-start(f32[8,1152]{1,0:T(8,128)S(1)} %constant_dynamic-slice_fusion), channel_id=1, source_target_pairs={{0,16},{1,17},{2,18},{3,19},{4,20},{5,21},{6,22},{7,23},{8,24},{9,... | collective-permute-start | bytes 110600 | tf_op jit(solution)/shard_map/ppermute | solution.py:676
  162.6 2.2 %collective-permute-done.19 = f32[8,1152]{1,0:T(8,128)S(1)} collective-permute-done((f32[8,1152]{1,0:T(8,128)S(1)}, f32[8,1152]{1,0:T(8,128)S(1)}, u32[]{:S(2)}, u32[]{:S(2)}) %collective-permute-start.19) | collective-permute-done | bytes 36896 | tf_op jit(solution)/shard_map/ppermute | solution.py:676
  165.4 4.1 %collective-permute-done.20 = f32[8,3072]{1,0:T(8,128)S(1)} collective-permute-done((f32[8,3072]{1,0:T(8,128)S(1)}, f32[8,3072]{1,0:T(8,128)S(1)}, u32[]{:S(2)}, u32[]{:S(2)}) %collective-permute-start.20) | collective-permute-done | bytes 98336 | tf_op jit(solution)/shard_map/ppermute | solution.py:800
  169.6 2.0 %collective-permute-start.21 = (bf16[8,3072]{1,0:T(8,128)(2,1)S(1)}, bf16[8,3072]{1,0:T(8,128)(2,1)S(1)}, u32[]{:S(2)}, u32[]{:S(2)}) collective-permute-start(bf16[8,3072]{1,0:T(8,128)(2,1)S(1)} %fusion.12), channel_id=1, source_target_pairs={{0,16},{1,17},{2,18},{3,19},{4,20},{5,21},{6,22},{7,23},{8,24},{9,... | collective-permute-start | bytes 147464 | tf_op jit(solution)/shard_map/ppermute | solution.py:683
  171.6 3.2 %collective-permute-done.21 = bf16[8,3072]{1,0:T(8,128)(2,1)S(1)} collective-permute-done((bf16[8,3072]{1,0:T(8,128)(2,1)S(1)}, bf16[8,3072]{1,0:T(8,128)(2,1)S(1)}, u32[]{:S(2)}, u32[]{:S(2)}) %collective-permute-start.21) | collective-permute-done | bytes 49184 | tf_op jit(solution)/shard_map/ppermute | solution.py:683
  174.8 1.4 collective-permute-start.22
  176.2 3.3 %collective-permute-done.22 = bf16[16,3072]{1,0:T(8,128)(2,1)S(1)} collective-permute-done((bf16[16,3072]{1,0:T(8,128)(2,1)S(1)}, bf16[16,3072]{1,0:T(8,128)(2,1)S(1)}, u32[]{:S(2)}, u32[]{:S(2)}) %collective-permute-start.22) | collective-permute-done | bytes 98336 | tf_op jit(solution)/shard_map/ppermute | solution.py:683
  179.7 5.5 %collective-permute-done.23 = bf16[32,3072]{1,0:T(8,128)(2,1)S(1)} collective-permute-done((bf16[32,3072]{1,0:T(8,128)(2,1)S(1)}, bf16[32,3072]{1,0:T(8,128)(2,1)S(1)}, u32[]{:S(2)}, u32[]{:S(2)}) %collective-permute-start.23) | collective-permute-done | bytes 196640 | tf_op jit(solution)/shard_map/ppermute | solution.py:683
  185.4 1.7 collective-permute-done.24
  187.6 1.1 copy.36
  188.7 1.0 copy.33
  (95 shorter events, 9.1 us)
Async XLA Ops:
  0.7 4.0 %copy-start.3 = (bf16[1,6,16,128,128]{4,3,2,1,0:T(8,128)(2,1)S(1)}, bf16[1,6,16,128,128]{4,3,2,1,0:T(8,128)(2,1)}, u32[]{:S(2)}) copy-start(bf16[1,6,16,128,128]{4,3,2,1,0:T(8,128)(2,1)} %param.9) | copy-start | bytes 9437188
  4.1 2.8 %copy-start.6 = (bf16[3,3,128,128]{3,2,1,0:T(8,128)(2,1)S(1)}, bf16[3,3,128,128]{3,2,1,0:T(8,128)(2,1)}, u32[]{:S(2)}) copy-start(bf16[3,3,128,128]{3,2,1,0:T(8,128)(2,1)} %param.11) | copy-start | bytes 884740
  4.1 3.7 %copy-start.12 = (s32[2]{0:T(128)S(1)}, s32[2]{0:T(128)}, u32[]{:S(2)}) copy-start(s32[2]{0:T(128)} %param.15) | copy-start | bytes 28
  4.1 3.8 %copy-start.7 = (bf16[3,3,128,128]{3,2,1,0:T(8,128)(2,1)S(1)}, bf16[3,3,128,128]{3,2,1,0:T(8,128)(2,1)}, u32[]{:S(2)}) copy-start(bf16[3,3,128,128]{3,2,1,0:T(8,128)(2,1)} %param.10) | copy-start | bytes 884740
  4.2 5.1 %collective-permute-start = (bf16[6,6,128,128]{3,2,1,0:T(8,128)(2,1)}, bf16[6,6,128,128]{3,2,1,0:T(8,128)(2,1)S(1)}, u32[]{:S(2)}, u32[]{:S(2)}) collective-permute-start(bf16[6,6,128,128]{3,2,1,0:T(8,128)(2,1)} %get-tuple-element.101), channel_id=1, source_target_pairs={{0,1},{1,0},{2,3},{3,2},{4,5},{5,4},{6,7},{7,6},{8,9},{9,8},{10,11... | collective-permute-start | bytes 3538952 | tf_op jit(solution)/shard_map/ppermute | solution.py:743
  6.2 3.2 %collective-permute-start.1 = (bf16[6,6,128,128]{3,2,1,0:T(8,128)(2,1)}, bf16[6,6,128,128]{3,2,1,0:T(8,128)(2,1)}, u32[]{:S(2)}, u32[]{:S(2)}) collective-permute-start(bf16[6,6,128,128]{3,2,1,0:T(8,128)(2,1)} %get-tuple-element.99), channel_id=1, source_target_pairs={{0,1},{1,0},{2,3},{3,2},{4,5},{5,4},{6,7},{7,6},{8,9},{9,8},{10,11... | collective-permute-start | bytes 3538952 | tf_op jit(solution)/shard_map/ppermute | solution.py:743
  9.2 1.1 copy-start.5
  10.3 15.5 %copy-start.10 = (bf16[3,128,128]{2,1,0:T(8,128)(2,1)S(1)}, bf16[3,128,128]{2,1,0:T(8,128)(2,1)}, u32[]{:S(2)}) copy-start(bf16[3,128,128]{2,1,0:T(8,128)(2,1)} %param.13) | copy-start | bytes 294916
  10.3 15.7 %copy-start = (bf16[3,128,128]{2,1,0:T(8,128)(2,1)S(1)}, bf16[3,128,128]{2,1,0:T(8,128)(2,1)}, u32[]{:S(2)}) copy-start(bf16[3,128,128]{2,1,0:T(8,128)(2,1)} %param.12) | copy-start | bytes 294916
  22.2 4.6 %collective-permute-start.3 = (bf16[6,6,128,128]{3,2,1,0:T(8,128)(2,1)}, bf16[6,6,128,128]{3,2,1,0:T(8,128)(2,1)}, u32[]{:S(2)}, u32[]{:S(2)}) collective-permute-start(bf16[6,6,128,128]{3,2,1,0:T(8,128)(2,1)} %get-tuple-element.55), channel_id=1, source_target_pairs={{0,1},{1,0},{2,3},{3,2},{4,5},{5,4},{6,7},{7,6},{8,9},{9,8},{10,11... | collective-permute-start | bytes 3538952 | tf_op jit(solution)/shard_map/ppermute | solution.py:743
  22.3 4.9 %collective-permute-start.4 = (bf16[6,6,128,128]{3,2,1,0:T(8,128)(2,1)}, bf16[6,6,128,128]{3,2,1,0:T(8,128)(2,1)}, u32[]{:S(2)}, u32[]{:S(2)}) collective-permute-start(bf16[6,6,128,128]{3,2,1,0:T(8,128)(2,1)} %get-tuple-element.56), channel_id=1, source_target_pairs={{0,1},{1,0},{2,3},{3,2},{4,5},{5,4},{6,7},{7,6},{8,9},{9,8},{10,11... | collective-permute-start | bytes 3538952 | tf_op jit(solution)/shard_map/ppermute | solution.py:743
  22.8 26.5 %collective-permute-start.2 = (bf16[8,4,128,128]{3,2,1,0:T(8,128)(2,1)}, bf16[8,4,128,128]{3,2,1,0:T(8,128)(2,1)S(1)}, u32[]{:S(2)}, u32[]{:S(2)}) collective-permute-start(bf16[8,4,128,128]{3,2,1,0:T(8,128)(2,1)} %get-tuple-element.52), channel_id=1, source_target_pairs={{0,2},{2,0},{1,3},{3,1},{4,6},{6,4},{5,7},{7,5},{8,10},{10,8},{9,1... | collective-permute-start | bytes 3145736 | tf_op jit(solution)/shard_map/ppermute | solution.py:753
  26.8 24.3 %copy-start.11 = (bf16[3,128,128]{1,2,0:T(8,128)(2,1)S(1)}, bf16[3,128,128]{1,2,0:T(8,128)(2,1)}, u32[]{:S(2)}) copy-start(bf16[3,128,128]{1,2,0:T(8,128)(2,1)} %copy.30) | copy-start | bytes 294916
  49.3 1.8 copy-start.8
  49.3 24.9 %collective-permute-start.5 = (bf16[8,4,128,128]{3,2,1,0:T(8,128)(2,1)}, bf16[8,4,128,128]{3,2,1,0:T(8,128)(2,1)}, u32[]{:S(2)}, u32[]{:S(2)}) collective-permute-start(bf16[8,4,128,128]{3,2,1,0:T(8,128)(2,1)} %get-tuple-element.58), channel_id=1, source_target_pairs={{0,2},{2,0},{1,3},{3,1},{4,6},{6,4},{5,7},{7,5},{8,10},{10,8},{9,1... | collective-permute-start | bytes 3145736 | tf_op jit(solution)/shard_map/ppermute | solution.py:753
  61.4 2.6 %collective-permute-start.6 = (bf16[6,4,128,128]{3,2,1,0:T(8,128)(2,1)}, bf16[6,4,128,128]{3,2,1,0:T(8,128)(2,1)}, u32[]{:S(2)}, u32[]{:S(2)}) collective-permute-start(bf16[6,4,128,128]{3,2,1,0:T(8,128)(2,1)} %get-tuple-element.60), channel_id=1, source_target_pairs={{0,1},{1,0},{2,3},{3,2},{4,5},{5,4},{6,7},{7,6},{8,9},{9,8},{10,11... | collective-permute-start | bytes 2359304 | tf_op jit(solution)/shard_map/ppermute | solution.py:763
  64.0 10.2 %copy-start.13 = (bf16[8,4,128,128]{3,2,1,0:T(8,128)(2,1)S(1)}, bf16[8,4,128,128]{3,2,1,0:T(8,128)(2,1)}, u32[]{:S(2)}) copy-start(bf16[8,4,128,128]{3,2,1,0:T(8,128)(2,1)} %get-tuple-element.62) | copy-start | bytes 3145732
  74.3 27.2 %collective-permute-start.7 = (bf16[8,4,128,128]{3,2,1,0:T(8,128)(2,1)S(1)}, bf16[8,4,128,128]{3,2,1,0:T(8,128)(2,1)}, u32[]{:S(2)}, u32[]{:S(2)}) collective-permute-start(bf16[8,4,128,128]{3,2,1,0:T(8,128)(2,1)S(1)} %copy-done.13), channel_id=1, source_target_pairs={{0,2},{2,0},{1,3},{3,1},{4,6},{6,4},{5,7},{7,5},{8,10},{10,8},{9,1... | collective-permute-start | bytes 3145736 | tf_op jit(solution)/shard_map/ppermute | solution.py:767
  85.9 0.9 copy-start.2
  86.8 2.5 %collective-permute-start.8 = (bf16[6,4,128,128]{3,2,1,0:T(8,128)(2,1)}, bf16[6,4,128,128]{3,2,1,0:T(8,128)(2,1)S(1)}, u32[]{:S(2)}, u32[]{:S(2)}) collective-permute-start(bf16[6,4,128,128]{3,2,1,0:T(8,128)(2,1)} %get-tuple-element.70), channel_id=1, source_target_pairs={{0,1},{1,0},{2,3},{3,2},{4,5},{5,4},{6,7},{7,6},{8,9},{9,8},{10,11... | collective-permute-start | bytes 2359304 | tf_op jit(solution)/shard_map/ppermute | solution.py:763
  89.3 0.9 copy-start.9
  101.5 25.6 %collective-permute-start.9 = (bf16[8,4,128,128]{3,2,1,0:T(8,128)(2,1)}, bf16[8,4,128,128]{3,2,1,0:T(8,128)(2,1)}, u32[]{:S(2)}, u32[]{:S(2)}) collective-permute-start(bf16[8,4,128,128]{3,2,1,0:T(8,128)(2,1)} %get-tuple-element.74), channel_id=1, source_target_pairs={{0,2},{2,0},{1,3},{3,1},{4,6},{6,4},{5,7},{7,5},{8,10},{10,8},{9,1... | collective-permute-start | bytes 3145736 | tf_op jit(solution)/shard_map/ppermute | solution.py:767
  107.4 2.6 %collective-permute-start.10 = (bf16[6,4,128,128]{3,2,1,0:T(8,128)(2,1)}, bf16[6,4,128,128]{3,2,1,0:T(8,128)(2,1)}, u32[]{:S(2)}, u32[]{:S(2)}) collective-permute-start(bf16[6,4,128,128]{3,2,1,0:T(8,128)(2,1)} %get-tuple-element.75), channel_id=1, source_target_pairs={{0,1},{1,0},{2,3},{3,2},{4,5},{5,4},{6,7},{7,6},{8,9},{9,8},{10,11... | collective-permute-start | bytes 2359304 | tf_op jit(solution)/shard_map/ppermute | solution.py:780
  107.5 19.5 %copy-start.4 = (f32[128,1920]{1,0:T(8,128)}, f32[128,1920]{1,0:T(8,128)S(1)}, u32[]{:S(2)}) copy-start(f32[128,1920]{1,0:T(8,128)S(1)} %pad_maximum_fusion) | copy-start | bytes 2949124
  127.1 6.0 %collective-permute-start.12 = (f32[64,1920]{1,0:T(8,128)S(1)}, f32[64,1920]{1,0:T(8,128)S(1)}, u32[]{:S(2)}, u32[]{:S(2)}) collective-permute-start(f32[64,1920]{1,0:T(8,128)S(1)} %constant_dynamic-slice_fusion.7), channel_id=1, source_target_pairs={{0,1},{1,0},{2,3},{3,2},{4,5},{5,4},{6,7},{7,6},{8,9},{9,8},{10,11... | collective-permute-start | bytes 1474568 | tf_op jit(solution)/shard_map/ppermute | solution.py:676
  131.7 0.9 copy-start.1
  132.5 3.2 %collective-permute-start.11 = (bf16[6,4,128,128]{3,2,1,0:T(8,128)(2,1)S(1)}, bf16[6,4,128,128]{3,2,1,0:T(8,128)(2,1)}, u32[]{:S(2)}, u32[]{:S(2)}) collective-permute-start(bf16[6,4,128,128]{3,2,1,0:T(8,128)(2,1)S(1)} %get-tuple-element.81), channel_id=1, source_target_pairs={{0,1},{1,0},{2,3},{3,2},{4,5},{5,4},{6,7},{7,6},{8,9},{9,8},{10,11... | collective-permute-start | bytes 2359304 | tf_op jit(solution)/shard_map/ppermute | solution.py:780
  134.2 12.7 %collective-permute-start.13 = (f32[32,1920]{1,0:T(8,128)S(1)}, f32[32,1920]{1,0:T(8,128)S(1)}, u32[]{:S(2)}, u32[]{:S(2)}) collective-permute-start(f32[32,1920]{1,0:T(8,128)S(1)} %constant_dynamic-slice_fusion.6), channel_id=1, source_target_pairs={{0,4},{1,5},{2,6},{3,7},{4,0},{5,1},{6,2},{7,3},{8,12},{9,13},{10,... | collective-permute-start | bytes 737288 | tf_op jit(solution)/shard_map/ppermute | solution.py:676
  146.8 1.8 collective-permute-start.16
  147.0 5.8 %collective-permute-start.14 = (f32[16,1920]{1,0:T(8,128)S(1)}, f32[16,1920]{1,0:T(8,128)S(1)}, u32[]{:S(2)}, u32[]{:S(2)}) collective-permute-start(f32[16,1920]{1,0:T(8,128)S(1)} %constant_dynamic-slice_fusion.5), channel_id=1, source_target_pairs={{0,8},{1,9},{2,10},{3,11},{4,12},{5,13},{6,14},{7,15},{8,0},{9,1},... | collective-permute-start | bytes 368648 | tf_op jit(solution)/shard_map/ppermute | solution.py:676
  148.7 6.0 %collective-permute-start.17 = (f32[32,1152]{1,0:T(8,128)S(1)}, f32[32,1152]{1,0:T(8,128)S(1)}, u32[]{:S(2)}, u32[]{:S(2)}) collective-permute-start(f32[32,1152]{1,0:T(8,128)S(1)} %constant_dynamic-slice_fusion.2), channel_id=1, source_target_pairs={{0,4},{1,5},{2,6},{3,7},{4,0},{5,1},{6,2},{7,3},{8,12},{9,13},{10,... | collective-permute-start | bytes 442376 | tf_op jit(solution)/shard_map/ppermute | solution.py:676
  154.7 5.1 %collective-permute-start.18 = (f32[16,1152]{1,0:T(8,128)S(1)}, f32[16,1152]{1,0:T(8,128)S(1)}, u32[]{:S(2)}, u32[]{:S(2)}) collective-permute-start(f32[16,1152]{1,0:T(8,128)S(1)} %constant_dynamic-slice_fusion.1), channel_id=1, source_target_pairs={{0,8},{1,9},{2,10},{3,11},{4,12},{5,13},{6,14},{7,15},{8,0},{9,1},... | collective-permute-start | bytes 221192 | tf_op jit(solution)/shard_map/ppermute | solution.py:676
  156.2 6.4 %collective-permute-start.15 = (f32[8,1920]{1,0:T(8,128)S(1)}, f32[8,1920]{1,0:T(8,128)S(1)}, u32[]{:S(2)}, u32[]{:S(2)}) collective-permute-start(f32[8,1920]{1,0:T(8,128)S(1)} %constant_dynamic-slice_fusion.4), channel_id=1, source_target_pairs={{0,16},{1,17},{2,18},{3,19},{4,20},{5,21},{6,22},{7,23},{8,24},{9,... | collective-permute-start | bytes 184328 | tf_op jit(solution)/shard_map/ppermute | solution.py:676
  159.8 4.9 %collective-permute-start.19 = (f32[8,1152]{1,0:T(8,128)S(1)}, f32[8,1152]{1,0:T(8,128)S(1)}, u32[]{:S(2)}, u32[]{:S(2)}) collective-permute-start(f32[8,1152]{1,0:T(8,128)S(1)} %constant_dynamic-slice_fusion), channel_id=1, source_target_pairs={{0,16},{1,17},{2,18},{3,19},{4,20},{5,21},{6,22},{7,23},{8,24},{9,... | collective-permute-start | bytes 110600 | tf_op jit(solution)/shard_map/ppermute | solution.py:676
  164.8 4.7 %collective-permute-start.20 = (f32[8,3072]{1,0:T(8,128)S(1)}, f32[8,3072]{1,0:T(8,128)S(1)}, u32[]{:S(2)}, u32[]{:S(2)}) collective-permute-start(f32[8,3072]{1,0:T(8,128)S(1)} %pad_maximum_fusion.1), channel_id=1, source_target_pairs={{0,2},{1,3},{2,0},{3,1},{4,6},{5,7},{6,4},{7,5},{8,10},{9,11},{10,... | collective-permute-start | bytes 294920 | tf_op jit(solution)/shard_map/ppermute | solution.py:800
  169.6 5.2 %collective-permute-start.21 = (bf16[8,3072]{1,0:T(8,128)(2,1)S(1)}, bf16[8,3072]{1,0:T(8,128)(2,1)S(1)}, u32[]{:S(2)}, u32[]{:S(2)}) collective-permute-start(bf16[8,3072]{1,0:T(8,128)(2,1)S(1)} %fusion.12), channel_id=1, source_target_pairs={{0,16},{1,17},{2,18},{3,19},{4,20},{5,21},{6,22},{7,23},{8,24},{9,... | collective-permute-start | bytes 147464 | tf_op jit(solution)/shard_map/ppermute | solution.py:683
  174.8 4.7 %collective-permute-start.22 = (bf16[16,3072]{1,0:T(8,128)(2,1)S(1)}, bf16[16,3072]{1,0:T(8,128)(2,1)S(1)}, u32[]{:S(2)}, u32[]{:S(2)}) collective-permute-start(bf16[16,3072]{1,0:T(8,128)(2,1)S(1)} %maximum_select_fusion.4), channel_id=1, source_target_pairs={{0,8},{1,9},{2,10},{3,11},{4,12},{5,13},{6,14},{7,15},{8,0},{9,1},... | collective-permute-start | bytes 294920 | tf_op jit(solution)/shard_map/ppermute | solution.py:683
  179.5 5.7 %collective-permute-start.23 = (bf16[32,3072]{1,0:T(8,128)(2,1)S(1)}, bf16[32,3072]{1,0:T(8,128)(2,1)S(1)}, u32[]{:S(2)}, u32[]{:S(2)}) collective-permute-start(bf16[32,3072]{1,0:T(8,128)(2,1)S(1)} %maximum_select_fusion.2), channel_id=1, source_target_pairs={{0,4},{1,5},{2,6},{3,7},{4,0},{5,1},{6,2},{7,3},{8,12},{9,13},{10,... | collective-permute-start | bytes 589832 | tf_op jit(solution)/shard_map/ppermute | solution.py:683
  185.3 1.8 collective-permute-start.24
